TPU v7x, 32 devices: a whole 2x2x4 slice. The times are simulated.
32 devices in a mesh: dp: 8 (over z, y), rep: 4 (over x, core).
Axes of the slice: x: 2, y: 2, z: 4, core: 2. Of those that a mesh axis runs over, the one named last changes fastest.
Arguments:
- tokens: bfloat16 [31488, 384], P(('dp', 'rep')), may hold values from -6 to 6
- cotangent: bfloat16 [31488, 384], P(('dp', 'rep')), may hold values from -6 to 6
- lengths: int32 [384], P(('dp', 'rep')), may hold values from 50 to 145, as said below
- pos_map: int32 [31488], P(('dp', 'rep')), may hold values from 0 to 144
- attn_params: float32 [592128], P(('dp', 'rep'))
- attn_first: float32 [592128], P(('dp', 'rep')), may hold values from -4 to 4
- attn_second: float32 [592128], P(('dp', 'rep')), may hold values from 0.0001 to 0.01
- mlp_params: float32 [1238016], P(('dp', 'rep'))
- mlp_first: float32 [1238016], P(('dp', 'rep')), may hold values from -4 to 4
- mlp_second: float32 [1238016], P(('dp', 'rep')), may hold values from 0.0001 to 0.01
Outputs:
- output: bfloat16 [31488, 384], P(('dp', 'rep'))
- in_grad: bfloat16 [31488, 384], P(('dp', 'rep'))
- attn_grad: float32 [592128], P(('dp', 'rep'))
- attn_step: float32 [592128], P(('dp', 'rep'))
- attn_first_new: float32 [592128], P(('dp', 'rep'))
- attn_second_new: float32 [592128], P(('dp', 'rep'))
- mlp_grad: float32 [1238016], P(('dp', 'rep'))
- mlp_step: float32 [1238016], P(('dp', 'rep'))
- mlp_first_new: float32 [1238016], P(('dp', 'rep'))
- mlp_second_new: float32 [1238016], P(('dp', 'rep'))
Inputs may be any that keep to these rules, and one draw needn't show every extreme that they name: `lengths`: every image has 50 or 145 tokens; one device's 12 images hold at most 4 of 145 tokens, and some device holds exactly 4 in every draw.
All inputs are finite; a program needn't handle non-finite values.
Results may differ from a plain program's by a relative error of at most 0.014.
Values may be sent and summed in bfloat16 or wider, within the bound.
No kernel may reach another device: no remote copies, remote signals or barrier semaphores. Data moves between devices by JAX's collectives and lax.ppermute only.
A program may use at most 128 MiB of HBM per device.

v0:
```python
import functools
import math

import jax
import jax.numpy as jnp
from jax import lax
from jax.experimental import pallas as pl
from jax.experimental.pallas import tpu as pltpu
from jax.sharding import PartitionSpec as P

D = 384
H = 6
DH = 64
FF = 1536
POS = 145
SHORT = 50
LONG = 145
MOST_LONG = 4
STEP = 10
LANES = 128
TILE = 8 * LANES
PAIRS = H // 2
QKV_COLS = 3 * D // LANES
D_COLS = D // LANES
FF_COLS = FF // LANES

LEARNING_RATE = 0.001
WEIGHT_DECAY = 0.05
BETA_FIRST = 0.9
BETA_SECOND = 0.999
adam_eps = 1e-08

F32 = jnp.float32
BF16 = jnp.bfloat16
NT = (((1,), (1,)), ((), ()))
TN = (((0,), (0,)), ((), ()))
NN = (((1,), (0,)), ((), ()))
BLOCK = 128
PART = 256

ROW_GAIN_ONE = 0
ROW_BIAS_ONE = ROW_GAIN_ONE + D_COLS
ROW_W_QKV = ROW_BIAS_ONE + D_COLS
ROW_B_QKV = ROW_W_QKV + D * QKV_COLS
ROW_W_OUT = ROW_B_QKV + QKV_COLS
ROW_B_OUT = ROW_W_OUT + D * D_COLS
ATTN_ROWS = ROW_B_OUT + D_COLS
ROW_POS = 0
ROW_GAIN_TWO = ROW_POS + POS * D_COLS
ROW_BIAS_TWO = ROW_GAIN_TWO + D_COLS
ROW_W_IN = ROW_BIAS_TWO + D_COLS
ROW_B_IN = ROW_W_IN + D * FF_COLS
ROW_W_BACK = ROW_B_IN + FF_COLS
ROW_B_BACK = ROW_W_BACK + FF * D_COLS
MLP_ROWS = ROW_B_BACK + D_COLS


def dot(a, b, dims=NN):
    return lax.dot_general(a, b, dims, preferred_element_type=F32)


def tile_row(entries, j):
    return pl.multiple_of(((j * entries) // TILE) * 8, 8)


def piece_rows(entries, count):
    most = max((entries * j) % TILE + entries for j in range(count))
    return -(-most // (16 * LANES)) * 16


def flat_rows(entries, count, rows):
    return max((entries * j) // TILE * 8 + rows for j in range(count))


def params(mebibytes):
    return pltpu.CompilerParams(vmem_limit_bytes=mebibytes * 1024 * 1024)


def cost(microseconds):
    return pl.CostEstimate(flops=int(microseconds * 1.15e9), bytes_accessed=1024, transcendentals=0)


def whole(shape):
    return pl.BlockSpec(shape, lambda *_: (0,) * len(shape))


SMEM_SPEC = pl.BlockSpec(memory_space=pltpu.SMEM)
VMEM_SPEC = pl.BlockSpec(memory_space=pltpu.VMEM)


def tall(vector, rows):
    entries = vector.shape[0]
    full = entries // TILE * TILE
    parts = [vector[pl.ds(0, full)].reshape(full // LANES, LANES)] if full else []
    if entries > full:
        rest = jnp.concatenate([vector[pl.ds(full, entries - full)], jnp.zeros((full + TILE - entries,), F32)])
        parts.append(rest.reshape(8, LANES))
    height = sum(part.shape[0] for part in parts)
    if height < rows:
        parts.append(jnp.zeros((rows - height, LANES), F32))
    return jnp.concatenate(parts, axis=0)


def put_flat(vector, value):
    entries = vector.shape[0]
    full = entries // TILE * TILE
    if full:
        vector[pl.ds(0, full)] = value[: full // LANES].reshape(full)
    if entries > full:
        vector[pl.ds(full, entries - full)] = value[full // LANES : full // LANES + 8].reshape(TILE)[: entries - full]


def align_kernel(place, attn, mlp, attn_out, mlp_out):
    for n, (source, target) in enumerate(((attn, attn_out), (mlp, mlp_out))):
        lanes, rows = place[2 * n], place[2 * n + 1]
        value = tall(source, target.shape[0])
        turned = pltpu.roll(value, lanes, 1)
        below = pltpu.roll(turned, 1, 0)
        lane = lax.broadcasted_iota(jnp.int32, value.shape, 1)
        moved = jnp.where(lane >= lanes, turned, below)
        target[...] = pltpu.roll(moved, rows, 0).astype(BF16)


def take_share(value, lanes, rows):
    height = value.shape[0]
    value = pltpu.roll(value, (height - rows) % height, 0)
    turned = pltpu.roll(value, (LANES - lanes) % LANES, 1)
    above = pltpu.roll(turned, height - 1, 0)
    lane = lax.broadcasted_iota(jnp.int32, value.shape, 1)
    return jnp.where(lane < LANES - lanes, turned, above)


def unpack(flat, arrays, entries, rows, me):
    flat[...] = jnp.zeros_like(flat)
    for ref, numbers in arrays:
        for t, number in enumerate(numbers):
            start = tile_row(entries, number ^ me)
            flat[pl.ds(start, rows), :] += ref[t * rows : (t + 1) * rows, :].astype(F32)


def read_matrix(flat, row, depth, cols, target):
    for c in range(cols):
        target[:, c * LANES : (c + 1) * LANES] = flat[pl.ds(row + c, depth, stride=cols), :].astype(BF16)


def read_row(flat, row, cols):
    return jnp.concatenate([flat[row + c : row + c + 1, :] for c in range(cols)], axis=1)


def write_row(flat, row, value):
    for c in range(value.shape[1] // LANES):
        flat[row + c : row + c + 1, :] = value[:, c * LANES : (c + 1) * LANES]


def norm_parts(value):
    average = jnp.mean(value, axis=-1, keepdims=True)
    centred = value - average
    variance = jnp.mean(centred * centred, axis=-1, keepdims=True)
    inverse = lax.rsqrt(variance + 1e-06)
    return centred * inverse, inverse


def norm_back(normed, inverse, gain, grad):
    scaled = grad * gain
    first = jnp.mean(scaled, axis=-1, keepdims=True)
    second = jnp.mean(scaled * normed, axis=-1, keepdims=True)
    return (scaled - first - normed * second) * inverse


def fold_rows(value):
    return jnp.sum(value.reshape(-1, 8, value.shape[-1]), axis=0)


def call(kernel, name, operands, outs, scratch, mebibytes, microseconds):
    return pl.pallas_call(
        kernel,
        in_specs=[SMEM_SPEC if a.dtype == jnp.int32 and a.ndim == 1 else VMEM_SPEC for a in operands],
        out_specs=[VMEM_SPEC] * len(outs),
        out_shape=[jax.ShapeDtypeStruct(shape, kind) for shape, kind in outs],
        scratch_shapes=scratch,
        compiler_params=params(mebibytes),
        cost_estimate=cost(microseconds),
        name=name,
    )(*operands)


def project_kernel(entries, attn_plan, pos_count, attn_rows, mlp_rows, me, pos_names, onehot, tokens, *refs):
    attn_arrays = [(refs[i], plan) for i, plan in enumerate(attn_plan)]
    refs = refs[len(attn_plan) :]
    pos_arrays, refs = refs[:pos_count], refs[pos_count:]
    embedded, normed_out, qkv, w_qkv, w_out, vectors = refs[:6]
    flat, pos_flat, pos_table = refs[6:]
    slots, rows = tokens.shape[0], embedded.shape[0]

    pos_flat[...] = jnp.zeros_like(pos_flat)
    for n, ref in enumerate(pos_arrays):
        start = tile_row(entries[1], pos_names[n])
        pos_flat[pl.ds(start, mlp_rows), :] += ref[...].astype(F32)
    pos_table[...] = jnp.zeros_like(pos_table)
    most = POS // 16 * 16
    for c in range(D_COLS):
        column = pos_flat[pl.ds(ROW_POS + c, most, stride=D_COLS), :]
        pos_table[0:most, c * LANES : (c + 1) * LANES] = column.astype(BF16)
    last = [read_row(pos_flat, ROW_POS + r * D_COLS, D_COLS) for r in range(most, POS)]
    last = jnp.concatenate(last + [jnp.zeros((16 - len(last), D), F32)], axis=0)
    pos_table[most : most + 16, :] = last.astype(BF16)

    unpack(flat, attn_arrays, entries[0], attn_rows, me[0])
    read_matrix(flat, ROW_W_QKV, D, QKV_COLS, w_qkv)
    read_matrix(flat, ROW_W_OUT, D, D_COLS, w_out)
    gain = read_row(flat, ROW_GAIN_ONE, D_COLS)
    bias = read_row(flat, ROW_BIAS_ONE, D_COLS)
    b_qkv = read_row(flat, ROW_B_QKV, QKV_COLS)
    vectors[...] = jnp.zeros_like(vectors)
    vectors[0:1, :] = gain
    vectors[1:2, :] = read_row(flat, ROW_B_OUT, D_COLS)

    embedded[0:slots, :] = tokens[...].astype(F32)
    embedded[slots:rows, :] = jnp.zeros((rows - slots, D), F32)
    for c in range(QKV_COLS):
        qkv[c, rows : qkv.shape[1], :] = jnp.zeros((qkv.shape[1] - rows, LANES), F32)

    def project(i, _):
        at = pl.ds(pl.multiple_of(i * PART, PART), PART)
        value = embedded[at, :] + dot(onehot[at, :], pos_table[...])
        embedded[at, :] = value
        normed, _ = norm_parts(value)
        normed = (normed * gain + bias).astype(BF16)
        normed_out[at, :] = normed
        for k in range(3):
            cols = slice(k * D, (k + 1) * D)
            part = (dot(normed, w_qkv[:, cols]) + b_qkv[:, cols]).astype(BF16).astype(F32)
            if k == 0:
                part = part * DH ** (-0.5)
            for c in range(D_COLS):
                qkv[k * D_COLS + c, at, :] = part[:, c * LANES : (c + 1) * LANES]
        return 0

    lax.fori_loop(0, rows // PART, project, 0)


def project(entries, attn_arrays, pos_arrays, pos_names, me, onehot, tokens, sizes):
    rows = onehot.shape[0]
    plan = [numbers for _, numbers in attn_arrays]
    operands = [me, pos_names, onehot, tokens] + [a for a, _ in attn_arrays] + list(pos_arrays)
    outs = [
        ((rows, D), F32),
        ((rows, D), BF16),
        ((QKV_COLS, sizes.reach, LANES), F32),
        ((D, 3 * D), BF16),
        ((D, D), BF16),
        ((8, D), F32),
    ]
    scratch = [
        pltpu.VMEM((sizes.attn_flat, LANES), F32),
        pltpu.VMEM((sizes.pos_flat, LANES), F32),
        pltpu.VMEM((256, D), BF16),
    ]
    kernel = functools.partial(
        project_kernel, entries, plan, len(pos_arrays), sizes.attn_rows, sizes.mlp_rows
    )
    return call(kernel, "project", operands, outs, scratch, 24, 8)


def image_table(lengths, table):
    images = table.shape[1]
    longs = sum((lengths[i] == LONG).astype(jnp.int32) for i in range(images))
    start, long_seen, short_seen = jnp.int32(0), jnp.int32(0), longs
    for i in range(images):
        length = lengths[i]
        is_long = length == LONG
        place = jnp.where(is_long, long_seen, short_seen)
        table[0, place] = start
        table[1, place] = length
        start = start + length
        long_seen = long_seen + is_long.astype(jnp.int32)
        short_seen = short_seen + 1 - is_long.astype(jnp.int32)
    return start


def image_rows(slot):
    return -(-((LONG if slot < MOST_LONG else SHORT) + 7) // 32) * 32


def both_heads(value):
    left = lax.broadcasted_iota(jnp.int32, value.shape, 1) < DH
    zero = jnp.zeros_like(value)
    return jnp.concatenate([jnp.where(left, value, zero), jnp.where(left, zero, value)], axis=0)


def one_of_heads(value):
    height = value.shape[0] // 2
    left = lax.broadcasted_iota(jnp.int32, (height, LANES), 1) < DH
    return jnp.where(left, value[:height], value[height:])


def inside(height, low, length):
    row = lax.broadcasted_iota(jnp.int32, (height, LANES), 0)
    return (row >= low) & (row < low + length)


def attend(queries, keys, values, mask):
    scores = dot(keys, both_heads(queries), NT)
    scores = jnp.where(mask, scores, -1e30)
    peak = jnp.max(scores, axis=0, keepdims=True)
    probs = jnp.exp(scores - peak)
    total = jnp.sum(probs, axis=0, keepdims=True)
    out = dot(values.T.astype(BF16), probs.astype(BF16)) * (1.0 / total)
    return one_of_heads(out.T), peak + jnp.log(total)


def key_mask(height, width, low, length):
    row = lax.broadcasted_iota(jnp.int32, (height, width), 0)
    return (row >= low) & (row < low + length)


def attend_kernel(slots, lengths, qkv, embedded, w_out, vectors, mixed, log_total, residual, table):
    images = lengths.shape[0]
    rows = residual.shape[0]
    live = image_table(lengths, table)
    mixed[...] = jnp.zeros_like(mixed)
    for slot in range(images):
        height = image_rows(slot)
        low = table[0, slot] % 8
        at = pl.ds(pl.multiple_of(table[0, slot] - low, 8), height)
        length = table[1, slot]
        mask = key_mask(height, 2 * height, low, length)
        valid = inside(height, low, length)
        for pair in range(PAIRS):
            out, total = attend(
                qkv[pair, at, :].astype(BF16),
                qkv[PAIRS + pair, at, :].astype(BF16),
                qkv[2 * PAIRS + pair, at, :],
                mask,
            )
            log_total[slot * PAIRS + pair, :, 0 : 2 * height] = total
            pltpu.store(mixed.at[pair, at, :], out.astype(BF16).astype(F32), mask=valid)

    low = live % 8
    base = pl.multiple_of(live - low, 8)
    length = slots - live
    most = -(-(slots - images * SHORT + 7) // BLOCK) if (images * SHORT) % 8 else -(-(slots - images * SHORT) // BLOCK)
    for blocks in range(1, most + 1):

        @pl.when((low + length > (blocks - 1) * BLOCK) & (low + length <= blocks * BLOCK))
        def _():
            height = blocks * BLOCK
            mask = key_mask(height, 2 * BLOCK, low, length)
            for pair in range(PAIRS):
                keys = qkv[PAIRS + pair, pl.ds(base, height), :].astype(BF16)
                values = qkv[2 * PAIRS + pair, pl.ds(base, height), :]
                for block in range(blocks):
                    at = pl.ds(pl.multiple_of(base + block * BLOCK, 8), BLOCK)
                    out, _ = attend(qkv[pair, at, :].astype(BF16), keys, values, mask)
                    valid = inside(BLOCK, low - block * BLOCK, length)
                    pltpu.store(mixed.at[pair, at, :], out.astype(BF16).astype(F32), mask=valid)

    def finish(i, _):
        at = pl.ds(pl.multiple_of(i * PART, PART), PART)
        together = jnp.concatenate([mixed[c, at, :] for c in range(D_COLS)], axis=1).astype(BF16)
        residual[at, :] = embedded[at, :] + dot(together, w_out[...]) + vectors[1:2, :]
        return 0

    lax.fori_loop(0, rows // PART, finish, 0)


def attend_all(slots, lengths, qkv, embedded, w_out, vectors):
    rows = embedded.shape[0]
    images = lengths.shape[0]
    outs = [((PAIRS,) + qkv.shape[1:], F32), ((images * PAIRS, 1, 2 * image_rows(0)), F32), ((rows, D), F32)]
    scratch = [pltpu.SMEM((2, images), jnp.int32)]
    operands = [lengths, qkv, embedded, w_out, vectors]
    return call(functools.partial(attend_kernel, slots), "attend", operands, outs, scratch, 24, 10)


def gelu_parts(value):
    size = jnp.abs(value)
    near = 1.0 / (1.0 + (0.3275911 * math.sqrt(0.5)) * size)
    bell = jnp.exp(-0.5 * value * value)
    series = near * (
        0.5 * 0.254829592
        + near
        * (0.5 * -0.284496736 + near * (0.5 * 1.421413741 + near * (0.5 * -1.453152027 + near * (0.5 * 1.061405429))))
    )
    tail = series * bell
    share = jnp.where(value >= 0, 1.0 - tail, tail)
    return value * share, share + value * bell * (1.0 / math.sqrt(2.0 * math.pi))


def pack(flat, entries, rows, me, targets):
    for ref, numbers in targets:
        for t, number in enumerate(numbers):
            start = tile_row(entries, number ^ me)
            ref[t * rows : (t + 1) * rows, :] = flat[pl.ds(start, rows), :].astype(BF16)


def mlp_kernel(entries, in_plan, out_plan, piece, mask, me, lengths, residual, cotangent, *refs):
    arrays = [(refs[i], plan) for i, plan in enumerate(in_plan)]
    refs = refs[len(in_plan) :]
    output, d_residual = refs[:2]
    targets = [(refs[2 + i], plan) for i, plan in enumerate(out_plan)]
    refs = refs[2 + len(out_plan) :]
    flat, w_in, w_back, normed_b, active_b, d_hidden_b, out_f32, sums_in, sums, out_grad = refs
    slots, rows = cotangent.shape[0], residual.shape[0]
    live = sum(lengths[i] for i in range(lengths.shape[0]))
    row = lax.broadcasted_iota(jnp.int32, (slots, D), 0)
    out_grad[0:slots, :] = jnp.where(row < live, cotangent[...].astype(F32), 0.0).astype(BF16)
    out_grad[slots:rows, :] = jnp.zeros((rows - slots, D), BF16)

    unpack(flat, arrays, entries, piece, mask[0])
    read_matrix(flat, ROW_W_IN, D, FF_COLS, w_in)
    read_matrix(flat, ROW_W_BACK, FF, D_COLS, w_back)
    gain = read_row(flat, ROW_GAIN_TWO, D_COLS)
    bias = read_row(flat, ROW_BIAS_TWO, D_COLS)
    b_in = read_row(flat, ROW_B_IN, FF_COLS)
    b_back = read_row(flat, ROW_B_BACK, D_COLS)
    sums[...] = jnp.zeros_like(sums)
    sums_in[...] = jnp.zeros_like(sums_in)

    def step(i, _):
        at = pl.ds(pl.multiple_of(i * PART, PART), PART)
        value = residual[at, :]
        grad_b = out_grad[at, :]
        normed, inverse = norm_parts(value)
        low = (normed * gain + bias).astype(BF16)
        normed_b[at, :] = low
        for c in range(FF // 256):
            cols = slice(c * 256, (c + 1) * 256)
            hidden = dot(low, w_in[:, cols]) + b_in[:, cols]
            d_active = dot(grad_b, w_back[cols, :], NT)
            active, slope = gelu_parts(hidden)
            d_hidden = (d_active * slope).astype(BF16)
            active_b[at, cols] = active.astype(BF16)
            d_hidden_b[at, cols] = d_hidden
            sums_in[:, cols] += fold_rows(d_hidden.astype(F32))
        out_f32[at, :] = value + b_back + dot(active_b[at, :], w_back[...])
        d_normed = dot(d_hidden_b[at, :], w_in[...], NT)
        grad = grad_b.astype(F32)
        d_residual[at, :] = grad + norm_back(normed, inverse, gain, d_normed)
        sums[0] += fold_rows(d_normed * normed)
        sums[1] += fold_rows(d_normed)
        sums[2] += fold_rows(grad)
        return 0

    lax.fori_loop(0, rows // PART, step, 0)
    output[...] = out_f32[0 : output.shape[0], :].astype(BF16)

    flat[...] = jnp.zeros_like(flat)
    write_row(flat, ROW_GAIN_TWO, jnp.sum(sums[0], axis=0, keepdims=True))
    write_row(flat, ROW_BIAS_TWO, jnp.sum(sums[1], axis=0, keepdims=True))
    write_row(flat, ROW_B_IN, jnp.sum(sums_in[...], axis=0, keepdims=True))
    write_row(flat, ROW_B_BACK, jnp.sum(sums[2], axis=0, keepdims=True))
    normed_t = normed_b[...].T
    for c in range(0, FF_COLS, 2):
        part = dot(normed_t, d_hidden_b[:, c * LANES : (c + 2) * LANES])
        for k in range(2):
            flat[pl.ds(ROW_W_IN + c + k, D, stride=FF_COLS), :] = part[:, k * LANES : (k + 1) * LANES]
    for r in range(0, FF, 256):
        part = dot(active_b[:, r : r + 256], out_grad[...], TN)
        for c in range(D_COLS):
            flat[pl.ds(ROW_W_BACK + r * D_COLS + c, 256, stride=D_COLS), :] = part[:, c * LANES : (c + 1) * LANES]
    pack(flat, entries, piece, me[0], targets)


def mlp_both(entries, arrays, mask, me, lengths, residual, cotangent, out_plan, sizes):
    rows = residual.shape[0]
    plan = [numbers for _, numbers in arrays]
    operands = [mask, me, lengths, residual, cotangent] + [a for a, _ in arrays]
    outs = [(cotangent.shape, BF16), ((rows, D), F32)]
    outs += [((len(n) * sizes.mlp_rows, LANES), BF16) for n in out_plan]
    scratch = [
        pltpu.VMEM((sizes.mlp_flat, LANES), F32),
        pltpu.VMEM((D, FF), BF16),
        pltpu.VMEM((FF, D), BF16),
        pltpu.VMEM((rows, D), BF16),
        pltpu.VMEM((rows, FF), BF16),
        pltpu.VMEM((rows, FF), BF16),
        pltpu.VMEM((rows, D), F32),
        pltpu.VMEM((8, FF), F32),
        pltpu.VMEM((3, 8, D), F32),
        pltpu.VMEM((rows, D), BF16),
    ]
    kernel = functools.partial(mlp_kernel, entries, plan, out_plan, sizes.mlp_rows)
    return call(kernel, "feed_forward", operands, outs, scratch, 36, 18)


def attend_back_kernel(lengths, qkv, mixed, log_total, w_out, d_residual, d_qkv, d_branch_b, b_out_sum, d_mixed, table):
    images = lengths.shape[0]
    rows = d_residual.shape[0]
    image_table(lengths, table)
    d_qkv[...] = jnp.zeros_like(d_qkv)
    b_out_sum[...] = jnp.zeros_like(b_out_sum)

    def enter(i, _):
        at = pl.ds(pl.multiple_of(i * PART, PART), PART)
        branch = d_residual[at, :].astype(BF16)
        d_branch_b[at, :] = branch
        b_out_sum[...] += fold_rows(branch.astype(F32))
        value = dot(branch, w_out[...], NT).astype(BF16).astype(F32)
        for c in range(D_COLS):
            d_mixed[c, at, :] = value[:, c * LANES : (c + 1) * LANES]
        return 0

    lax.fori_loop(0, rows // PART, enter, 0)
    for c in range(D_COLS):
        d_mixed[c, rows : d_mixed.shape[1], :] = jnp.zeros((d_mixed.shape[1] - rows, LANES), F32)

    ones = jnp.ones((8, LANES), BF16)
    for slot in range(images):
        height = image_rows(slot)
        low = table[0, slot] % 8
        at = pl.ds(pl.multiple_of(table[0, slot] - low, 8), height)
        length = table[1, slot]
        mask = key_mask(height, 2 * height, low, length)
        valid = inside(height, low, length)
        for pair in range(PAIRS):
            queries = both_heads(qkv[pair, at, :].astype(BF16))
            keys = qkv[PAIRS + pair, at, :]
            grad = jnp.where(valid, d_mixed[pair, at, :], 0.0)
            grads = both_heads(grad.astype(BF16))
            scores = dot(keys.astype(BF16), queries, NT)
            scores = jnp.where(mask, scores, -1e30)
            probs = jnp.exp(scores - log_total[slot * PAIRS + pair, :, 0 : 2 * height])
            product = both_heads(grad * mixed[pair, at, :])
            upper = product.astype(BF16)
            lower = (product - upper.astype(F32)).astype(BF16)
            delta = (dot(ones, upper, NT) + dot(ones, lower, NT))[0:1, :]
            d_probs = dot(qkv[2 * PAIRS + pair, at, :].astype(BF16), grads, NT)
            d_scores = (probs * (d_probs - delta)).astype(BF16)
            d_values = dot(probs.astype(BF16), grads)
            d_keys = dot(d_scores, queries)
            d_queries = one_of_heads((dot(keys.T.astype(BF16), d_scores) * DH ** (-0.5)).T)
            pltpu.store(d_qkv.at[pair, at, :], d_queries, mask=valid)
            pltpu.store(d_qkv.at[PAIRS + pair, at, :], d_keys, mask=valid)
            pltpu.store(d_qkv.at[2 * PAIRS + pair, at, :], d_values, mask=valid)


def attend_back(lengths, qkv, mixed, log_total, w_out, d_residual):
    rows = d_residual.shape[0]
    outs = [(qkv.shape, F32), ((rows, D), BF16), ((8, D), F32)]
    scratch = [pltpu.VMEM(mixed.shape, F32), pltpu.SMEM((2, lengths.shape[0]), jnp.int32)]
    operands = [lengths, qkv, mixed, log_total, w_out, d_residual]
    return call(attend_back_kernel, "attend_back", operands, outs, scratch, 28, 12)


def project_back_kernel(entries, out_plan, piece, me, *refs):
    (onehot, embedded, normed_b, mixed, d_qkv, d_branch_b, b_out_sum, w_qkv, vectors, d_residual) = refs[:10]
    in_grad, pos_out = refs[10:12]
    targets = [(refs[12 + i], plan) for i, plan in enumerate(out_plan)]
    flat, d_qkv_b, d_embedded_b, mixed_b, sums = refs[12 + len(out_plan) :]
    rows = embedded.shape[0]
    gain = vectors[0:1, :]
    sums[...] = jnp.zeros_like(sums)

    def leave(i, _):
        at = pl.ds(pl.multiple_of(i * PART, PART), PART)
        grads = jnp.concatenate([d_qkv[c, at, :] for c in range(QKV_COLS)], axis=1).astype(BF16)
        d_qkv_b[at, :] = grads
        mixed_b[at, :] = jnp.concatenate([mixed[c, at, :] for c in range(D_COLS)], axis=1).astype(BF16)
        d_normed = dot(grads, w_qkv[...], NT)
        normed, inverse = norm_parts(embedded[at, :])
        value = d_residual[at, :] + norm_back(normed, inverse, gain, d_normed)
        d_embedded_b[at, :] = value.astype(BF16)
        sums[0] += fold_rows(d_normed * normed)
        sums[1] += fold_rows(d_normed)
        return 0

    lax.fori_loop(0, rows // PART, leave, 0)
    in_grad[...] = d_embedded_b[0 : in_grad.shape[0], :]

    flat[...] = jnp.zeros_like(flat)
    write_row(flat, ROW_GAIN_ONE, jnp.sum(sums[0], axis=0, keepdims=True))
    write_row(flat, ROW_BIAS_ONE, jnp.sum(sums[1], axis=0, keepdims=True))
    write_row(flat, ROW_B_OUT, jnp.sum(b_out_sum[...], axis=0, keepdims=True))
    normed_t = normed_b[...].T
    for k in range(3):
        cols = slice(k * D, (k + 1) * D)
        part = dot(normed_t, d_qkv_b[:, cols])
        total = jnp.sum(fold_rows(d_qkv_b[:, cols].astype(F32)), axis=0, keepdims=True)
        write_row(flat, ROW_B_QKV + k * D_COLS, total)
        for c in range(D_COLS):
            flat[pl.ds(ROW_W_QKV + k * D_COLS + c, D, stride=QKV_COLS), :] = part[:, c * LANES : (c + 1) * LANES]
    part = dot(mixed_b[...].T, d_branch_b[...])
    for c in range(D_COLS):
        flat[pl.ds(ROW_W_OUT + c, D, stride=D_COLS), :] = part[:, c * LANES : (c + 1) * LANES]
    pack(flat, entries, piece, me[0], targets)

    pos_grad = dot(onehot[...], d_embedded_b[...], TN)
    flat[...] = jnp.zeros_like(flat)
    for c in range(D_COLS):
        flat[pl.ds(ROW_POS + c, POS, stride=D_COLS), :] = pos_grad[0:POS, c * LANES : (c + 1) * LANES]
    pos_out[...] = flat[0 : pos_out.shape[0], :].astype(BF16)


def project_back(entries, me, kept, out_rows, out_plan, sizes):
    rows = kept[1].shape[0]
    outs = [((out_rows, D), BF16), ((sizes.pos_flat, LANES), BF16)]
    outs += [((len(n) * sizes.attn_rows, LANES), BF16) for n in out_plan]
    scratch = [
        pltpu.VMEM((max(sizes.attn_flat, sizes.pos_flat), LANES), F32),
        pltpu.VMEM((rows, 3 * D), BF16),
        pltpu.VMEM((rows, D), BF16),
        pltpu.VMEM((rows, D), BF16),
        pltpu.VMEM((2, 8, D), F32),
    ]
    kernel = functools.partial(project_back_kernel, entries, out_plan, sizes.attn_rows)
    return call(kernel, "project_back", [me, *kept], outs, scratch, 28, 10)


def adamw_step(gradient, weights, first, second):
    first_new = BETA_FIRST * first + (1.0 - BETA_FIRST) * gradient
    second_new = BETA_SECOND * second + (1.0 - BETA_SECOND) * gradient * gradient
    first_hat = first_new / (1.0 - BETA_FIRST**STEP)
    second_hat = second_new / (1.0 - BETA_SECOND**STEP)
    update = LEARNING_RATE * (first_hat / (jnp.sqrt(second_hat) + adam_eps) + WEIGHT_DECAY * weights)
    return (update, first_new, second_new)


def settle_kernel(scale, counts, place, *refs):
    attn = refs[: counts[0]]
    mlp = refs[counts[0] : counts[0] + counts[1]]
    pos = refs[counts[0] + counts[1] : sum(counts)]
    refs = refs[sum(counts) :]
    state, outs = (refs[:3], refs[3:6]), (refs[6:10], refs[10:14])
    total = sum(ref[...].astype(F32) for ref in attn)
    extra = sum(ref[...].astype(F32) for ref in pos)
    other = sum(ref[...].astype(F32) for ref in mlp) + jnp.where(place[4] > 0, extra, 0.0)
    for n, value in enumerate((total, other)):
        rows = value.shape[0]
        gradient = take_share(value, place[2 * n], place[2 * n + 1]) * scale
        weights, first, second = (tall(ref, rows) for ref in state[n])
        for ref, result in zip(outs[n], (gradient, *adamw_step(gradient, weights, first, second))):
            put_flat(ref, result)


def settle(scale, place, attn, mlp, pos, attn_state, mlp_state):
    operands = list(attn) + list(mlp) + list(pos) + list(attn_state) + list(mlp_state)
    shapes = [attn_state[0].shape] * 4 + [mlp_state[0].shape] * 4
    return pl.pallas_call(
        functools.partial(settle_kernel, scale, (len(attn), len(mlp), len(pos))),
        in_specs=[SMEM_SPEC] + [VMEM_SPEC] * len(operands),
        out_specs=[VMEM_SPEC] * len(shapes),
        out_shape=[jax.ShapeDtypeStruct(shape, F32) for shape in shapes],
        compiler_params=params(8),
        name="settle",
    )(place, *operands)


AXES = ("dp", "rep")
BIT_CORE, BIT_X, BIT_Y, BIT_Z = 1, 2, 4, 8
PLANE = (BIT_X, BIT_Y, BIT_X | BIT_Y)
DEVICES = 32


def swap(value, bits):
    return lax.ppermute(value, AXES, [(j, j ^ bits) for j in range(DEVICES)])


def together(*values):
    return lax.optimization_barrier(values)


def spread_z(piece):
    return [piece] + [swap(piece, k * BIT_Z) for k in (1, 2, 3)]


def spread_xy(value):
    return [value] + [swap(value, bits) for bits in PLANE]


def numbered(arrays):
    offsets = [core | bits for core in (0, BIT_CORE) for bits in (0, *PLANE)]
    return [(a, [offset | z * BIT_Z for z in range(4)]) for a, offset in zip(arrays, offsets)]


def sum_plan():
    return [[BIT_CORE | bits | z * BIT_Z for bits in (0, *PLANE) for z in range(4)]] + [
        [bits | z * BIT_Z for z in range(4)] for bits in (0, *PLANE)
    ]


def total(values):
    return sum(value.astype(F32) for value in values).astype(BF16)


def quarters(value):
    return [value[k * value.shape[0] // 4 : (k + 1) * value.shape[0] // 4] for k in range(4)]


def add_core(sent):
    came = quarters(swap(sent[0], BIT_CORE))
    return [total(both) for both in zip(sent[1:], came)]


def swap_xy(parts):
    return [parts[0]] + [swap(part, bits) for part, bits in zip(parts[1:], PLANE)]


def swap_z(parts):
    return [parts[0]] + [swap(parts[k], k * BIT_Z) for k in (1, 2, 3)]


class Sizes:
    def __init__(self, count, slots, attn_entries, mlp_entries):
        self.attn_rows = piece_rows(attn_entries, count)
        self.mlp_rows = piece_rows(mlp_entries, count)
        self.attn_flat = max(flat_rows(attn_entries, count, self.attn_rows), ATTN_ROWS)
        self.mlp_flat = max(flat_rows(mlp_entries, count, self.mlp_rows), MLP_ROWS)
        self.pos_count = -(-POS * D // mlp_entries)
        self.pos_flat = flat_rows(mlp_entries, self.pos_count, self.mlp_rows)
        self.pos_flat = max(-(-self.pos_flat // 16) * 16, -(-POS * D_COLS // 16) * 16)
        self.reach = slots + max(image_rows(0), 2 * BLOCK)


class Layer:
    def __init__(self, entries, sizes, slots, tokens, cotangent, lengths, onehot):
        self.entries, self.sizes, self.slots = entries, sizes, slots
        self.tokens, self.cotangent, self.lengths, self.onehot = tokens, cotangent, lengths, onehot

    def project(self, mask, attn_arrays, pos_arrays, pos_names):
        self.mask = mask
        (self.embedded, self.normed_b, self.qkv, self.w_qkv, self.w_out, self.vectors) = project(
            self.entries, attn_arrays, pos_arrays, pos_names, mask, self.onehot, self.tokens, self.sizes
        )

    def attend(self):
        self.mixed, self.log_total, self.residual = attend_all(
            self.slots, self.lengths, self.qkv, self.embedded, self.w_out, self.vectors
        )

    def feed_forward(self, mlp_arrays, mask, plan):
        self.output, self.d_residual, *sent = mlp_both(
            self.entries[1], mlp_arrays, mask, self.mask, self.lengths, self.residual, self.cotangent, plan, self.sizes
        )
        return sent

    def attend_back(self):
        self.d_qkv, self.d_branch_b, self.b_out_sum = attend_back(
            self.lengths, self.qkv, self.mixed, self.log_total, self.w_out, self.d_residual
        )

    def project_back(self, plan):
        kept = (self.onehot, self.embedded, self.normed_b, self.mixed, self.d_qkv, self.d_branch_b)
        kept += (self.b_out_sum, self.w_qkv, self.vectors, self.d_residual)
        self.in_grad, pos_grad, *sent = project_back(self.entries[0], self.mask, kept, self.slots, plan, self.sizes)
        return pos_grad, sent


def step_by_axes(layer, me, attn_piece, mlp_piece):
    sizes, count = layer.sizes, lax.axis_size("dp") * lax.axis_size("rep")
    order = list(range(count))
    height = sizes.mlp_rows
    attn_all = lax.all_gather(attn_piece, AXES, axis=0, tiled=True)
    mlp_all = lax.all_gather(mlp_piece, AXES, axis=0, tiled=True)
    pos_arrays = [mlp_all[j * height : (j + 1) * height] for j in range(sizes.pos_count)]
    pos_names = jnp.arange(sizes.pos_count, dtype=jnp.int32)
    layer.project(jnp.zeros((1,), jnp.int32), [(attn_all, order)], pos_arrays, pos_names)
    layer.attend()
    mlp_sent = layer.feed_forward([(mlp_all, order)], layer.mask, [order])
    layer.attend_back()
    pos_grad, attn_sent = layer.project_back([order])
    mlp_terms = [lax.psum_scatter(mlp_sent[0], AXES, scatter_dimension=0, tiled=True)]
    attn_terms = [lax.psum_scatter(attn_sent[0], AXES, scatter_dimension=0, tiled=True)]
    pos_sum = jnp.pad(lax.psum(pos_grad, AXES), ((0, height), (0, 0)))
    first_row = jnp.minimum((me * layer.entries[1]) // TILE * 8, sizes.pos_flat)
    pos_terms = [lax.dynamic_slice_in_dim(pos_sum, first_row, height, axis=0)]
    return (layer.output, layer.in_grad), (attn_terms, mlp_terms, pos_terms)


def step_by_hand(layer, me, attn_piece, mlp_piece):
    sizes = layer.sizes
    z, plane, core = me // BIT_Z, (me // BIT_X) % 4, me % 2
    plan = sum_plan()
    attn_z, mlp_z = spread_z(attn_piece), spread_z(mlp_piece)
    attn_z, layer.onehot = together(attn_z, layer.onehot)
    attn = jnp.concatenate(attn_z, axis=0)
    attn = spread_xy(attn)
    pos = lax.select_n(z, *mlp_z)
    pos = lax.select_n(plane, *spread_xy(pos))
    attn, pos, mlp_z = together(attn, pos, mlp_z)
    attn = attn + [swap(a, BIT_CORE) for a in attn]
    pos_arrays = [pos, swap(pos, BIT_CORE)]
    pos_names = jnp.stack([core, 1 - core])
    mlp = jnp.concatenate(mlp_z, axis=0)
    attn, pos_arrays, mlp = together(attn, pos_arrays, mlp)
    mlp = spread_xy(mlp)
    layer.project(me.reshape(1), numbered(attn), pos_arrays, pos_names)
    layer.attend()
    mlp, layer.residual = together(mlp, layer.residual)
    mlp = mlp + [swap(a, BIT_CORE) for a in mlp]
    mlp_sent = layer.feed_forward(numbered(mlp), layer.mask, plan)

    parts = add_core(mlp_sent)
    parts, layer.d_residual = together(parts, layer.d_residual)
    mlp_terms = swap_xy(parts)
    layer.attend_back()
    pos_grad, attn_sent = layer.project_back(plan)
    mlp_terms, pos_grad, attn_sent = together(mlp_terms, pos_grad, attn_sent)

    offset = layer.entries[1] // TILE * 8
    pos_parts = [pos_grad[: sizes.mlp_rows], pos_grad[offset : offset + sizes.mlp_rows]]
    pos_keep = jnp.where(core == 0, pos_parts[0], pos_parts[1])
    pos_send = jnp.where(core == 0, pos_parts[1], pos_parts[0])
    parts, pos = add_core(attn_sent), total([pos_keep, swap(pos_send, BIT_CORE)])
    mlp_parts = quarters(total(mlp_terms))
    parts, pos, mlp_parts = together(parts, pos, mlp_parts)
    attn_terms, pos_terms = swap_xy(parts), spread_xy(pos)
    mlp_terms = swap_z(mlp_parts)
    parts, pos = quarters(total(attn_terms)), total(pos_terms)
    parts, pos = together(parts, pos)
    attn_terms, pos_terms = swap_z(parts), spread_z(pos)
    return (layer.output, layer.in_grad), (attn_terms, mlp_terms, pos_terms)


def body(
    by_hand,
    tokens,
    cotangent,
    lengths,
    pos_map,
    attn_params,
    attn_first,
    attn_second,
    mlp_params,
    mlp_first,
    mlp_second,
):
    slots = tokens.shape[0]
    rows = -(-slots // PART) * PART
    count = lax.axis_size("dp") * lax.axis_size("rep")
    entries = (attn_params.shape[0], mlp_params.shape[0])
    sizes = Sizes(count, slots, *entries)
    me = lax.axis_index("dp") * lax.axis_size("rep") + lax.axis_index("rep")
    me = me.astype(jnp.int32)

    starts = [(me * n) % TILE for n in entries]
    place = jnp.stack(
        [starts[0] % LANES, starts[0] // LANES, starts[1] % LANES, starts[1] // LANES, (me < 2).astype(jnp.int32)]
    )
    attn_piece, mlp_piece = pl.pallas_call(
        align_kernel,
        in_specs=[SMEM_SPEC, VMEM_SPEC, VMEM_SPEC],
        out_specs=[VMEM_SPEC, VMEM_SPEC],
        out_shape=[
            jax.ShapeDtypeStruct((sizes.attn_rows, LANES), BF16),
            jax.ShapeDtypeStruct((sizes.mlp_rows, LANES), BF16),
        ],
        compiler_params=params(8),
        name="align",
    )(place, attn_params, mlp_params)

    pos_full = jnp.pad(pos_map, (0, rows - slots), constant_values=255)
    onehot = (pos_full[:, None] == jnp.arange(256, dtype=jnp.int32)[None, :]).astype(BF16)
    layer = Layer(entries, sizes, slots, tokens, cotangent, lengths, onehot)
    if by_hand:
        outputs, terms = step_by_hand(layer, me, attn_piece, mlp_piece)
    else:
        outputs, terms = step_by_axes(layer, me, attn_piece, mlp_piece)
        place = place.at[4].set(1)
    scale = 1.0 / math.sqrt(slots * count)
    attn_state, mlp_state = (attn_params, attn_first, attn_second), (mlp_params, mlp_first, mlp_second)
    updated = settle(scale, place, *terms, attn_state, mlp_state)
    return (*outputs, *updated)


def solution(mesh):
    split = P(AXES)
    split_rows = P(AXES, None)
    by_hand = mesh.shape["dp"] == 8 and mesh.shape["rep"] == 4
    return jax.shard_map(
        functools.partial(body, by_hand),
        mesh=mesh,
        in_specs=(split_rows, split_rows) + (split,) * 8,
        out_specs=(split_rows, split_rows) + (split,) * 8,
        check_vma=False,
    )
```

profile of v0, /device:TPU:0, one launch (start us, length us, event | category | flops | bytes accessed | tf_op | source)
XLA Modules:
  0.0 143.8 jit_solution(10808517799382685247)
XLA Ops:
  3.3 5.1 %collective-permute-start.2 = (bf16[160,128]{1,0:T(8,128)(2,1)S(1)}, bf16[160,128]{1,0:T(8,128)(2,1)S(1)}, u32[]{:S(2)}, u32[]{:S(2)}) collective-permute-start(bf16[160,128]{1,0:T(8,128)(2,1)S(1)} %get-tuple-element.106), channel_id=1, source_target_pairs={{0,24},{1,25},{2,26},{3,27},{4,28},{5,29},{6,30},{7,31},{8,16},{9,... | collective-permute-start | bytes 122888 | tf_op jit(solution)/shard_map/ppermute | solution.py:656
  9.1 3.7 %collective-permute-start.8 = (bf16[320,128]{1,0:T(8,128)(2,1)S(1)}, bf16[320,128]{1,0:T(8,128)(2,1)S(1)}, u32[]{:S(2)}, u32[]{:S(2)}) collective-permute-start(bf16[320,128]{1,0:T(8,128)(2,1)S(1)} %get-tuple-element.116), channel_id=1, source_target_pairs={{0,24},{1,25},{2,26},{3,27},{4,28},{5,29},{6,30},{7,31},{8,16},{9,... | collective-permute-start | bytes 245768 | tf_op jit(solution)/shard_map/ppermute | solution.py:656
  14.5 2.8 %collective-permute-done.1 = bf16[160,128]{1,0:T(8,128)(2,1)S(1)} collective-permute-done((bf16[160,128]{1,0:T(8,128)(2,1)S(1)}, bf16[160,128]{1,0:T(8,128)(2,1)S(1)}, u32[]{:S(2)}, u32[]{:S(2)}) %collective-permute-start.1) | collective-permute-done | bytes 40992 | tf_op jit(solution)/shard_map/ppermute | solution.py:656
  17.4 2.5 %collective-permute-done.7 = bf16[320,128]{1,0:T(8,128)(2,1)S(1)} collective-permute-done((bf16[320,128]{1,0:T(8,128)(2,1)S(1)}, bf16[320,128]{1,0:T(8,128)(2,1)S(1)}, u32[]{:S(2)}, u32[]{:S(2)}) %collective-permute-start.7) | collective-permute-done | bytes 81952 | tf_op jit(solution)/shard_map/ppermute | solution.py:656
  19.9 2.5 %collective-permute-start.11 = (bf16[320,128]{1,0:T(8,128)(2,1)S(1)}, bf16[320,128]{1,0:T(8,128)(2,1)S(1)}, u32[]{:S(2)}, u32[]{:S(2)}) collective-permute-start(bf16[320,128]{1,0:T(8,128)(2,1)S(1)} %select_select_fusion.1), channel_id=1, source_target_pairs={{0,6},{1,7},{2,4},{3,5},{4,2},{5,3},{6,0},{7,1},{8,14},{9,15},{10,... | collective-permute-start | bytes 245768 | tf_op jit(solution)/shard_map/ppermute | solution.py:656
  23.5 2.4 %collective-permute-start.5 = (bf16[640,128]{1,0:T(8,128)(2,1)S(1)}, bf16[640,128]{1,0:T(8,128)(2,1)S(1)}, u32[]{:S(2)}, u32[]{:S(2)}) collective-permute-start(bf16[640,128]{1,0:T(8,128)(2,1)S(1)} %constant_dynamic-update-slice_fusion.refs_0_), channel_id=1, source_target_pairs={{0,6},{1,7},{2,4},{3,5},{4,2},{5,3},{6,0},{7,1},{8,14},{9,15},{10,... | collective-permute-start | bytes 491528 | tf_op jit(solution)/shard_map/ppermute | solution.py:656
  27.6 1.8 %collective-permute-done.10 = bf16[320,128]{1,0:T(8,128)(2,1)S(1)} collective-permute-done((bf16[320,128]{1,0:T(8,128)(2,1)S(1)}, bf16[320,128]{1,0:T(8,128)(2,1)S(1)}, u32[]{:S(2)}, u32[]{:S(2)}) %collective-permute-start.10) | collective-permute-done | bytes 81952 | tf_op jit(solution)/shard_map/ppermute | solution.py:656
  29.4 3.0 %collective-permute-done.5.refs_3_ = bf16[640,128]{1,0:T(8,128)(2,1)S(1)} collective-permute-done((bf16[640,128]{1,0:T(8,128)(2,1)S(1)}, bf16[640,128]{1,0:T(8,128)(2,1)S(1)}, u32[]{:S(2)}, u32[]{:S(2)}) %collective-permute-start.5) | collective-permute-done | bytes 163872 | tf_op jit(solution)/shard_map/ppermute | solution.py:656
  32.5 1.4 collective-permute-done.4.refs_2_
  36.3 1.4 collective-permute-start.19
  39.8 5.0 %project.1 = (f32[1024,384]{1,0:T(8,128)S(1)}, bf16[1024,384]{1,0:T(8,128)(2,1)S(1)}, f32[9,1240,128]{2,1,0:T(8,128)S(1)}, bf16[384,1152]{1,0:T(8,128)(2,1)S(1)}...) custom-call(s32[1]{0:T(128)} %bitcast.me.mask, s32[2]{0:T(128)S(1)} %pad_add_fusion.pos_names, ...), custom_call_target="tpu_custom_call" | custom-call | flops 9200000000 | bytes 1024 | tf_op jit(solution)/shard_map/project/pallas_call | solution.py:175
  44.9 10.1 %attend.1 = (f32[3,1240,128]{2,1,0:T(8,128)S(1)}, f32[36,1,320]{2,1,0:T(1,128)S(1)}, f32[1024,384]{1,0:T(8,128)S(1)}) custom-call(s32[12]{0:T(128)S(1)} %copy-done.10, f32[9,1240,128]{2,1,0:T(8,128)S(1)} %get-tuple-element.132.qkv, f32[1024,384]{1,0:T(8,128)S(1)} %get-tuple-element.133.embedded.refs_1_, bf16[384,384]{1,0:T(8,128)(2,1)S(1)} %get-tuple-element.134.w_out, ...), custom_call_target="tpu_custom_call" | custom-call | flops 11500000256 | bytes 1024 | tf_op jit(solution)/shard_map/attend/pallas_call | solution.py:175
  59.7 18.7 %feed_forward.1 = (bf16[984,384]{1,0:T(8,128)(2,1)}, f32[1024,384]{1,0:T(8,128)S(1)}, bf16[5120,128]{1,0:T(8,128)(2,1)S(1)}, bf16[1280,128]{1,0:T(8,128)(2,1)S(1...) custom-call(s32[1]{0:T(128)} %bitcast.me.mask, s32[1]{0:T(128)} %bitcast.me.mask, ...), custom_call_target="tpu_custom_call" | custom-call | flops 20700000256 | bytes 1024 | tf_op jit(solution)/shard_map/feed_forward/pallas_call | solution.py:175
  80.0 2.8 %collective-permute-done.24 = bf16[5120,128]{1,0:T(8,128)(2,1)} collective-permute-done((bf16[5120,128]{1,0:T(8,128)(2,1)S(1)}, bf16[5120,128]{1,0:T(8,128)(2,1)}, u32[]{:S(2)}, u32[]{:S(2)}) %collective-permute-start.24) | collective-permute-done | bytes 1310752 | tf_op jit(solution)/shard_map/ppermute | solution.py:656
  82.8 1.8 %add_convert_fusion.1 = (bf16[1280,128]{1,0:T(8,128)(2,1)S(1)}, bf16[1280,128]{1,0:T(8,128)(2,1)S(1)}, bf16[1280,128]{1,0:T(8,128)(2,1)S(1)}, bf16[1280,128]{1,0:T(8,128)(2,1)S(1)}) fusion(bf16[1280,128]{1,0:T(8,128)(2,1)S(1)} %get-tuple-element.150, bf16[5120,128]{1,0:T(8,128)(2,1)} %collective-permute-done.24, bf16[1280,128]{1,0:T(8,128)(2,1)S(1)} %get-tuple-element.149, ...), kind=kLoop, calls=%fused_computation.3 | loop fusion | flops 2621440 | bytes 3932160 | tf_op jit(solution)/shard_map/convert_element_type | solution.py:683
  84.5 3.5 %collective-permute-start.25 = (bf16[1280,128]{1,0:T(8,128)(2,1)S(1)}, bf16[1280,128]{1,0:T(8,128)(2,1)S(1)}, u32[]{:S(2)}, u32[]{:S(2)}) collective-permute-start(bf16[1280,128]{1,0:T(8,128)(2,1)S(1)} %get-tuple-element.159), channel_id=1, source_target_pairs={{0,2},{1,3},{2,0},{3,1},{4,6},{5,7},{6,4},{7,5},{8,10},{9,11},{10,... | collective-permute-start | bytes 983048 | tf_op jit(solution)/shard_map/ppermute | solution.py:656
  88.1 1.5 %collective-permute-start.27 = (bf16[1280,128]{1,0:T(8,128)(2,1)S(1)}, bf16[1280,128]{1,0:T(8,128)(2,1)S(1)}, u32[]{:S(2)}, u32[]{:S(2)}) collective-permute-start(bf16[1280,128]{1,0:T(8,128)(2,1)S(1)} %get-tuple-element.161), channel_id=1, source_target_pairs={{0,6},{1,7},{2,4},{3,5},{4,2},{5,3},{6,0},{7,1},{8,14},{9,15},{10,... | collective-permute-start | bytes 983048 | tf_op jit(solution)/shard_map/ppermute | solution.py:656
  89.6 2.6 %copy-done.12 = f32[9,1240,128]{2,1,0:T(8,128)S(1)} copy-done((f32[9,1240,128]{2,1,0:T(8,128)S(1)}, f32[9,1240,128]{2,1,0:T(8,128)}, u32[]{:S(2)}) %copy-start.12) | copy-done | bytes 5713944
  92.2 11.1 %attend_back.1 = (f32[9,1240,128]{2,1,0:T(8,128)S(1)}, bf16[1024,384]{1,0:T(8,128)(2,1)S(1)}, f32[8,384]{1,0:T(8,128)S(1)}) custom-call(s32[12]{0:T(128)S(1)} %copy-done.10, f32[9,1240,128]{2,1,0:T(8,128)S(1)} %copy-done.12, f32[3,1240,128]{2,1,0:T(8,128)S(1)} %copy-done.14, f32[36,1,320]{2,1,0:T(1,128)S(1)} %get-tuple-element.145.log_total, ...), custom_call_target="tpu_custom_call" | custom-call | flops 13799999488 | bytes 1024 | tf_op jit(solution)/shard_map/attend_back/pallas_call | solution.py:175
  103.4 6.3 %project_back.1 = (bf16[984,384]{1,0:T(8,128)(2,1)}, bf16[624,128]{1,0:T(8,128)(2,1)S(1)}, bf16[2560,128]{1,0:T(8,128)(2,1)S(1)}, bf16[640,128]{1,0:T(8,128)(2,1...) custom-call(s32[1]{0:T(128)} %bitcast.me.mask, ...), custom_call_target="tpu_custom_call" | custom-call | flops 11500000256 | bytes 1024 | tf_op jit(solution)/shard_map/project_back/pallas_call | solution.py:175
  112.2 1.5 %collective-permute-start.35 = (bf16[320,128]{1,0:T(8,128)(2,1)S(1)}, bf16[320,128]{1,0:T(8,128)(2,1)S(1)}, u32[]{:S(2)}, u32[]{:S(2)}) collective-permute-start(bf16[320,128]{1,0:T(8,128)(2,1)S(1)} %add_convert_fusion.11), channel_id=1, source_target_pairs={{0,6},{1,7},{2,4},{3,5},{4,2},{5,3},{6,0},{7,1},{8,14},{9,15},{10,... | collective-permute-start | bytes 245768 | tf_op jit(solution)/shard_map/ppermute | solution.py:656
  113.7 2.0 %collective-permute-start.34 = (bf16[320,128]{1,0:T(8,128)(2,1)S(1)}, bf16[320,128]{1,0:T(8,128)(2,1)S(1)}, u32[]{:S(2)}, u32[]{:S(2)}) collective-permute-start(bf16[320,128]{1,0:T(8,128)(2,1)S(1)} %add_convert_fusion.11), channel_id=1, source_target_pairs={{0,4},{1,5},{2,6},{3,7},{4,0},{5,1},{6,2},{7,3},{8,12},{9,13},{10,... | collective-permute-start | bytes 245768 | tf_op jit(solution)/shard_map/ppermute | solution.py:656
  116.4 2.1 %collective-permute-start.40 = (bf16[320,128]{1,0:T(8,128)(2,1)S(1)}, bf16[320,128]{1,0:T(8,128)(2,1)S(1)}, u32[]{:S(2)}, u32[]{:S(2)}) collective-permute-start(bf16[320,128]{1,0:T(8,128)(2,1)S(1)} %get-tuple-element.189), channel_id=1, source_target_pairs={{0,16},{1,17},{2,18},{3,19},{4,20},{5,21},{6,22},{7,23},{8,24},{9,... | collective-permute-start | bytes 245768 | tf_op jit(solution)/shard_map/ppermute | solution.py:656
  118.5 2.0 %collective-permute-start.30 = (bf16[640,128]{1,0:T(8,128)(2,1)S(1)}, bf16[640,128]{1,0:T(8,128)(2,1)S(1)}, u32[]{:S(2)}, u32[]{:S(2)}) collective-permute-start(bf16[640,128]{1,0:T(8,128)(2,1)S(1)} %get-tuple-element.179), channel_id=1, source_target_pairs={{0,2},{1,3},{2,0},{3,1},{4,6},{5,7},{6,4},{7,5},{8,10},{9,11},{10,... | collective-permute-start | bytes 491528 | tf_op jit(solution)/shard_map/ppermute | solution.py:656
  121.6 1.5 %collective-permute-start.32 = (bf16[640,128]{1,0:T(8,128)(2,1)S(1)}, bf16[640,128]{1,0:T(8,128)(2,1)S(1)}, u32[]{:S(2)}, u32[]{:S(2)}) collective-permute-start(bf16[640,128]{1,0:T(8,128)(2,1)S(1)} %get-tuple-element.181), channel_id=1, source_target_pairs={{0,6},{1,7},{2,4},{3,5},{4,2},{5,3},{6,0},{7,1},{8,14},{9,15},{10,... | collective-permute-start | bytes 491528 | tf_op jit(solution)/shard_map/ppermute | solution.py:656
  124.0 2.1 %collective-permute-start.41 = (bf16[320,128]{1,0:T(8,128)(2,1)S(1)}, bf16[320,128]{1,0:T(8,128)(2,1)S(1)}, u32[]{:S(2)}, u32[]{:S(2)}) collective-permute-start(bf16[320,128]{1,0:T(8,128)(2,1)S(1)} %get-tuple-element.190), channel_id=1, source_target_pairs={{0,24},{1,25},{2,26},{3,27},{4,28},{5,29},{6,30},{7,31},{8,16},{9,... | collective-permute-start | bytes 245768 | tf_op jit(solution)/shard_map/ppermute | solution.py:656
  126.0 3.5 %collective-permute-done.31 = bf16[640,128]{1,0:T(8,128)(2,1)S(1)} collective-permute-done((bf16[640,128]{1,0:T(8,128)(2,1)S(1)}, bf16[640,128]{1,0:T(8,128)(2,1)S(1)}, u32[]{:S(2)}, u32[]{:S(2)}) %collective-permute-start.31) | collective-permute-done | bytes 163872 | tf_op jit(solution)/shard_map/ppermute | solution.py:656
  129.8 2.0 %collective-permute-start.44 = (bf16[320,128]{1,0:T(8,128)(2,1)S(1)}, bf16[320,128]{1,0:T(8,128)(2,1)S(1)}, u32[]{:S(2)}, u32[]{:S(2)}) collective-permute-start(bf16[320,128]{1,0:T(8,128)(2,1)S(1)} %add_convert_fusion.10.refs_8_), channel_id=1, source_target_pairs={{0,24},{1,25},{2,26},{3,27},{4,28},{5,29},{6,30},{7,31},{8,16},{9,... | collective-permute-start | bytes 245768 | tf_op jit(solution)/shard_map/ppermute | solution.py:656
  134.2 1.6 %collective-permute-start.37 = (bf16[160,128]{1,0:T(8,128)(2,1)S(1)}, bf16[160,128]{1,0:T(8,128)(2,1)S(1)}, u32[]{:S(2)}, u32[]{:S(2)}) collective-permute-start(bf16[160,128]{1,0:T(8,128)(2,1)S(1)} %get-tuple-element.185), channel_id=1, source_target_pairs={{0,16},{1,17},{2,18},{3,19},{4,20},{5,21},{6,22},{7,23},{8,24},{9,... | collective-permute-start | bytes 122888 | tf_op jit(solution)/shard_map/ppermute | solution.py:656
  135.9 1.7 %collective-permute-start.38 = (bf16[160,128]{1,0:T(8,128)(2,1)S(1)}, bf16[160,128]{1,0:T(8,128)(2,1)S(1)}, u32[]{:S(2)}, u32[]{:S(2)}) collective-permute-start(bf16[160,128]{1,0:T(8,128)(2,1)S(1)} %get-tuple-element.186), channel_id=1, source_target_pairs={{0,24},{1,25},{2,26},{3,27},{4,28},{5,29},{6,30},{7,31},{8,16},{9,... | collective-permute-start | bytes 122888 | tf_op jit(solution)/shard_map/ppermute | solution.py:656
  137.6 4.4 %collective-permute-done.37.refs_2_ = bf16[160,128]{1,0:T(8,128)(2,1)S(1)} collective-permute-done((bf16[160,128]{1,0:T(8,128)(2,1)S(1)}, bf16[160,128]{1,0:T(8,128)(2,1)S(1)}, u32[]{:S(2)}, u32[]{:S(2)}) %collective-permute-start.37) | collective-permute-done | bytes 40992 | tf_op jit(solution)/shard_map/ppermute | solution.py:656
  142.1 1.8 %settle.1 = (f32[18504]{0:T(1024)}, f32[18504]{0:T(1024)}, f32[18504]{0:T(1024)}, f32[18504]{0:T(1024)}, f32[38688]{0:T(1024)}, /*index=5*/f32[38688]{0:T(1024)}, f32[38688]{0:T(1024)}, f32[38688]{0:T(1024)}) custom-call(s32[5]{0:T(128)S(1)} %stack.36.place, bf16[160,128]{1,0:T(8,128)(2,1)S(1)} %get-tuple-element.183.refs_0_, ...), custom_call_target="tpu_custom_call" | custom-call | tf_op jit(solution)/shard_map/settle/pallas_call | solution.py:639
  (131 shorter events, 26.5 us)
Async XLA Ops:
  3.3 10.5 %collective-permute-start.2 = (bf16[160,128]{1,0:T(8,128)(2,1)S(1)}, bf16[160,128]{1,0:T(8,128)(2,1)S(1)}, u32[]{:S(2)}, u32[]{:S(2)}) collective-permute-start(bf16[160,128]{1,0:T(8,128)(2,1)S(1)} %get-tuple-element.106), channel_id=1, source_target_pairs={{0,24},{1,25},{2,26},{3,27},{4,28},{5,29},{6,30},{7,31},{8,16},{9,... | collective-permute-start | bytes 122888 | tf_op jit(solution)/shard_map/ppermute | solution.py:656
  8.4 8.9 %collective-permute-start.1 = (bf16[160,128]{1,0:T(8,128)(2,1)S(1)}, bf16[160,128]{1,0:T(8,128)(2,1)S(1)}, u32[]{:S(2)}, u32[]{:S(2)}) collective-permute-start(bf16[160,128]{1,0:T(8,128)(2,1)S(1)} %get-tuple-element.106), channel_id=1, source_target_pairs={{0,16},{1,17},{2,18},{3,19},{4,20},{5,21},{6,22},{7,23},{8,24},{9,... | collective-permute-start | bytes 122888 | tf_op jit(solution)/shard_map/ppermute | solution.py:656
  8.4 8.9 %collective-permute-start = (bf16[160,128]{1,0:T(8,128)(2,1)S(1)}, bf16[160,128]{1,0:T(8,128)(2,1)S(1)}, u32[]{:S(2)}, u32[]{:S(2)}) collective-permute-start(bf16[160,128]{1,0:T(8,128)(2,1)S(1)} %get-tuple-element.106), channel_id=1, source_target_pairs={{0,8},{1,9},{2,10},{3,11},{4,12},{5,13},{6,14},{7,15},{8,0},{9,1},... | collective-permute-start | bytes 122888 | tf_op jit(solution)/shard_map/ppermute | solution.py:656
  9.1 8.3 %collective-permute-start.8 = (bf16[320,128]{1,0:T(8,128)(2,1)S(1)}, bf16[320,128]{1,0:T(8,128)(2,1)S(1)}, u32[]{:S(2)}, u32[]{:S(2)}) collective-permute-start(bf16[320,128]{1,0:T(8,128)(2,1)S(1)} %get-tuple-element.116), channel_id=1, source_target_pairs={{0,24},{1,25},{2,26},{3,27},{4,28},{5,29},{6,30},{7,31},{8,16},{9,... | collective-permute-start | bytes 245768 | tf_op jit(solution)/shard_map/ppermute | solution.py:656
  12.8 7.0 %collective-permute-start.7 = (bf16[320,128]{1,0:T(8,128)(2,1)S(1)}, bf16[320,128]{1,0:T(8,128)(2,1)S(1)}, u32[]{:S(2)}, u32[]{:S(2)}) collective-permute-start(bf16[320,128]{1,0:T(8,128)(2,1)S(1)} %get-tuple-element.116), channel_id=1, source_target_pairs={{0,16},{1,17},{2,18},{3,19},{4,20},{5,21},{6,22},{7,23},{8,24},{9,... | collective-permute-start | bytes 245768 | tf_op jit(solution)/shard_map/ppermute | solution.py:656
  13.8 6.1 %collective-permute-start.6 = (bf16[320,128]{1,0:T(8,128)(2,1)S(1)}, bf16[320,128]{1,0:T(8,128)(2,1)S(1)}, u32[]{:S(2)}, u32[]{:S(2)}) collective-permute-start(bf16[320,128]{1,0:T(8,128)(2,1)S(1)} %get-tuple-element.116), channel_id=1, source_target_pairs={{0,8},{1,9},{2,10},{3,11},{4,12},{5,13},{6,14},{7,15},{8,0},{9,1},... | collective-permute-start | bytes 245768 | tf_op jit(solution)/shard_map/ppermute | solution.py:656
  19.9 6.5 %collective-permute-start.11 = (bf16[320,128]{1,0:T(8,128)(2,1)S(1)}, bf16[320,128]{1,0:T(8,128)(2,1)S(1)}, u32[]{:S(2)}, u32[]{:S(2)}) collective-permute-start(bf16[320,128]{1,0:T(8,128)(2,1)S(1)} %select_select_fusion.1), channel_id=1, source_target_pairs={{0,6},{1,7},{2,4},{3,5},{4,2},{5,3},{6,0},{7,1},{8,14},{9,15},{10,... | collective-permute-start | bytes 245768 | tf_op jit(solution)/shard_map/ppermute | solution.py:656
  22.4 7.0 %collective-permute-start.10 = (bf16[320,128]{1,0:T(8,128)(2,1)S(1)}, bf16[320,128]{1,0:T(8,128)(2,1)S(1)}, u32[]{:S(2)}, u32[]{:S(2)}) collective-permute-start(bf16[320,128]{1,0:T(8,128)(2,1)S(1)} %select_select_fusion.1), channel_id=1, source_target_pairs={{0,4},{1,5},{2,6},{3,7},{4,0},{5,1},{6,2},{7,3},{8,12},{9,13},{10,... | collective-permute-start | bytes 245768 | tf_op jit(solution)/shard_map/ppermute | solution.py:656
  22.9 6.5 %collective-permute-start.9 = (bf16[320,128]{1,0:T(8,128)(2,1)S(1)}, bf16[320,128]{1,0:T(8,128)(2,1)S(1)}, u32[]{:S(2)}, u32[]{:S(2)}) collective-permute-start(bf16[320,128]{1,0:T(8,128)(2,1)S(1)} %select_select_fusion.1), channel_id=1, source_target_pairs={{0,2},{1,3},{2,0},{3,1},{4,6},{5,7},{6,4},{7,5},{8,10},{9,11},{10,... | collective-permute-start | bytes 245768 | tf_op jit(solution)/shard_map/ppermute | solution.py:656
  23.5 9.0 %collective-permute-start.5 = (bf16[640,128]{1,0:T(8,128)(2,1)S(1)}, bf16[640,128]{1,0:T(8,128)(2,1)S(1)}, u32[]{:S(2)}, u32[]{:S(2)}) collective-permute-start(bf16[640,128]{1,0:T(8,128)(2,1)S(1)} %constant_dynamic-update-slice_fusion.refs_0_), channel_id=1, source_target_pairs={{0,6},{1,7},{2,4},{3,5},{4,2},{5,3},{6,0},{7,1},{8,14},{9,15},{10,... | collective-permute-start | bytes 491528 | tf_op jit(solution)/shard_map/ppermute | solution.py:656
  25.9 8.0 %collective-permute-start.4 = (bf16[640,128]{1,0:T(8,128)(2,1)S(1)}, bf16[640,128]{1,0:T(8,128)(2,1)S(1)}, u32[]{:S(2)}, u32[]{:S(2)}) collective-permute-start(bf16[640,128]{1,0:T(8,128)(2,1)S(1)} %constant_dynamic-update-slice_fusion.refs_0_), channel_id=1, source_target_pairs={{0,4},{1,5},{2,6},{3,7},{4,0},{5,1},{6,2},{7,3},{8,12},{9,13},{10,... | collective-permute-start | bytes 491528 | tf_op jit(solution)/shard_map/ppermute | solution.py:656
  26.4 7.5 %collective-permute-start.3 = (bf16[640,128]{1,0:T(8,128)(2,1)S(1)}, bf16[640,128]{1,0:T(8,128)(2,1)S(1)}, u32[]{:S(2)}, u32[]{:S(2)}) collective-permute-start(bf16[640,128]{1,0:T(8,128)(2,1)S(1)} %constant_dynamic-update-slice_fusion.refs_0_), channel_id=1, source_target_pairs={{0,2},{1,3},{2,0},{3,1},{4,6},{5,7},{6,4},{7,5},{8,10},{9,11},{10,... | collective-permute-start | bytes 491528 | tf_op jit(solution)/shard_map/ppermute | solution.py:656
  36.3 20.0 %collective-permute-start.19 = (bf16[1280,128]{1,0:T(8,128)(2,1)S(1)}, bf16[1280,128]{1,0:T(8,128)(2,1)S(1)}, u32[]{:S(2)}, u32[]{:S(2)}) collective-permute-start(bf16[1280,128]{1,0:T(8,128)(2,1)S(1)} %pad_maximum_fusion.refs_0_), channel_id=1, source_target_pairs={{0,6},{1,7},{2,4},{3,5},{4,2},{5,3},{6,0},{7,1},{8,14},{9,15},{10,... | collective-permute-start | bytes 983048 | tf_op jit(solution)/shard_map/ppermute | solution.py:656
  37.7 18.6 %collective-permute-start.18 = (bf16[1280,128]{1,0:T(8,128)(2,1)S(1)}, bf16[1280,128]{1,0:T(8,128)(2,1)S(1)}, u32[]{:S(2)}, u32[]{:S(2)}) collective-permute-start(bf16[1280,128]{1,0:T(8,128)(2,1)S(1)} %pad_maximum_fusion.refs_0_), channel_id=1, source_target_pairs={{0,4},{1,5},{2,6},{3,7},{4,0},{5,1},{6,2},{7,3},{8,12},{9,13},{10,... | collective-permute-start | bytes 983048 | tf_op jit(solution)/shard_map/ppermute | solution.py:656
  38.7 17.6 %collective-permute-start.17 = (bf16[1280,128]{1,0:T(8,128)(2,1)S(1)}, bf16[1280,128]{1,0:T(8,128)(2,1)S(1)}, u32[]{:S(2)}, u32[]{:S(2)}) collective-permute-start(bf16[1280,128]{1,0:T(8,128)(2,1)S(1)} %pad_maximum_fusion.refs_0_), channel_id=1, source_target_pairs={{0,2},{1,3},{2,0},{3,1},{4,6},{5,7},{6,4},{7,5},{8,10},{9,11},{10,... | collective-permute-start | bytes 983048 | tf_op jit(solution)/shard_map/ppermute | solution.py:656
  84.5 25.2 %collective-permute-start.25 = (bf16[1280,128]{1,0:T(8,128)(2,1)S(1)}, bf16[1280,128]{1,0:T(8,128)(2,1)S(1)}, u32[]{:S(2)}, u32[]{:S(2)}) collective-permute-start(bf16[1280,128]{1,0:T(8,128)(2,1)S(1)} %get-tuple-element.159), channel_id=1, source_target_pairs={{0,2},{1,3},{2,0},{3,1},{4,6},{5,7},{6,4},{7,5},{8,10},{9,11},{10,... | collective-permute-start | bytes 983048 | tf_op jit(solution)/shard_map/ppermute | solution.py:656
  88.1 21.6 %collective-permute-start.26 = (bf16[1280,128]{1,0:T(8,128)(2,1)S(1)}, bf16[1280,128]{1,0:T(8,128)(2,1)S(1)}, u32[]{:S(2)}, u32[]{:S(2)}) collective-permute-start(bf16[1280,128]{1,0:T(8,128)(2,1)S(1)} %get-tuple-element.160), channel_id=1, source_target_pairs={{0,4},{1,5},{2,6},{3,7},{4,0},{5,1},{6,2},{7,3},{8,12},{9,13},{10,... | collective-permute-start | bytes 983048 | tf_op jit(solution)/shard_map/ppermute | solution.py:656
  88.1 21.6 %collective-permute-start.27 = (bf16[1280,128]{1,0:T(8,128)(2,1)S(1)}, bf16[1280,128]{1,0:T(8,128)(2,1)S(1)}, u32[]{:S(2)}, u32[]{:S(2)}) collective-permute-start(bf16[1280,128]{1,0:T(8,128)(2,1)S(1)} %get-tuple-element.161), channel_id=1, source_target_pairs={{0,6},{1,7},{2,4},{3,5},{4,2},{5,3},{6,0},{7,1},{8,14},{9,15},{10,... | collective-permute-start | bytes 983048 | tf_op jit(solution)/shard_map/ppermute | solution.py:656
  112.2 6.3 %collective-permute-start.35 = (bf16[320,128]{1,0:T(8,128)(2,1)S(1)}, bf16[320,128]{1,0:T(8,128)(2,1)S(1)}, u32[]{:S(2)}, u32[]{:S(2)}) collective-permute-start(bf16[320,128]{1,0:T(8,128)(2,1)S(1)} %add_convert_fusion.11), channel_id=1, source_target_pairs={{0,6},{1,7},{2,4},{3,5},{4,2},{5,3},{6,0},{7,1},{8,14},{9,15},{10,... | collective-permute-start | bytes 245768 | tf_op jit(solution)/shard_map/ppermute | solution.py:656
  113.7 6.8 %collective-permute-start.34 = (bf16[320,128]{1,0:T(8,128)(2,1)S(1)}, bf16[320,128]{1,0:T(8,128)(2,1)S(1)}, u32[]{:S(2)}, u32[]{:S(2)}) collective-permute-start(bf16[320,128]{1,0:T(8,128)(2,1)S(1)} %add_convert_fusion.11), channel_id=1, source_target_pairs={{0,4},{1,5},{2,6},{3,7},{4,0},{5,1},{6,2},{7,3},{8,12},{9,13},{10,... | collective-permute-start | bytes 245768 | tf_op jit(solution)/shard_map/ppermute | solution.py:656
  115.7 5.9 %collective-permute-start.33 = (bf16[320,128]{1,0:T(8,128)(2,1)S(1)}, bf16[320,128]{1,0:T(8,128)(2,1)S(1)}, u32[]{:S(2)}, u32[]{:S(2)}) collective-permute-start(bf16[320,128]{1,0:T(8,128)(2,1)S(1)} %add_convert_fusion.11), channel_id=1, source_target_pairs={{0,2},{1,3},{2,0},{3,1},{4,6},{5,7},{6,4},{7,5},{8,10},{9,11},{10,... | collective-permute-start | bytes 245768 | tf_op jit(solution)/shard_map/ppermute | solution.py:656
  115.8 16.1 %collective-permute-start.39 = (bf16[320,128]{1,0:T(8,128)(2,1)S(1)}, bf16[320,128]{1,0:T(8,128)(2,1)S(1)}, u32[]{:S(2)}, u32[]{:S(2)}) collective-permute-start(bf16[320,128]{1,0:T(8,128)(2,1)S(1)} %get-tuple-element.188), channel_id=1, source_target_pairs={{0,8},{1,9},{2,10},{3,11},{4,12},{5,13},{6,14},{7,15},{8,0},{9,1},... | collective-permute-start | bytes 245768 | tf_op jit(solution)/shard_map/ppermute | solution.py:656
  116.4 16.8 %collective-permute-start.40 = (bf16[320,128]{1,0:T(8,128)(2,1)S(1)}, bf16[320,128]{1,0:T(8,128)(2,1)S(1)}, u32[]{:S(2)}, u32[]{:S(2)}) collective-permute-start(bf16[320,128]{1,0:T(8,128)(2,1)S(1)} %get-tuple-element.189), channel_id=1, source_target_pairs={{0,16},{1,17},{2,18},{3,19},{4,20},{5,21},{6,22},{7,23},{8,24},{9,... | collective-permute-start | bytes 245768 | tf_op jit(solution)/shard_map/ppermute | solution.py:656
  120.5 9.0 %collective-permute-start.31 = (bf16[640,128]{1,0:T(8,128)(2,1)S(1)}, bf16[640,128]{1,0:T(8,128)(2,1)S(1)}, u32[]{:S(2)}, u32[]{:S(2)}) collective-permute-start(bf16[640,128]{1,0:T(8,128)(2,1)S(1)} %get-tuple-element.180), channel_id=1, source_target_pairs={{0,4},{1,5},{2,6},{3,7},{4,0},{5,1},{6,2},{7,3},{8,12},{9,13},{10,... | collective-permute-start | bytes 491528 | tf_op jit(solution)/shard_map/ppermute | solution.py:656
  121.6 7.9 %collective-permute-start.32 = (bf16[640,128]{1,0:T(8,128)(2,1)S(1)}, bf16[640,128]{1,0:T(8,128)(2,1)S(1)}, u32[]{:S(2)}, u32[]{:S(2)}) collective-permute-start(bf16[640,128]{1,0:T(8,128)(2,1)S(1)} %get-tuple-element.181), channel_id=1, source_target_pairs={{0,6},{1,7},{2,4},{3,5},{4,2},{5,3},{6,0},{7,1},{8,14},{9,15},{10,... | collective-permute-start | bytes 491528 | tf_op jit(solution)/shard_map/ppermute | solution.py:656
  124.0 10.3 %collective-permute-start.41 = (bf16[320,128]{1,0:T(8,128)(2,1)S(1)}, bf16[320,128]{1,0:T(8,128)(2,1)S(1)}, u32[]{:S(2)}, u32[]{:S(2)}) collective-permute-start(bf16[320,128]{1,0:T(8,128)(2,1)S(1)} %get-tuple-element.190), channel_id=1, source_target_pairs={{0,24},{1,25},{2,26},{3,27},{4,28},{5,29},{6,30},{7,31},{8,16},{9,... | collective-permute-start | bytes 245768 | tf_op jit(solution)/shard_map/ppermute | solution.py:656
  129.6 6.3 %collective-permute-start.36 = (bf16[160,128]{1,0:T(8,128)(2,1)S(1)}, bf16[160,128]{1,0:T(8,128)(2,1)S(1)}, u32[]{:S(2)}, u32[]{:S(2)}) collective-permute-start(bf16[160,128]{1,0:T(8,128)(2,1)S(1)} %get-tuple-element.184), channel_id=1, source_target_pairs={{0,8},{1,9},{2,10},{3,11},{4,12},{5,13},{6,14},{7,15},{8,0},{9,1},... | collective-permute-start | bytes 122888 | tf_op jit(solution)/shard_map/ppermute | solution.py:656
  129.8 12.2 %collective-permute-start.44 = (bf16[320,128]{1,0:T(8,128)(2,1)S(1)}, bf16[320,128]{1,0:T(8,128)(2,1)S(1)}, u32[]{:S(2)}, u32[]{:S(2)}) collective-permute-start(bf16[320,128]{1,0:T(8,128)(2,1)S(1)} %add_convert_fusion.10.refs_8_), channel_id=1, source_target_pairs={{0,24},{1,25},{2,26},{3,27},{4,28},{5,29},{6,30},{7,31},{8,16},{9,... | collective-permute-start | bytes 245768 | tf_op jit(solution)/shard_map/ppermute | solution.py:656
  131.9 10.1 %collective-permute-start.43 = (bf16[320,128]{1,0:T(8,128)(2,1)S(1)}, bf16[320,128]{1,0:T(8,128)(2,1)S(1)}, u32[]{:S(2)}, u32[]{:S(2)}) collective-permute-start(bf16[320,128]{1,0:T(8,128)(2,1)S(1)} %add_convert_fusion.10.refs_8_), channel_id=1, source_target_pairs={{0,16},{1,17},{2,18},{3,19},{4,20},{5,21},{6,22},{7,23},{8,24},{9,... | collective-permute-start | bytes 245768 | tf_op jit(solution)/shard_map/ppermute | solution.py:656
  133.2 8.8 %collective-permute-start.42 = (bf16[320,128]{1,0:T(8,128)(2,1)S(1)}, bf16[320,128]{1,0:T(8,128)(2,1)S(1)}, u32[]{:S(2)}, u32[]{:S(2)}) collective-permute-start(bf16[320,128]{1,0:T(8,128)(2,1)S(1)} %add_convert_fusion.10.refs_8_), channel_id=1, source_target_pairs={{0,8},{1,9},{2,10},{3,11},{4,12},{5,13},{6,14},{7,15},{8,0},{9,1},... | collective-permute-start | bytes 245768 | tf_op jit(solution)/shard_map/ppermute | solution.py:656
  134.2 7.7 %collective-permute-start.37 = (bf16[160,128]{1,0:T(8,128)(2,1)S(1)}, bf16[160,128]{1,0:T(8,128)(2,1)S(1)}, u32[]{:S(2)}, u32[]{:S(2)}) collective-permute-start(bf16[160,128]{1,0:T(8,128)(2,1)S(1)} %get-tuple-element.185), channel_id=1, source_target_pairs={{0,16},{1,17},{2,18},{3,19},{4,20},{5,21},{6,22},{7,23},{8,24},{9,... | collective-permute-start | bytes 122888 | tf_op jit(solution)/shard_map/ppermute | solution.py:656
  135.9 6.1 %collective-permute-start.38 = (bf16[160,128]{1,0:T(8,128)(2,1)S(1)}, bf16[160,128]{1,0:T(8,128)(2,1)S(1)}, u32[]{:S(2)}, u32[]{:S(2)}) collective-permute-start(bf16[160,128]{1,0:T(8,128)(2,1)S(1)} %get-tuple-element.186), channel_id=1, source_target_pairs={{0,24},{1,25},{2,26},{3,27},{4,28},{5,29},{6,30},{7,31},{8,16},{9,... | collective-permute-start | bytes 122888 | tf_op jit(solution)/shard_map/ppermute | solution.py:656
  (36 other events, 364.4 us)
where the time goes:
time: 144 us
  Pallas kernels  53.7 us (37%)
  starting transfers between devices  50.6 us (35%)
  waiting for transfers between devices  28 us (19%)
  local copies, waits for them, and re-layouts  7.84 us (5%)
  other arithmetic  2.64 us (2%)
    pallas_call x5, Pallas kernels, call(): pl.pallas_call(kernel, in_specs=[SMEM_SPEC if a.dtype == jnp.int32 and a....  51.2 us
    ppermute x45, starting transfers between devices, swap(): return lax.ppermute(value, AXES, [(j, j ^ bits) for j in range(DEVICES)])  50.6 us
    ppermute x45, waiting for transfers between devices, swap(): return lax.ppermute(value, AXES, [(j, j ^ bits) for j in range(DEVICES)])  28 us
    unnamed x49, local copies, waits for them, and re-layouts  7.01 us
  transfers between devices with their start and end apart: 45, of which 20 were waited for; matrix products, arithmetic and copies ran while one was open for 1% of the time, Pallas kernels for 23%

commit v1 on v0

--- a/solution.py
+++ b/solution.py
@@ -36,7 +36,7 @@
 TN = (((0,), (0,)), ((), ()))
 NN = (((1,), (0,)), ((), ()))
 BLOCK = 128
-PART = 256
+PART = 512
 
 ROW_GAIN_ONE = 0
 ROW_BIAS_ONE = ROW_GAIN_ONE + D_COLS
@@ -86,6 +86,7 @@
 
 SMEM_SPEC = pl.BlockSpec(memory_space=pltpu.SMEM)
 VMEM_SPEC = pl.BlockSpec(memory_space=pltpu.VMEM)
+HBM_SPEC = pl.BlockSpec(memory_space=pltpu.HBM)
 
 
 def tall(vector, rows):
@@ -110,15 +111,22 @@
         vector[pl.ds(full, entries - full)] = value[full // LANES : full // LANES + 8].reshape(TILE)[: entries - full]
 
 
-def align_kernel(place, attn, mlp, attn_out, mlp_out):
-    for n, (source, target) in enumerate(((attn, attn_out), (mlp, mlp_out))):
+def align_kernel(heights, place, attn, mlp, out, attn_here, mlp_here, arrived):
+    sources = ((attn, attn_here), (mlp, mlp_here))
+    copies = [pltpu.make_async_copy(*source, arrived.at[n]) for n, source in enumerate(sources)]
+    for copy in copies:
+        copy.start()
+    first = 0
+    for n, height in enumerate(heights):
+        copies[n].wait()
         lanes, rows = place[2 * n], place[2 * n + 1]
-        value = tall(source, target.shape[0])
+        value = tall(sources[n][1], height)
         turned = pltpu.roll(value, lanes, 1)
         below = pltpu.roll(turned, 1, 0)
         lane = lax.broadcasted_iota(jnp.int32, value.shape, 1)
         moved = jnp.where(lane >= lanes, turned, below)
-        target[...] = pltpu.roll(moved, rows, 0).astype(BF16)
+        out[first : first + height, :] = pltpu.roll(moved, rows, 0).astype(BF16)
+        first += height
 
 
 def take_share(value, lanes, rows):
@@ -131,11 +139,21 @@
 
 
 def unpack(flat, arrays, entries, rows, me):
-    flat[...] = jnp.zeros_like(flat)
-    for ref, numbers in arrays:
-        for t, number in enumerate(numbers):
-            start = tile_row(entries, number ^ me)
-            flat[pl.ds(start, rows), :] += ref[t * rows : (t + 1) * rows, :].astype(F32)
+    alone = entries // TILE * 8
+    edges = [(0, 8), (alone, rows)] if alone > 8 else [(0, rows)]
+    for add in (False, True):
+        for ref, numbers in arrays:
+            for t, number in enumerate(numbers):
+                start = tile_row(entries, number ^ me)
+                for low, high in edges:
+                    at = pl.ds(pl.multiple_of(start + low, 8), high - low)
+                    if add:
+                        flat[at, :] += ref[t * rows + low : t * rows + high, :].astype(F32)
+                    else:
+                        flat[at, :] = jnp.zeros((high - low, LANES), F32)
+                if add and alone > 8:
+                    at = pl.ds(pl.multiple_of(start + 8, 8), alone - 8)
+                    flat[at, :] = ref[t * rows + 8 : t * rows + alone, :].astype(F32)
 
 
 def read_matrix(flat, row, depth, cols, target):
@@ -184,18 +202,22 @@
     )(*operands)
 
 
-def project_kernel(entries, attn_plan, pos_count, attn_rows, mlp_rows, me, pos_names, onehot, tokens, *refs):
+def project_kernel(entries, attn_plan, pos_plan, attn_rows, mlp_rows, me, pos_names, onehot, tokens, *refs):
     attn_arrays = [(refs[i], plan) for i, plan in enumerate(attn_plan)]
     refs = refs[len(attn_plan) :]
-    pos_arrays, refs = refs[:pos_count], refs[pos_count:]
     embedded, normed_out, qkv, w_qkv, w_out, vectors = refs[:6]
     flat, pos_flat, pos_table = refs[6:]
     slots, rows = tokens.shape[0], embedded.shape[0]
 
     pos_flat[...] = jnp.zeros_like(pos_flat)
-    for n, ref in enumerate(pos_arrays):
-        start = tile_row(entries[1], pos_names[n])
-        pos_flat[pl.ds(start, mlp_rows), :] += ref[...].astype(F32)
+    for n, (array, first) in enumerate(pos_plan):
+        name = pos_names[n]
+
+        @pl.when(name >= 0)
+        def _():
+            at = pl.ds(tile_row(entries[1], name), mlp_rows)
+            pos_flat[at, :] += attn_arrays[array][0][first : first + mlp_rows, :].astype(F32)
+
     pos_table[...] = jnp.zeros_like(pos_table)
     most = POS // 16 * 16
     for c in range(D_COLS):
@@ -239,10 +261,10 @@
     lax.fori_loop(0, rows // PART, project, 0)
 
 
-def project(entries, attn_arrays, pos_arrays, pos_names, me, onehot, tokens, sizes):
+def project(entries, attn_arrays, pos_plan, pos_names, me, onehot, tokens, sizes):
     rows = onehot.shape[0]
     plan = [numbers for _, numbers in attn_arrays]
-    operands = [me, pos_names, onehot, tokens] + [a for a, _ in attn_arrays] + list(pos_arrays)
+    operands = [me, pos_names, onehot, tokens] + [a for a, _ in attn_arrays]
     outs = [
         ((rows, D), F32),
         ((rows, D), BF16),
@@ -257,9 +279,9 @@
         pltpu.VMEM((256, D), BF16),
     ]
     kernel = functools.partial(
-        project_kernel, entries, plan, len(pos_arrays), sizes.attn_rows, sizes.mlp_rows
+        project_kernel, entries, plan, pos_plan, sizes.attn_rows, sizes.mlp_rows
     )
-    return call(kernel, "project", operands, outs, scratch, 24, 8)
+    return call(kernel, "project", operands, outs, scratch, 17, 8)
 
 
 def image_table(lengths, table):
@@ -282,6 +304,45 @@
     return -(-((LONG if slot < MOST_LONG else SHORT) + 7) // 32) * 32
 
 
+class Unit:
+    def __init__(self, slots, table):
+        self.slots = slots
+        self.height = image_rows(slots[0])
+        self.lows = [table[0, slot] % 8 for slot in slots]
+        self.at = [pl.ds(pl.multiple_of(table[0, s] - low, 8), self.height) for s, low in zip(slots, self.lows)]
+        self.lengths = [table[1, slot] for slot in slots]
+        self.valid = jnp.concatenate([inside(self.height, *span) for span in zip(self.lows, self.lengths)], axis=0)
+
+    def load(self, ref, *index):
+        return jnp.concatenate([ref[(*index, at, slice(None))] for at in self.at], axis=0)
+
+    def store(self, ref, index, value):
+        for n, at in enumerate(self.at):
+            here = slice(n * self.height, (n + 1) * self.height)
+            pltpu.store(ref.at[index, at, :], value[here], mask=self.valid[here])
+
+    def mask(self):
+        count, height = len(self.slots), self.height
+        shape = (count * height, count * height)
+        key = lax.broadcasted_iota(jnp.int32, shape, 1)
+        row = lax.broadcasted_iota(jnp.int32, shape, 0)
+        seen = None
+        for n in range(count):
+            low = n * height + self.lows[n]
+            part = (key >= low) & (key < low + self.lengths[n])
+            if count > 1:
+                part = part & (row >= n * height) & (row < (n + 1) * height)
+            seen = part if seen is None else seen | part
+        bias = jnp.where(seen, 0.0, -1e30)
+        return jnp.concatenate([bias, bias], axis=0)
+
+
+def units(images, table):
+    shorts = list(range(MOST_LONG, images))
+    slots = [[slot] for slot in range(MOST_LONG)] + [shorts[i : i + 2] for i in range(0, len(shorts), 2)]
+    return [Unit(these, table) for these in slots]
+
+
 def both_heads(value):
     left = lax.broadcasted_iota(jnp.int32, value.shape, 1) < DH
     zero = jnp.zeros_like(value)
@@ -299,59 +360,72 @@
     return (row >= low) & (row < low + length)
 
 
-def attend(queries, keys, values, mask):
-    scores = dot(keys, both_heads(queries), NT)
-    scores = jnp.where(mask, scores, -1e30)
-    peak = jnp.max(scores, axis=0, keepdims=True)
-    probs = jnp.exp(scores - peak)
-    total = jnp.sum(probs, axis=0, keepdims=True)
-    out = dot(values.T.astype(BF16), probs.astype(BF16)) * (1.0 / total)
-    return one_of_heads(out.T), peak + jnp.log(total)
-
-
-def key_mask(height, width, low, length):
-    row = lax.broadcasted_iota(jnp.int32, (height, width), 0)
-    return (row >= low) & (row < low + length)
+def attend(queries, keys, values, bias):
+    scores = dot(both_heads(queries), keys, NT) + bias
+    peak = jnp.max(scores, axis=1, keepdims=True)
+    probs = jnp.exp(scores - peak).astype(BF16)
+    out = dot(probs, jnp.concatenate([values, jnp.ones_like(values)], axis=1))
+    total = out[:, LANES:]
+    return one_of_heads(out[:, :LANES] / total), peak + jnp.log(total)
 
 
 def attend_kernel(slots, lengths, qkv, embedded, w_out, vectors, mixed, log_total, residual, table):
     images = lengths.shape[0]
     rows = residual.shape[0]
     live = image_table(lengths, table)
-    mixed[...] = jnp.zeros_like(mixed)
-    for slot in range(images):
-        height = image_rows(slot)
-        low = table[0, slot] % 8
-        at = pl.ds(pl.multiple_of(table[0, slot] - low, 8), height)
-        length = table[1, slot]
-        mask = key_mask(height, 2 * height, low, length)
-        valid = inside(height, low, length)
-        for pair in range(PAIRS):
-            out, total = attend(
-                qkv[pair, at, :].astype(BF16),
-                qkv[PAIRS + pair, at, :].astype(BF16),
-                qkv[2 * PAIRS + pair, at, :],
-                mask,
-            )
-            log_total[slot * PAIRS + pair, :, 0 : 2 * height] = total
-            pltpu.store(mixed.at[pair, at, :], out.astype(BF16).astype(F32), mask=valid)
+    ahead = slots // 8 * 8
+    for pair in range(PAIRS):
+        mixed[pair, ahead:, :] = jnp.zeros((mixed.shape[1] - ahead, LANES), F32)
+    items = [(n, unit, pair) for n, unit in enumerate(units(images, table)) for pair in range(PAIRS)]
+    biases, log_totals = {}, {}
+
+    def first(n, unit, pair):
+        if n not in biases:
+            biases[n] = unit.mask()
+            log_totals[n] = jnp.zeros((biases[n].shape[0], LANES), F32)
+        queries, keys, values = (unit.load(qkv, k * PAIRS + pair).astype(BF16) for k in range(3))
+        return values, dot(both_heads(queries), keys, NT)
+
+    def second(n, unit, pair, values, scores):
+        scores = scores + biases[n]
+        peak = jnp.max(scores, axis=1, keepdims=True)
+        return values, peak, jnp.exp(scores - peak).astype(BF16)
+
+    def third(n, unit, pair, values, peak, probs):
+        out = dot(probs, jnp.concatenate([values, jnp.ones_like(values)], axis=1))
+        total = out[:, LANES:]
+        lane = lax.broadcasted_iota(jnp.int32, total.shape, 1)
+        log_totals[n] = jnp.where(lane == pair, peak + jnp.log(total), log_totals[n])
+        unit.store(mixed, pair, one_of_heads(out[:, :LANES] / total).astype(BF16).astype(F32))
+        if pair == PAIRS - 1:
+            log_total[n, 0 : total.shape[0], :] = log_totals.pop(n)
+
+    ones, twos = {}, {}
+    for t in range(len(items) + 2):
+        if t < len(items):
+            ones[t] = first(*items[t])
+        if 0 <= t - 1 < len(items):
+            twos[t - 1] = second(*items[t - 1], *ones.pop(t - 1))
+        if 0 <= t - 2 < len(items):
+            third(*items[t - 2], *twos.pop(t - 2))
 
     low = live % 8
     base = pl.multiple_of(live - low, 8)
     length = slots - live
-    most = -(-(slots - images * SHORT + 7) // BLOCK) if (images * SHORT) % 8 else -(-(slots - images * SHORT) // BLOCK)
+    most = -(-(slots - images * SHORT + (7 if (images * SHORT) % 8 else 0)) // BLOCK)
     for blocks in range(1, most + 1):
 
         @pl.when((low + length > (blocks - 1) * BLOCK) & (low + length <= blocks * BLOCK))
         def _():
             height = blocks * BLOCK
-            mask = key_mask(height, 2 * BLOCK, low, length)
+            key = lax.broadcasted_iota(jnp.int32, (2 * BLOCK, height), 1)
+            bias = jnp.where((key >= low) & (key < low + length), 0.0, -1e30)
             for pair in range(PAIRS):
                 keys = qkv[PAIRS + pair, pl.ds(base, height), :].astype(BF16)
-                values = qkv[2 * PAIRS + pair, pl.ds(base, height), :]
+                values = qkv[2 * PAIRS + pair, pl.ds(base, height), :].astype(BF16)
                 for block in range(blocks):
                     at = pl.ds(pl.multiple_of(base + block * BLOCK, 8), BLOCK)
-                    out, _ = attend(qkv[pair, at, :].astype(BF16), keys, values, mask)
+                    out, _ = attend(qkv[pair, at, :].astype(BF16), keys, values, bias)
                     valid = inside(BLOCK, low - block * BLOCK, length)
                     pltpu.store(mixed.at[pair, at, :], out.astype(BF16).astype(F32), mask=valid)
 
@@ -367,24 +441,22 @@
 def attend_all(slots, lengths, qkv, embedded, w_out, vectors):
     rows = embedded.shape[0]
     images = lengths.shape[0]
-    outs = [((PAIRS,) + qkv.shape[1:], F32), ((images * PAIRS, 1, 2 * image_rows(0)), F32), ((rows, D), F32)]
+    units_count = MOST_LONG + -(-(images - MOST_LONG) // 2)
+    height = 2 * max(image_rows(0), 2 * image_rows(MOST_LONG))
+    outs = [((PAIRS,) + qkv.shape[1:], F32), ((units_count, height, LANES), F32), ((rows, D), F32)]
     scratch = [pltpu.SMEM((2, images), jnp.int32)]
     operands = [lengths, qkv, embedded, w_out, vectors]
-    return call(functools.partial(attend_kernel, slots), "attend", operands, outs, scratch, 24, 10)
+    return call(functools.partial(attend_kernel, slots), "attend", operands, outs, scratch, 15, 10)
 
 
 def gelu_parts(value):
-    size = jnp.abs(value)
-    near = 1.0 / (1.0 + (0.3275911 * math.sqrt(0.5)) * size)
-    bell = jnp.exp(-0.5 * value * value)
-    series = near * (
-        0.5 * 0.254829592
-        + near
-        * (0.5 * -0.284496736 + near * (0.5 * 1.421413741 + near * (0.5 * -1.453152027 + near * (0.5 * 1.061405429))))
-    )
-    tail = series * bell
-    share = jnp.where(value >= 0, 1.0 - tail, tail)
-    return value * share, share + value * bell * (1.0 / math.sqrt(2.0 * math.pi))
+    share = 0.5 + 0.5 * lax.erf(value * math.sqrt(0.5))
+    bell = jnp.exp2((value * value) * (-0.5 * math.log2(math.e)))
+    return value * share, share + value * (bell * (1.0 / math.sqrt(2.0 * math.pi)))
+
+
+def with_ones(value_t):
+    return jnp.concatenate([value_t, jnp.ones((16, value_t.shape[1]), BF16)], axis=0)
 
 
 def pack(flat, entries, rows, me, targets):
@@ -400,7 +472,7 @@
     output, d_residual = refs[:2]
     targets = [(refs[2 + i], plan) for i, plan in enumerate(out_plan)]
     refs = refs[2 + len(out_plan) :]
-    flat, w_in, w_back, normed_b, active_b, d_hidden_b, out_f32, sums_in, sums, out_grad = refs
+    flat, w_in, w_back, normed_b, active_b, d_hidden_b, out_f32, sums, out_grad = refs
     slots, rows = cotangent.shape[0], residual.shape[0]
     live = sum(lengths[i] for i in range(lengths.shape[0]))
     row = lax.broadcasted_iota(jnp.int32, (slots, D), 0)
@@ -415,7 +487,6 @@
     b_in = read_row(flat, ROW_B_IN, FF_COLS)
     b_back = read_row(flat, ROW_B_BACK, D_COLS)
     sums[...] = jnp.zeros_like(sums)
-    sums_in[...] = jnp.zeros_like(sums_in)
 
     def step(i, _):
         at = pl.ds(pl.multiple_of(i * PART, PART), PART)
@@ -432,29 +503,29 @@
             d_hidden = (d_active * slope).astype(BF16)
             active_b[at, cols] = active.astype(BF16)
             d_hidden_b[at, cols] = d_hidden
-            sums_in[:, cols] += fold_rows(d_hidden.astype(F32))
         out_f32[at, :] = value + b_back + dot(active_b[at, :], w_back[...])
         d_normed = dot(d_hidden_b[at, :], w_in[...], NT)
         grad = grad_b.astype(F32)
         d_residual[at, :] = grad + norm_back(normed, inverse, gain, d_normed)
         sums[0] += fold_rows(d_normed * normed)
         sums[1] += fold_rows(d_normed)
-        sums[2] += fold_rows(grad)
         return 0
 
     lax.fori_loop(0, rows // PART, step, 0)
     output[...] = out_f32[0 : output.shape[0], :].astype(BF16)
 
-    flat[...] = jnp.zeros_like(flat)
+    flat[0:ROW_GAIN_TWO, :] = jnp.zeros((ROW_GAIN_TWO, LANES), F32)
+    flat[MLP_ROWS:, :] = jnp.zeros((flat.shape[0] - MLP_ROWS, LANES), F32)
     write_row(flat, ROW_GAIN_TWO, jnp.sum(sums[0], axis=0, keepdims=True))
     write_row(flat, ROW_BIAS_TWO, jnp.sum(sums[1], axis=0, keepdims=True))
-    write_row(flat, ROW_B_IN, jnp.sum(sums_in[...], axis=0, keepdims=True))
-    write_row(flat, ROW_B_BACK, jnp.sum(sums[2], axis=0, keepdims=True))
-    normed_t = normed_b[...].T
+    normed_t = with_ones(normed_b[...].T)
+    column_sums = dot(jnp.ones((16, rows), BF16), out_grad[...])
+    write_row(flat, ROW_B_BACK, column_sums[0:1])
     for c in range(0, FF_COLS, 2):
         part = dot(normed_t, d_hidden_b[:, c * LANES : (c + 2) * LANES])
         for k in range(2):
-            flat[pl.ds(ROW_W_IN + c + k, D, stride=FF_COLS), :] = part[:, k * LANES : (k + 1) * LANES]
+            flat[pl.ds(ROW_W_IN + c + k, D, stride=FF_COLS), :] = part[0:D, k * LANES : (k + 1) * LANES]
+        write_row(flat, ROW_B_IN + c, part[D : D + 1])
     for r in range(0, FF, 256):
         part = dot(active_b[:, r : r + 256], out_grad[...], TN)
         for c in range(D_COLS):
@@ -476,26 +547,25 @@
         pltpu.VMEM((rows, FF), BF16),
         pltpu.VMEM((rows, FF), BF16),
         pltpu.VMEM((rows, D), F32),
-        pltpu.VMEM((8, FF), F32),
-        pltpu.VMEM((3, 8, D), F32),
+        pltpu.VMEM((2, 8, D), F32),
         pltpu.VMEM((rows, D), BF16),
     ]
     kernel = functools.partial(mlp_kernel, entries, plan, out_plan, sizes.mlp_rows)
-    return call(kernel, "feed_forward", operands, outs, scratch, 36, 18)
-
-
-def attend_back_kernel(lengths, qkv, mixed, log_total, w_out, d_residual, d_qkv, d_branch_b, b_out_sum, d_mixed, table):
+    return call(kernel, "feed_forward", operands, outs, scratch, 28, 18)
+
+
+def attend_back_kernel(lengths, qkv, mixed, log_total, w_out, d_residual, d_qkv, d_branch_b, d_mixed, table):
     images = lengths.shape[0]
     rows = d_residual.shape[0]
     image_table(lengths, table)
-    d_qkv[...] = jnp.zeros_like(d_qkv)
-    b_out_sum[...] = jnp.zeros_like(b_out_sum)
+    ahead = images * SHORT // 8 * 8
+    for c in range(QKV_COLS):
+        d_qkv[c, ahead:, :] = jnp.zeros((d_qkv.shape[1] - ahead, LANES), F32)
 
     def enter(i, _):
         at = pl.ds(pl.multiple_of(i * PART, PART), PART)
         branch = d_residual[at, :].astype(BF16)
         d_branch_b[at, :] = branch
-        b_out_sum[...] += fold_rows(branch.astype(F32))
         value = dot(branch, w_out[...], NT).astype(BF16).astype(F32)
         for c in range(D_COLS):
             d_mixed[c, at, :] = value[:, c * LANES : (c + 1) * LANES]
@@ -505,49 +575,54 @@
     for c in range(D_COLS):
         d_mixed[c, rows : d_mixed.shape[1], :] = jnp.zeros((d_mixed.shape[1] - rows, LANES), F32)
 
-    ones = jnp.ones((8, LANES), BF16)
-    for slot in range(images):
-        height = image_rows(slot)
-        low = table[0, slot] % 8
-        at = pl.ds(pl.multiple_of(table[0, slot] - low, 8), height)
-        length = table[1, slot]
-        mask = key_mask(height, 2 * height, low, length)
-        valid = inside(height, low, length)
-        for pair in range(PAIRS):
-            queries = both_heads(qkv[pair, at, :].astype(BF16))
-            keys = qkv[PAIRS + pair, at, :]
-            grad = jnp.where(valid, d_mixed[pair, at, :], 0.0)
-            grads = both_heads(grad.astype(BF16))
-            scores = dot(keys.astype(BF16), queries, NT)
-            scores = jnp.where(mask, scores, -1e30)
-            probs = jnp.exp(scores - log_total[slot * PAIRS + pair, :, 0 : 2 * height])
-            product = both_heads(grad * mixed[pair, at, :])
-            upper = product.astype(BF16)
-            lower = (product - upper.astype(F32)).astype(BF16)
-            delta = (dot(ones, upper, NT) + dot(ones, lower, NT))[0:1, :]
-            d_probs = dot(qkv[2 * PAIRS + pair, at, :].astype(BF16), grads, NT)
-            d_scores = (probs * (d_probs - delta)).astype(BF16)
-            d_values = dot(probs.astype(BF16), grads)
-            d_keys = dot(d_scores, queries)
-            d_queries = one_of_heads((dot(keys.T.astype(BF16), d_scores) * DH ** (-0.5)).T)
-            pltpu.store(d_qkv.at[pair, at, :], d_queries, mask=valid)
-            pltpu.store(d_qkv.at[PAIRS + pair, at, :], d_keys, mask=valid)
-            pltpu.store(d_qkv.at[2 * PAIRS + pair, at, :], d_values, mask=valid)
+    items = [(n, unit, pair) for n, unit in enumerate(units(images, table)) for pair in range(PAIRS)]
+    biases = {}
+
+    def first(n, unit, pair):
+        if n not in biases:
+            biases[n] = unit.mask()
+        queries, keys, values = (unit.load(qkv, k * PAIRS + pair).astype(BF16) for k in range(3))
+        queries = both_heads(queries)
+        grad = jnp.where(unit.valid, unit.load(d_mixed, pair), 0.0)
+        grads = both_heads(grad.astype(BF16))
+        product = both_heads((grad * unit.load(mixed, pair)).astype(BF16))
+        left = jnp.concatenate([grads, product], axis=1)
+        right = jnp.concatenate([values, -jnp.ones_like(values)], axis=1)
+        return queries, keys, grads, dot(queries, keys, NT), dot(left, right, NT)
+
+    def second(n, unit, pair, queries, keys, grads, scores, d_probs):
+        log_totals = log_total[n, 0 : scores.shape[0], :]
+        probs = jnp.exp(scores + biases[n] - log_totals[:, pair : pair + 1])
+        return queries, keys, grads, probs.astype(BF16), (probs * d_probs).astype(BF16)
+
+    def third(n, unit, pair, queries, keys, grads, probs, d_scores):
+        unit.store(d_qkv, pair, one_of_heads(dot(d_scores, keys)) * DH ** (-0.5))
+        unit.store(d_qkv, PAIRS + pair, dot(d_scores, queries, TN))
+        unit.store(d_qkv, 2 * PAIRS + pair, dot(probs, grads, TN))
+
+    ones, twos = {}, {}
+    for t in range(len(items) + 2):
+        if t < len(items):
+            ones[t] = first(*items[t])
+        if 0 <= t - 1 < len(items):
+            twos[t - 1] = second(*items[t - 1], *ones.pop(t - 1))
+        if 0 <= t - 2 < len(items):
+            third(*items[t - 2], *twos.pop(t - 2))
 
 
 def attend_back(lengths, qkv, mixed, log_total, w_out, d_residual):
     rows = d_residual.shape[0]
-    outs = [(qkv.shape, F32), ((rows, D), BF16), ((8, D), F32)]
+    outs = [(qkv.shape, F32), ((rows, D), BF16)]
     scratch = [pltpu.VMEM(mixed.shape, F32), pltpu.SMEM((2, lengths.shape[0]), jnp.int32)]
     operands = [lengths, qkv, mixed, log_total, w_out, d_residual]
-    return call(attend_back_kernel, "attend_back", operands, outs, scratch, 28, 12)
+    return call(attend_back_kernel, "attend_back", operands, outs, scratch, 22, 12)
 
 
 def project_back_kernel(entries, out_plan, piece, me, *refs):
-    (onehot, embedded, normed_b, mixed, d_qkv, d_branch_b, b_out_sum, w_qkv, vectors, d_residual) = refs[:10]
-    in_grad, pos_out = refs[10:12]
-    targets = [(refs[12 + i], plan) for i, plan in enumerate(out_plan)]
-    flat, d_qkv_b, d_embedded_b, mixed_b, sums = refs[12 + len(out_plan) :]
+    (onehot, embedded, normed_b, mixed, d_qkv, d_branch_b, w_qkv, vectors, d_residual) = refs[:9]
+    in_grad, pos_out = refs[9:11]
+    targets = [(refs[11 + i], plan) for i, plan in enumerate(out_plan)]
+    flat, d_qkv_b, d_embedded_b, mixed_b, sums = refs[11 + len(out_plan) :]
     rows = embedded.shape[0]
     gain = vectors[0:1, :]
     sums[...] = jnp.zeros_like(sums)
@@ -568,25 +643,24 @@
     lax.fori_loop(0, rows // PART, leave, 0)
     in_grad[...] = d_embedded_b[0 : in_grad.shape[0], :]
 
-    flat[...] = jnp.zeros_like(flat)
+    flat[ATTN_ROWS:, :] = jnp.zeros((flat.shape[0] - ATTN_ROWS, LANES), F32)
     write_row(flat, ROW_GAIN_ONE, jnp.sum(sums[0], axis=0, keepdims=True))
     write_row(flat, ROW_BIAS_ONE, jnp.sum(sums[1], axis=0, keepdims=True))
-    write_row(flat, ROW_B_OUT, jnp.sum(b_out_sum[...], axis=0, keepdims=True))
-    normed_t = normed_b[...].T
+    normed_t = with_ones(normed_b[...].T)
     for k in range(3):
         cols = slice(k * D, (k + 1) * D)
         part = dot(normed_t, d_qkv_b[:, cols])
-        total = jnp.sum(fold_rows(d_qkv_b[:, cols].astype(F32)), axis=0, keepdims=True)
-        write_row(flat, ROW_B_QKV + k * D_COLS, total)
+        write_row(flat, ROW_B_QKV + k * D_COLS, part[D : D + 1])
         for c in range(D_COLS):
-            flat[pl.ds(ROW_W_QKV + k * D_COLS + c, D, stride=QKV_COLS), :] = part[:, c * LANES : (c + 1) * LANES]
-    part = dot(mixed_b[...].T, d_branch_b[...])
+            flat[pl.ds(ROW_W_QKV + k * D_COLS + c, D, stride=QKV_COLS), :] = part[0:D, c * LANES : (c + 1) * LANES]
+    part = dot(with_ones(mixed_b[...].T), d_branch_b[...])
+    write_row(flat, ROW_B_OUT, part[D : D + 1])
     for c in range(D_COLS):
-        flat[pl.ds(ROW_W_OUT + c, D, stride=D_COLS), :] = part[:, c * LANES : (c + 1) * LANES]
+        flat[pl.ds(ROW_W_OUT + c, D, stride=D_COLS), :] = part[0:D, c * LANES : (c + 1) * LANES]
     pack(flat, entries, piece, me[0], targets)
 
     pos_grad = dot(onehot[...], d_embedded_b[...], TN)
-    flat[...] = jnp.zeros_like(flat)
+    flat[ROW_GAIN_TWO : pos_out.shape[0], :] = jnp.zeros((pos_out.shape[0] - ROW_GAIN_TWO, LANES), F32)
     for c in range(D_COLS):
         flat[pl.ds(ROW_POS + c, POS, stride=D_COLS), :] = pos_grad[0:POS, c * LANES : (c + 1) * LANES]
     pos_out[...] = flat[0 : pos_out.shape[0], :].astype(BF16)
@@ -604,7 +678,7 @@
         pltpu.VMEM((2, 8, D), F32),
     ]
     kernel = functools.partial(project_back_kernel, entries, out_plan, sizes.attn_rows)
-    return call(kernel, "project_back", [me, *kept], outs, scratch, 28, 10)
+    return call(kernel, "project_back", [me, *kept], outs, scratch, 25, 10)
 
 
 def adamw_step(gradient, weights, first, second):
@@ -616,16 +690,15 @@
     return (update, first_new, second_new)
 
 
-def settle_kernel(scale, counts, place, *refs):
-    attn = refs[: counts[0]]
-    mlp = refs[counts[0] : counts[0] + counts[1]]
-    pos = refs[counts[0] + counts[1] : sum(counts)]
-    refs = refs[sum(counts) :]
+def settle_kernel(scale, plans, count, place, *refs):
+    terms, refs = refs[:count], refs[count:]
     state, outs = (refs[:3], refs[3:6]), (refs[6:10], refs[10:14])
-    total = sum(ref[...].astype(F32) for ref in attn)
-    extra = sum(ref[...].astype(F32) for ref in pos)
-    other = sum(ref[...].astype(F32) for ref in mlp) + jnp.where(place[4] > 0, extra, 0.0)
-    for n, value in enumerate((total, other)):
+
+    def added(plan):
+        return sum(terms[n][first : first + rows, :].astype(F32) for n, first, rows in plan)
+
+    other = added(plans[1]) + jnp.where(place[4] > 0, added(plans[2]), 0.0)
+    for n, value in enumerate((added(plans[0]), other)):
         rows = value.shape[0]
         gradient = take_share(value, place[2 * n], place[2 * n + 1]) * scale
         weights, first, second = (tall(ref, rows) for ref in state[n])
@@ -633,11 +706,11 @@
             put_flat(ref, result)
 
 
-def settle(scale, place, attn, mlp, pos, attn_state, mlp_state):
-    operands = list(attn) + list(mlp) + list(pos) + list(attn_state) + list(mlp_state)
+def settle(scale, place, terms, plans, attn_state, mlp_state):
+    operands = list(terms) + list(attn_state) + list(mlp_state)
     shapes = [attn_state[0].shape] * 4 + [mlp_state[0].shape] * 4
     return pl.pallas_call(
-        functools.partial(settle_kernel, scale, (len(attn), len(mlp), len(pos))),
+        functools.partial(settle_kernel, scale, plans, len(terms)),
         in_specs=[SMEM_SPEC] + [VMEM_SPEC] * len(operands),
         out_specs=[VMEM_SPEC] * len(shapes),
         out_shape=[jax.ShapeDtypeStruct(shape, F32) for shape in shapes],
@@ -709,7 +782,7 @@
         self.pos_count = -(-POS * D // mlp_entries)
         self.pos_flat = flat_rows(mlp_entries, self.pos_count, self.mlp_rows)
         self.pos_flat = max(-(-self.pos_flat // 16) * 16, -(-POS * D_COLS // 16) * 16)
-        self.reach = slots + max(image_rows(0), 2 * BLOCK)
+        self.reach = -(-max(slots + BLOCK, slots - SHORT + image_rows(0)) // 8) * 8
 
 
 class Layer:
@@ -717,10 +790,10 @@
         self.entries, self.sizes, self.slots = entries, sizes, slots
         self.tokens, self.cotangent, self.lengths, self.onehot = tokens, cotangent, lengths, onehot
 
-    def project(self, mask, attn_arrays, pos_arrays, pos_names):
+    def project(self, mask, attn_arrays, pos_plan, pos_names):
         self.mask = mask
         (self.embedded, self.normed_b, self.qkv, self.w_qkv, self.w_out, self.vectors) = project(
-            self.entries, attn_arrays, pos_arrays, pos_names, mask, self.onehot, self.tokens, self.sizes
+            self.entries, attn_arrays, pos_plan, pos_names, mask, self.onehot, self.tokens, self.sizes
         )
 
     def attend(self):
@@ -735,26 +808,26 @@
         return sent
 
     def attend_back(self):
-        self.d_qkv, self.d_branch_b, self.b_out_sum = attend_back(
+        self.d_qkv, self.d_branch_b = attend_back(
             self.lengths, self.qkv, self.mixed, self.log_total, self.w_out, self.d_residual
         )
 
     def project_back(self, plan):
         kept = (self.onehot, self.embedded, self.normed_b, self.mixed, self.d_qkv, self.d_branch_b)
-        kept += (self.b_out_sum, self.w_qkv, self.vectors, self.d_residual)
+        kept += (self.w_qkv, self.vectors, self.d_residual)
         self.in_grad, pos_grad, *sent = project_back(self.entries[0], self.mask, kept, self.slots, plan, self.sizes)
         return pos_grad, sent
 
 
-def step_by_axes(layer, me, attn_piece, mlp_piece):
+def step_by_axes(layer, me, piece):
     sizes, count = layer.sizes, lax.axis_size("dp") * lax.axis_size("rep")
     order = list(range(count))
     height = sizes.mlp_rows
-    attn_all = lax.all_gather(attn_piece, AXES, axis=0, tiled=True)
-    mlp_all = lax.all_gather(mlp_piece, AXES, axis=0, tiled=True)
-    pos_arrays = [mlp_all[j * height : (j + 1) * height] for j in range(sizes.pos_count)]
+    attn_all = lax.all_gather(piece[: sizes.attn_rows], AXES, axis=0, tiled=True)
+    mlp_all = lax.all_gather(piece[sizes.attn_rows :], AXES, axis=0, tiled=True)
+    pos_plan = [(1, j * height) for j in range(sizes.pos_count)]
     pos_names = jnp.arange(sizes.pos_count, dtype=jnp.int32)
-    layer.project(jnp.zeros((1,), jnp.int32), [(attn_all, order)], pos_arrays, pos_names)
+    layer.project(jnp.zeros((1,), jnp.int32), [(attn_all, order), (mlp_all, [])], pos_plan, pos_names)
     layer.attend()
     mlp_sent = layer.feed_forward([(mlp_all, order)], layer.mask, [order])
     layer.attend_back()
@@ -764,30 +837,32 @@
     pos_sum = jnp.pad(lax.psum(pos_grad, AXES), ((0, height), (0, 0)))
     first_row = jnp.minimum((me * layer.entries[1]) // TILE * 8, sizes.pos_flat)
     pos_terms = [lax.dynamic_slice_in_dim(pos_sum, first_row, height, axis=0)]
-    return (layer.output, layer.in_grad), (attn_terms, mlp_terms, pos_terms)
-
-
-def step_by_hand(layer, me, attn_piece, mlp_piece):
+    plans = ([(0, 0, sizes.attn_rows)], [(1, 0, height)], [(2, 0, height)])
+    return (layer.output, layer.in_grad), (attn_terms + mlp_terms + pos_terms, plans)
+
+
+def step_by_hand(layer, me, piece):
     sizes = layer.sizes
+    small, large = sizes.attn_rows, sizes.mlp_rows
     z, plane, core = me // BIT_Z, (me // BIT_X) % 4, me % 2
     plan = sum_plan()
-    attn_z, mlp_z = spread_z(attn_piece), spread_z(mlp_piece)
-    attn_z, layer.onehot = together(attn_z, layer.onehot)
-    attn = jnp.concatenate(attn_z, axis=0)
-    attn = spread_xy(attn)
-    pos = lax.select_n(z, *mlp_z)
-    pos = lax.select_n(plane, *spread_xy(pos))
-    attn, pos, mlp_z = together(attn, pos, mlp_z)
+    pieces = spread_z(piece)
+    pieces, layer.onehot = together(pieces, layer.onehot)
+    table = lax.select_n(z, *[p[small:] for p in pieces])
+    attn = spread_xy(jnp.concatenate([p[:small] for p in pieces] + [table], axis=0))
+    attn, pieces = together(attn, pieces)
     attn = attn + [swap(a, BIT_CORE) for a in attn]
-    pos_arrays = [pos, swap(pos, BIT_CORE)]
-    pos_names = jnp.stack([core, 1 - core])
-    mlp = jnp.concatenate(mlp_z, axis=0)
-    attn, pos_arrays, mlp = together(attn, pos_arrays, mlp)
+    mlp = jnp.concatenate([p[small:] for p in pieces], axis=0)
+    attn, mlp = together(attn, mlp)
+    mlp_far = swap(mlp, BIT_CORE)
     mlp = spread_xy(mlp)
-    layer.project(me.reshape(1), numbered(attn), pos_arrays, pos_names)
+    at = 4 * small
+    pos_plan = [(n, at) for n in range(8)]
+    pos_names = jnp.stack([jnp.where(plane == n % 4, core if n < 4 else 1 - core, -1) for n in range(8)])
+    layer.project(me.reshape(1), numbered(attn), pos_plan, pos_names)
     layer.attend()
-    mlp, layer.residual = together(mlp, layer.residual)
-    mlp = mlp + [swap(a, BIT_CORE) for a in mlp]
+    mlp, mlp_far, layer.residual = together(mlp, mlp_far, layer.residual)
+    mlp = mlp + [mlp_far] + [swap(a, BIT_CORE) for a in mlp[1:]]
     mlp_sent = layer.feed_forward(numbered(mlp), layer.mask, plan)
 
     parts = add_core(mlp_sent)
@@ -798,18 +873,25 @@
     mlp_terms, pos_grad, attn_sent = together(mlp_terms, pos_grad, attn_sent)
 
     offset = layer.entries[1] // TILE * 8
-    pos_parts = [pos_grad[: sizes.mlp_rows], pos_grad[offset : offset + sizes.mlp_rows]]
+    pos_parts = [pos_grad[:large], pos_grad[offset : offset + large]]
     pos_keep = jnp.where(core == 0, pos_parts[0], pos_parts[1])
     pos_send = jnp.where(core == 0, pos_parts[1], pos_parts[0])
     parts, pos = add_core(attn_sent), total([pos_keep, swap(pos_send, BIT_CORE)])
-    mlp_parts = quarters(total(mlp_terms))
-    parts, pos, mlp_parts = together(parts, pos, mlp_parts)
-    attn_terms, pos_terms = swap_xy(parts), spread_xy(pos)
-    mlp_terms = swap_z(mlp_parts)
-    parts, pos = quarters(total(attn_terms)), total(pos_terms)
-    parts, pos = together(parts, pos)
-    attn_terms, pos_terms = swap_z(parts), spread_z(pos)
-    return (layer.output, layer.in_grad), (attn_terms, mlp_terms, pos_terms)
+    sent = [jnp.concatenate([part, pos], axis=0) for part in parts]
+    sent, mlp_terms = together(sent, mlp_terms)
+    came = swap_xy(sent)
+    mlp_came = swap_z(quarters(total(mlp_terms)))
+    came = together(came)[0]
+    whole_sum = total(came)
+    pos = whole_sum[at:]
+    sent = [jnp.concatenate([part, pos], axis=0) for part in quarters(whole_sum[:at])]
+    came = swap_z(together(sent)[0])
+    plans = (
+        [(n, 0, small) for n in range(4)],
+        [(n, 0, large) for n in range(4, 8)],
+        [(n, small, large) for n in range(4)],
+    )
+    return (layer.output, layer.in_grad), (came + mlp_came, plans)
 
 
 def body(
@@ -837,13 +919,16 @@
     place = jnp.stack(
         [starts[0] % LANES, starts[0] // LANES, starts[1] % LANES, starts[1] // LANES, (me < 2).astype(jnp.int32)]
     )
-    attn_piece, mlp_piece = pl.pallas_call(
-        align_kernel,
-        in_specs=[SMEM_SPEC, VMEM_SPEC, VMEM_SPEC],
-        out_specs=[VMEM_SPEC, VMEM_SPEC],
-        out_shape=[
-            jax.ShapeDtypeStruct((sizes.attn_rows, LANES), BF16),
-            jax.ShapeDtypeStruct((sizes.mlp_rows, LANES), BF16),
+    heights = (sizes.attn_rows, sizes.mlp_rows)
+    piece = pl.pallas_call(
+        functools.partial(align_kernel, heights),
+        in_specs=[SMEM_SPEC, HBM_SPEC, HBM_SPEC],
+        out_specs=VMEM_SPEC,
+        out_shape=jax.ShapeDtypeStruct((sum(heights), LANES), BF16),
+        scratch_shapes=[
+            pltpu.VMEM(attn_params.shape, F32),
+            pltpu.VMEM(mlp_params.shape, F32),
+            pltpu.SemaphoreType.DMA((2,)),
         ],
         compiler_params=params(8),
         name="align",
@@ -853,9 +938,9 @@
     onehot = (pos_full[:, None] == jnp.arange(256, dtype=jnp.int32)[None, :]).astype(BF16)
     layer = Layer(entries, sizes, slots, tokens, cotangent, lengths, onehot)
     if by_hand:
-        outputs, terms = step_by_hand(layer, me, attn_piece, mlp_piece)
+        outputs, terms = step_by_hand(layer, me, piece)
     else:
-        outputs, terms = step_by_axes(layer, me, attn_piece, mlp_piece)
+        outputs, terms = step_by_axes(layer, me, piece)
         place = place.at[4].set(1)
     scale = 1.0 / math.sqrt(slots * count)
     attn_state, mlp_state = (attn_params, attn_first, attn_second), (mlp_params, mlp_first, mlp_second)

time: 144 us -> 128 us (0.89)
  waiting for transfers between devices: 28 us -> 50 us
  starting transfers between devices: 50.6 us -> 32 us
  Pallas kernels: 53.7 us -> 39.7 us
  local copies, waits for them, and re-layouts: 7.84 us -> 3.68 us
    ppermute x45 -> x32, waiting for transfers between devices: 28 us -> 50 us  [swap(): return lax.ppermute(value, AXES, [(j, j ^ bits) for j in range(DEVICES)])]
    ppermute x45 -> x32, starting transfers between devices: 50.6 us -> 32 us  [swap(): return lax.ppermute(value, AXES, [(j, j ^ bits) for j in range(DEVICES)])]
    pallas_call x5, Pallas kernels: 51.2 us -> 36.9 us  [call(): pl.pallas_call(kernel, in_specs=[SMEM_SPEC if a.dtype == jnp.int32 and a....]
    unnamed x49 -> x34, local copies, waits for them, and re-layouts: 7.01 us -> 2.74 us
  transfers between devices with their start and end apart: 45 -> 32, of which waited for: 20 -> 20; matrix products, arithmetic and copies ran while one was open for 1% -> 1% of each run, Pallas kernels for 23% -> 18%
where the time goes in v1:
time: 128 us
  waiting for transfers between devices  50 us (39%)
  Pallas kernels  39.7 us (31%)
  starting transfers between devices  32 us (25%)
  local copies, waits for them, and re-layouts  3.68 us (3%)
  other arithmetic  1.29 us (1%)
    ppermute x32, waiting for transfers between devices, swap(): return lax.ppermute(value, AXES, [(j, j ^ bits) for j in range(DEVICES)])  50 us
    pallas_call x5, Pallas kernels, call(): pl.pallas_call(kernel, in_specs=[SMEM_SPEC if a.dtype == jnp.int32 and a....  36.9 us
    ppermute x32, starting transfers between devices, swap(): return lax.ppermute(value, AXES, [(j, j ^ bits) for j in range(DEVICES)])  32 us
    unnamed x34, local copies, waits for them, and re-layouts  2.74 us
  transfers between devices with their start and end apart: 32, of which 20 were waited for; matrix products, arithmetic and copies ran while one was open for 1% of the time, Pallas kernels for 18%

profile of v1, /device:TPU:0, one launch (start us, length us, event | category | flops | bytes accessed | tf_op | source)
XLA Modules:
  0.0 127.8 jit_solution(1979375668303720795)
XLA Ops:
  0.8 0.9 copy-done
  2.6 1.1 align.1
  3.7 5.1 %collective-permute-start.2 = (bf16[480,128]{1,0:T(8,128)(2,1)S(1)}, bf16[480,128]{1,0:T(8,128)(2,1)S(1)}, u32[]{:S(2)}, u32[]{:S(2)}) collective-permute-start(bf16[480,128]{1,0:T(8,128)(2,1)S(1)} %align.1), channel_id=1, source_target_pairs={{0,24},{1,25},{2,26},{3,27},{4,28},{5,29},{6,30},{7,31},{8,16},{9,... | collective-permute-start | bytes 368648 | tf_op jit(solution)/shard_map/ppermute | solution.py:729
  10.4 2.7 %collective-permute-done.2 = bf16[480,128]{1,0:T(8,128)(2,1)S(1)} collective-permute-done((bf16[480,128]{1,0:T(8,128)(2,1)S(1)}, bf16[480,128]{1,0:T(8,128)(2,1)S(1)}, u32[]{:S(2)}, u32[]{:S(2)}) %collective-permute-start.2) | collective-permute-done | bytes 122912 | tf_op jit(solution)/shard_map/ppermute | solution.py:729
  13.1 6.1 %collective-permute-done.1 = bf16[480,128]{1,0:T(8,128)(2,1)S(1)} collective-permute-done((bf16[480,128]{1,0:T(8,128)(2,1)S(1)}, bf16[480,128]{1,0:T(8,128)(2,1)S(1)}, u32[]{:S(2)}, u32[]{:S(2)}) %collective-permute-start.1) | collective-permute-done | bytes 122912 | tf_op jit(solution)/shard_map/ppermute | solution.py:729
  19.3 2.5 %collective-permute-start.5 = (bf16[960,128]{1,0:T(8,128)(2,1)S(1)}, bf16[960,128]{1,0:T(8,128)(2,1)S(1)}, u32[]{:S(2)}, u32[]{:S(2)}) collective-permute-start(bf16[960,128]{1,0:T(8,128)(2,1)S(1)} %select_dynamic-update-slice_fusion.refs_0_), channel_id=1, source_target_pairs={{0,6},{1,7},{2,4},{3,5},{4,2},{5,3},{6,0},{7,1},{8,14},{9,15},{10,... | collective-permute-start | bytes 737288 | tf_op jit(solution)/shard_map/ppermute | solution.py:729
  22.9 6.3 %collective-permute-done.5.refs_3_ = bf16[960,128]{1,0:T(8,128)(2,1)S(1)} collective-permute-done((bf16[960,128]{1,0:T(8,128)(2,1)S(1)}, bf16[960,128]{1,0:T(8,128)(2,1)S(1)}, u32[]{:S(2)}, u32[]{:S(2)}) %collective-permute-start.5) | collective-permute-done | bytes 245792 | tf_op jit(solution)/shard_map/ppermute | solution.py:729
  29.2 3.3 %collective-permute-done.4.refs_2_ = bf16[960,128]{1,0:T(8,128)(2,1)S(1)} collective-permute-done((bf16[960,128]{1,0:T(8,128)(2,1)S(1)}, bf16[960,128]{1,0:T(8,128)(2,1)S(1)}, u32[]{:S(2)}, u32[]{:S(2)}) %collective-permute-start.4) | collective-permute-done | bytes 245792 | tf_op jit(solution)/shard_map/ppermute | solution.py:729
  35.5 1.7 %collective-permute-start.12 = (bf16[1280,128]{1,0:T(8,128)(2,1)S(1)}, bf16[1280,128]{1,0:T(8,128)(2,1)S(1)}, u32[]{:S(2)}, u32[]{:S(2)}) collective-permute-start(bf16[1280,128]{1,0:T(8,128)(2,1)S(1)} %pad_maximum_fusion.4.refs_0_), channel_id=1, source_target_pairs={{0,6},{1,7},{2,4},{3,5},{4,2},{5,3},{6,0},{7,1},{8,14},{9,15},{10,... | collective-permute-start | bytes 983048 | tf_op jit(solution)/shard_map/ppermute | solution.py:729
  37.2 1.3 %collective-permute-start.11 = (bf16[1280,128]{1,0:T(8,128)(2,1)S(1)}, bf16[1280,128]{1,0:T(8,128)(2,1)S(1)}, u32[]{:S(2)}, u32[]{:S(2)}) collective-permute-start(bf16[1280,128]{1,0:T(8,128)(2,1)S(1)} %pad_maximum_fusion.4.refs_0_), channel_id=1, source_target_pairs={{0,4},{1,5},{2,6},{3,7},{4,0},{5,1},{6,2},{7,3},{8,12},{9,13},{10,... | collective-permute-start | bytes 983048 | tf_op jit(solution)/shard_map/ppermute | solution.py:729
  39.0 4.6 %project.1 = (f32[1024,384]{1,0:T(8,128)S(1)}, bf16[1024,384]{1,0:T(8,128)(2,1)S(1)}, f32[9,1112,128]{2,1,0:T(8,128)S(1)}, bf16[384,1152]{1,0:T(8,128)(2,1)S(1)}...) custom-call(s32[1]{0:T(128)} %bitcast.me.mask, s32[8]{0:T(128)S(1)} %stack.63.pos_names, ...), custom_call_target="tpu_custom_call" | custom-call | flops 9200000000 | bytes 1024 | tf_op jit(solution)/shard_map/project/pallas_call | solution.py:193
  43.6 5.5 %attend.1 = (f32[3,1112,128]{2,1,0:T(8,128)S(1)}, f32[8,320,128]{2,1,0:T(8,128)S(1)}, f32[1024,384]{1,0:T(8,128)S(1)}) custom-call(s32[12]{0:T(128)S(1)} %copy-done.10, f32[9,1112,128]{2,1,0:T(8,128)S(1)} %get-tuple-element.124.qkv, f32[1024,384]{1,0:T(8,128)S(1)} %get-tuple-element.125.embedded.refs_1_, bf16[384,384]{1,0:T(8,128)(2,1)S(1)} %get-tuple-element.126.w_out, ...), custom_call_target="tpu_custom_call" | custom-call | flops 11500000256 | bytes 1024 | tf_op jit(solution)/shard_map/attend/pallas_call | solution.py:193
  49.2 4.2 %collective-permute-done.11.refs_2_ = bf16[1280,128]{1,0:T(8,128)(2,1)S(1)} collective-permute-done((bf16[1280,128]{1,0:T(8,128)(2,1)S(1)}, bf16[1280,128]{1,0:T(8,128)(2,1)S(1)}, u32[]{:S(2)}, u32[]{:S(2)}) %collective-permute-start.11) | collective-permute-done | bytes 327712 | tf_op jit(solution)/shard_map/ppermute | solution.py:729
  54.0 1.1 collective-permute-done.14.refs_5_
  56.0 14.4 %feed_forward.1 = (bf16[984,384]{1,0:T(8,128)(2,1)}, f32[1024,384]{1,0:T(8,128)S(1)}, bf16[5120,128]{1,0:T(8,128)(2,1)S(1)}, bf16[1280,128]{1,0:T(8,128)(2,1)S(1...) custom-call(s32[1]{0:T(128)} %bitcast.me.mask, s32[1]{0:T(128)} %bitcast.me.mask, ...), custom_call_target="tpu_custom_call" | custom-call | flops 20700000256 | bytes 1024 | tf_op jit(solution)/shard_map/feed_forward/pallas_call | solution.py:193
  70.5 2.9 %collective-permute-done.17 = bf16[5120,128]{1,0:T(8,128)(2,1)S(1)} collective-permute-done((bf16[5120,128]{1,0:T(8,128)(2,1)S(1)}, bf16[5120,128]{1,0:T(8,128)(2,1)S(1)}, u32[]{:S(2)}, u32[]{:S(2)}) %collective-permute-start.17) | collective-permute-done | bytes 1310752 | tf_op jit(solution)/shard_map/ppermute | solution.py:729
  73.7 1.6 %collective-permute-start.18 = (bf16[1280,128]{1,0:T(8,128)(2,1)S(1)}, bf16[1280,128]{1,0:T(8,128)(2,1)S(1)}, u32[]{:S(2)}, u32[]{:S(2)}) collective-permute-start(bf16[1280,128]{1,0:T(8,128)(2,1)S(1)} %get-tuple-element.151), channel_id=1, source_target_pairs={{0,2},{1,3},{2,0},{3,1},{4,6},{5,7},{6,4},{7,5},{8,10},{9,11},{10,... | collective-permute-start | bytes 983048 | tf_op jit(solution)/shard_map/ppermute | solution.py:729
  76.0 1.3 collective-permute-start.20
  77.3 6.7 %attend_back.1 = (f32[9,1112,128]{2,1,0:T(8,128)S(1)}, bf16[1024,384]{1,0:T(8,128)(2,1)S(1)}) custom-call(s32[12]{0:T(128)S(1)} %copy-done.10, f32[9,1112,128]{2,1,0:T(8,128)S(1)} %get-tuple-element.124.qkv, f32[3,1112,128]{2,1,0:T(8,128)S(1)} %get-tuple-element.137.mixed.refs_3_, f32[8,320,128]{2,1,0:T(8,128)S(1)} %get-tuple-element.138.log_total, ...), custom_call_target="tpu_custom_call" | custom-call | flops 13799999488 | bytes 1024 | tf_op jit(solution)/shard_map/attend_back/pallas_call | solution.py:193
  84.0 5.7 %project_back.1 = (bf16[984,384]{1,0:T(8,128)(2,1)}, bf16[624,128]{1,0:T(8,128)(2,1)S(1)}, bf16[2560,128]{1,0:T(8,128)(2,1)S(1)}, bf16[640,128]{1,0:T(8,128)(2,1...) custom-call(s32[1]{0:T(128)} %bitcast.me.mask, ...), custom_call_target="tpu_custom_call" | custom-call | flops 11500000256 | bytes 1024 | tf_op jit(solution)/shard_map/project_back/pallas_call | solution.py:193
  89.7 2.1 %collective-permute-done.19 = bf16[1280,128]{1,0:T(8,128)(2,1)S(1)} collective-permute-done((bf16[1280,128]{1,0:T(8,128)(2,1)S(1)}, bf16[1280,128]{1,0:T(8,128)(2,1)S(1)}, u32[]{:S(2)}, u32[]{:S(2)}) %collective-permute-start.19) | collective-permute-done | bytes 327712 | tf_op jit(solution)/shard_map/ppermute | solution.py:729
  93.2 1.6 %collective-permute-done.22 = bf16[320,128]{1,0:T(8,128)(2,1)S(1)} collective-permute-done((bf16[320,128]{1,0:T(8,128)(2,1)S(1)}, bf16[320,128]{1,0:T(8,128)(2,1)S(1)}, u32[]{:S(2)}, u32[]{:S(2)}) %collective-permute-start.22) | collective-permute-done | bytes 81952 | tf_op jit(solution)/shard_map/ppermute | solution.py:729
  95.7 1.5 %collective-permute-start.24 = (bf16[960,128]{1,0:T(8,128)(2,1)S(1)}, bf16[960,128]{1,0:T(8,128)(2,1)S(1)}, u32[]{:S(2)}, u32[]{:S(2)}) collective-permute-start(bf16[960,128]{1,0:T(8,128)(2,1)S(1)} %get-tuple-element.172), channel_id=1, source_target_pairs={{0,4},{1,5},{2,6},{3,7},{4,0},{5,1},{6,2},{7,3},{8,12},{9,13},{10,... | collective-permute-start | bytes 737288 | tf_op jit(solution)/shard_map/ppermute | solution.py:729
  97.2 1.5 %collective-permute-start.25 = (bf16[960,128]{1,0:T(8,128)(2,1)S(1)}, bf16[960,128]{1,0:T(8,128)(2,1)S(1)}, u32[]{:S(2)}, u32[]{:S(2)}) collective-permute-start(bf16[960,128]{1,0:T(8,128)(2,1)S(1)} %get-tuple-element.173), channel_id=1, source_target_pairs={{0,6},{1,7},{2,4},{3,5},{4,2},{5,3},{6,0},{7,1},{8,14},{9,15},{10,... | collective-permute-start | bytes 737288 | tf_op jit(solution)/shard_map/ppermute | solution.py:729
  99.1 2.4 %collective-permute-start.31 = (bf16[320,128]{1,0:T(8,128)(2,1)S(1)}, bf16[320,128]{1,0:T(8,128)(2,1)S(1)}, u32[]{:S(2)}, u32[]{:S(2)}) collective-permute-start(bf16[320,128]{1,0:T(8,128)(2,1)S(1)} %get-tuple-element.202), channel_id=1, source_target_pairs={{0,24},{1,25},{2,26},{3,27},{4,28},{5,29},{6,30},{7,31},{8,16},{9,... | collective-permute-start | bytes 245768 | tf_op jit(solution)/shard_map/ppermute | solution.py:729
  101.4 2.7 %collective-permute-done.23 = bf16[960,128]{1,0:T(8,128)(2,1)S(1)} collective-permute-done((bf16[960,128]{1,0:T(8,128)(2,1)S(1)}, bf16[960,128]{1,0:T(8,128)(2,1)S(1)}, u32[]{:S(2)}, u32[]{:S(2)}) %collective-permute-start.23) | collective-permute-done | bytes 245792 | tf_op jit(solution)/shard_map/ppermute | solution.py:729
  104.2 4.5 %collective-permute-done.25 = bf16[960,128]{1,0:T(8,128)(2,1)S(1)} collective-permute-done((bf16[960,128]{1,0:T(8,128)(2,1)S(1)}, bf16[960,128]{1,0:T(8,128)(2,1)S(1)}, u32[]{:S(2)}, u32[]{:S(2)}) %collective-permute-start.25) | collective-permute-done | bytes 245792 | tf_op jit(solution)/shard_map/ppermute | solution.py:729
  109.0 2.8 %collective-permute-start.27 = (bf16[480,128]{1,0:T(8,128)(2,1)S(1)}, bf16[480,128]{1,0:T(8,128)(2,1)S(1)}, u32[]{:S(2)}, u32[]{:S(2)}) collective-permute-start(bf16[480,128]{1,0:T(8,128)(2,1)S(1)} %get-tuple-element.180), channel_id=1, source_target_pairs={{0,16},{1,17},{2,18},{3,19},{4,20},{5,21},{6,22},{7,23},{8,24},{9,... | collective-permute-start | bytes 368648 | tf_op jit(solution)/shard_map/ppermute | solution.py:729
  111.8 1.5 %collective-permute-start.28 = (bf16[480,128]{1,0:T(8,128)(2,1)S(1)}, bf16[480,128]{1,0:T(8,128)(2,1)S(1)}, u32[]{:S(2)}, u32[]{:S(2)}) collective-permute-start(bf16[480,128]{1,0:T(8,128)(2,1)S(1)} %concatenate.40), channel_id=1, source_target_pairs={{0,24},{1,25},{2,26},{3,27},{4,28},{5,29},{6,30},{7,31},{8,16},{9,... | collective-permute-start | bytes 368648 | tf_op jit(solution)/shard_map/ppermute | solution.py:729
  113.4 2.8 %collective-permute-start.29 = (bf16[320,128]{1,0:T(8,128)(2,1)S(1)}, bf16[320,128]{1,0:T(8,128)(2,1)S(1)}, u32[]{:S(2)}, u32[]{:S(2)}) collective-permute-start(bf16[320,128]{1,0:T(8,128)(2,1)S(1)} %get-tuple-element.204), channel_id=1, source_target_pairs={{0,8},{1,9},{2,10},{3,11},{4,12},{5,13},{6,14},{7,15},{8,0},{9,1},... | collective-permute-start | bytes 245768 | tf_op jit(solution)/shard_map/ppermute | solution.py:729
  116.2 9.7 %collective-permute-done.30.refs_6_ = bf16[320,128]{1,0:T(8,128)(2,1)S(1)} collective-permute-done((bf16[320,128]{1,0:T(8,128)(2,1)S(1)}, bf16[320,128]{1,0:T(8,128)(2,1)S(1)}, u32[]{:S(2)}, u32[]{:S(2)}) %collective-permute-start.30) | collective-permute-done | bytes 81952 | tf_op jit(solution)/shard_map/ppermute | solution.py:729
  126.0 1.8 %settle.1 = (f32[18504]{0:T(1024)}, f32[18504]{0:T(1024)}, f32[18504]{0:T(1024)}, f32[18504]{0:T(1024)}, f32[38688]{0:T(1024)}, /*index=5*/f32[38688]{0:T(1024)}, f32[38688]{0:T(1024)}, f32[38688]{0:T(1024)}) custom-call(s32[5]{0:T(128)S(1)} %stack.54.place, bf16[480,128]{1,0:T(8,128)(2,1)S(1)} %get-tuple-element.178.refs_0_, ...), custom_call_target="tpu_custom_call" | custom-call | tf_op jit(solution)/shard_map/settle/pallas_call | solution.py:712
  (95 shorter events, 12.7 us)
Async XLA Ops:
  3.7 9.4 %collective-permute-start.2 = (bf16[480,128]{1,0:T(8,128)(2,1)S(1)}, bf16[480,128]{1,0:T(8,128)(2,1)S(1)}, u32[]{:S(2)}, u32[]{:S(2)}) collective-permute-start(bf16[480,128]{1,0:T(8,128)(2,1)S(1)} %align.1), channel_id=1, source_target_pairs={{0,24},{1,25},{2,26},{3,27},{4,28},{5,29},{6,30},{7,31},{8,16},{9,... | collective-permute-start | bytes 368648 | tf_op jit(solution)/shard_map/ppermute | solution.py:729
  8.8 10.4 %collective-permute-start.1 = (bf16[480,128]{1,0:T(8,128)(2,1)S(1)}, bf16[480,128]{1,0:T(8,128)(2,1)S(1)}, u32[]{:S(2)}, u32[]{:S(2)}) collective-permute-start(bf16[480,128]{1,0:T(8,128)(2,1)S(1)} %align.1), channel_id=1, source_target_pairs={{0,16},{1,17},{2,18},{3,19},{4,20},{5,21},{6,22},{7,23},{8,24},{9,... | collective-permute-start | bytes 368648 | tf_op jit(solution)/shard_map/ppermute | solution.py:729
  8.8 10.4 %collective-permute-start = (bf16[480,128]{1,0:T(8,128)(2,1)S(1)}, bf16[480,128]{1,0:T(8,128)(2,1)S(1)}, u32[]{:S(2)}, u32[]{:S(2)}) collective-permute-start(bf16[480,128]{1,0:T(8,128)(2,1)S(1)} %align.1), channel_id=1, source_target_pairs={{0,8},{1,9},{2,10},{3,11},{4,12},{5,13},{6,14},{7,15},{8,0},{9,1},... | collective-permute-start | bytes 368648 | tf_op jit(solution)/shard_map/ppermute | solution.py:729
  19.3 9.9 %collective-permute-start.5 = (bf16[960,128]{1,0:T(8,128)(2,1)S(1)}, bf16[960,128]{1,0:T(8,128)(2,1)S(1)}, u32[]{:S(2)}, u32[]{:S(2)}) collective-permute-start(bf16[960,128]{1,0:T(8,128)(2,1)S(1)} %select_dynamic-update-slice_fusion.refs_0_), channel_id=1, source_target_pairs={{0,6},{1,7},{2,4},{3,5},{4,2},{5,3},{6,0},{7,1},{8,14},{9,15},{10,... | collective-permute-start | bytes 737288 | tf_op jit(solution)/shard_map/ppermute | solution.py:729
  21.8 10.7 %collective-permute-start.4 = (bf16[960,128]{1,0:T(8,128)(2,1)S(1)}, bf16[960,128]{1,0:T(8,128)(2,1)S(1)}, u32[]{:S(2)}, u32[]{:S(2)}) collective-permute-start(bf16[960,128]{1,0:T(8,128)(2,1)S(1)} %select_dynamic-update-slice_fusion.refs_0_), channel_id=1, source_target_pairs={{0,4},{1,5},{2,6},{3,7},{4,0},{5,1},{6,2},{7,3},{8,12},{9,13},{10,... | collective-permute-start | bytes 737288 | tf_op jit(solution)/shard_map/ppermute | solution.py:729
  22.3 10.3 %collective-permute-start.3 = (bf16[960,128]{1,0:T(8,128)(2,1)S(1)}, bf16[960,128]{1,0:T(8,128)(2,1)S(1)}, u32[]{:S(2)}, u32[]{:S(2)}) collective-permute-start(bf16[960,128]{1,0:T(8,128)(2,1)S(1)} %select_dynamic-update-slice_fusion.refs_0_), channel_id=1, source_target_pairs={{0,2},{1,3},{2,0},{3,1},{4,6},{5,7},{6,4},{7,5},{8,10},{9,11},{10,... | collective-permute-start | bytes 737288 | tf_op jit(solution)/shard_map/ppermute | solution.py:729
  32.7 1.5 %collective-permute-start.6 = (bf16[960,128]{1,0:T(8,128)(2,1)S(1)}, bf16[960,128]{1,0:T(8,128)(2,1)S(1)}, u32[]{:S(2)}, u32[]{:S(2)}) collective-permute-start(bf16[960,128]{1,0:T(8,128)(2,1)S(1)} %select_dynamic-update-slice_fusion.refs_0_), channel_id=1, source_target_pairs={{0,1},{1,0},{2,3},{3,2},{4,5},{5,4},{6,7},{7,6},{8,9},{9,8},{10,11... | collective-permute-start | bytes 737288 | tf_op jit(solution)/shard_map/ppermute | solution.py:729
  32.7 1.9 %collective-permute-start.7 = (bf16[960,128]{1,0:T(8,128)(2,1)S(1)}, bf16[960,128]{1,0:T(8,128)(2,1)S(1)}, u32[]{:S(2)}, u32[]{:S(2)}) collective-permute-start(bf16[960,128]{1,0:T(8,128)(2,1)S(1)} %collective-permute-done.3.refs_1_), channel_id=1, source_target_pairs={{0,1},{1,0},{2,3},{3,2},{4,5},{5,4},{6,7},{7,6},{8,9},{9,8},{10,11... | collective-permute-start | bytes 737288 | tf_op jit(solution)/shard_map/ppermute | solution.py:729
  33.2 2.1 %collective-permute-start.8 = (bf16[960,128]{1,0:T(8,128)(2,1)S(1)}, bf16[960,128]{1,0:T(8,128)(2,1)S(1)}, u32[]{:S(2)}, u32[]{:S(2)}) collective-permute-start(bf16[960,128]{1,0:T(8,128)(2,1)S(1)} %collective-permute-done.4.refs_2_), channel_id=1, source_target_pairs={{0,1},{1,0},{2,3},{3,2},{4,5},{5,4},{6,7},{7,6},{8,9},{9,8},{10,11... | collective-permute-start | bytes 737288 | tf_op jit(solution)/shard_map/ppermute | solution.py:729
  33.2 2.2 %collective-permute-start.9 = (bf16[960,128]{1,0:T(8,128)(2,1)S(1)}, bf16[960,128]{1,0:T(8,128)(2,1)}, u32[]{:S(2)}, u32[]{:S(2)}) collective-permute-start(bf16[960,128]{1,0:T(8,128)(2,1)S(1)} %collective-permute-done.5.refs_3_), channel_id=1, source_target_pairs={{0,1},{1,0},{2,3},{3,2},{4,5},{5,4},{6,7},{7,6},{8,9},{9,8},{10,11... | collective-permute-start | bytes 737288 | tf_op jit(solution)/shard_map/ppermute | solution.py:729
  35.4 13.8 %collective-permute-start.13 = (bf16[1280,128]{1,0:T(8,128)(2,1)S(1)}, bf16[1280,128]{1,0:T(8,128)(2,1)S(1)}, u32[]{:S(2)}, u32[]{:S(2)}) collective-permute-start(bf16[1280,128]{1,0:T(8,128)(2,1)S(1)} %pad_maximum_fusion.4.refs_0_), channel_id=1, source_target_pairs={{0,1},{1,0},{2,3},{3,2},{4,5},{5,4},{6,7},{7,6},{8,9},{9,8},{10,11... | collective-permute-start | bytes 983048 | tf_op jit(solution)/shard_map/ppermute | solution.py:729
  35.5 13.7 %collective-permute-start.12 = (bf16[1280,128]{1,0:T(8,128)(2,1)S(1)}, bf16[1280,128]{1,0:T(8,128)(2,1)S(1)}, u32[]{:S(2)}, u32[]{:S(2)}) collective-permute-start(bf16[1280,128]{1,0:T(8,128)(2,1)S(1)} %pad_maximum_fusion.4.refs_0_), channel_id=1, source_target_pairs={{0,6},{1,7},{2,4},{3,5},{4,2},{5,3},{6,0},{7,1},{8,14},{9,15},{10,... | collective-permute-start | bytes 983048 | tf_op jit(solution)/shard_map/ppermute | solution.py:729
  37.2 16.2 %collective-permute-start.11 = (bf16[1280,128]{1,0:T(8,128)(2,1)S(1)}, bf16[1280,128]{1,0:T(8,128)(2,1)S(1)}, u32[]{:S(2)}, u32[]{:S(2)}) collective-permute-start(bf16[1280,128]{1,0:T(8,128)(2,1)S(1)} %pad_maximum_fusion.4.refs_0_), channel_id=1, source_target_pairs={{0,4},{1,5},{2,6},{3,7},{4,0},{5,1},{6,2},{7,3},{8,12},{9,13},{10,... | collective-permute-start | bytes 983048 | tf_op jit(solution)/shard_map/ppermute | solution.py:729
  38.5 14.9 %collective-permute-start.10 = (bf16[1280,128]{1,0:T(8,128)(2,1)S(1)}, bf16[1280,128]{1,0:T(8,128)(2,1)S(1)}, u32[]{:S(2)}, u32[]{:S(2)}) collective-permute-start(bf16[1280,128]{1,0:T(8,128)(2,1)S(1)} %pad_maximum_fusion.4.refs_0_), channel_id=1, source_target_pairs={{0,2},{1,3},{2,0},{3,1},{4,6},{5,7},{6,4},{7,5},{8,10},{9,11},{10,... | collective-permute-start | bytes 983048 | tf_op jit(solution)/shard_map/ppermute | solution.py:729
  53.4 1.6 %collective-permute-start.14 = (bf16[1280,128]{1,0:T(8,128)(2,1)S(1)}, bf16[1280,128]{1,0:T(8,128)(2,1)S(1)}, u32[]{:S(2)}, u32[]{:S(2)}) collective-permute-start(bf16[1280,128]{1,0:T(8,128)(2,1)S(1)} %collective-permute-done.10.refs_1_), channel_id=1, source_target_pairs={{0,1},{1,0},{2,3},{3,2},{4,5},{5,4},{6,7},{7,6},{8,9},{9,8},{10,11... | collective-permute-start | bytes 983048 | tf_op jit(solution)/shard_map/ppermute | solution.py:729
  53.4 2.1 %collective-permute-start.15 = (bf16[1280,128]{1,0:T(8,128)(2,1)S(1)}, bf16[1280,128]{1,0:T(8,128)(2,1)S(1)}, u32[]{:S(2)}, u32[]{:S(2)}) collective-permute-start(bf16[1280,128]{1,0:T(8,128)(2,1)S(1)} %collective-permute-done.11.refs_2_), channel_id=1, source_target_pairs={{0,1},{1,0},{2,3},{3,2},{4,5},{5,4},{6,7},{7,6},{8,9},{9,8},{10,11... | collective-permute-start | bytes 983048 | tf_op jit(solution)/shard_map/ppermute | solution.py:729
  53.9 2.1 %collective-permute-start.16 = (bf16[1280,128]{1,0:T(8,128)(2,1)S(1)}, bf16[1280,128]{1,0:T(8,128)(2,1)S(1)}, u32[]{:S(2)}, u32[]{:S(2)}) collective-permute-start(bf16[1280,128]{1,0:T(8,128)(2,1)S(1)} %collective-permute-done.12.refs_3_), channel_id=1, source_target_pairs={{0,1},{1,0},{2,3},{3,2},{4,5},{5,4},{6,7},{7,6},{8,9},{9,8},{10,11... | collective-permute-start | bytes 983048 | tf_op jit(solution)/shard_map/ppermute | solution.py:729
  70.4 3.0 %collective-permute-start.17 = (bf16[5120,128]{1,0:T(8,128)(2,1)S(1)}, bf16[5120,128]{1,0:T(8,128)(2,1)S(1)}, u32[]{:S(2)}, u32[]{:S(2)}) collective-permute-start(bf16[5120,128]{1,0:T(8,128)(2,1)S(1)} %get-tuple-element.140), channel_id=1, source_target_pairs={{0,1},{1,0},{2,3},{3,2},{4,5},{5,4},{6,7},{7,6},{8,9},{9,8},{10,11... | collective-permute-start | bytes 3932168 | tf_op jit(solution)/shard_map/ppermute | solution.py:729
  73.7 16.0 %collective-permute-start.18 = (bf16[1280,128]{1,0:T(8,128)(2,1)S(1)}, bf16[1280,128]{1,0:T(8,128)(2,1)S(1)}, u32[]{:S(2)}, u32[]{:S(2)}) collective-permute-start(bf16[1280,128]{1,0:T(8,128)(2,1)S(1)} %get-tuple-element.151), channel_id=1, source_target_pairs={{0,2},{1,3},{2,0},{3,1},{4,6},{5,7},{6,4},{7,5},{8,10},{9,11},{10,... | collective-permute-start | bytes 983048 | tf_op jit(solution)/shard_map/ppermute | solution.py:729
  75.3 16.5 %collective-permute-start.19 = (bf16[1280,128]{1,0:T(8,128)(2,1)S(1)}, bf16[1280,128]{1,0:T(8,128)(2,1)S(1)}, u32[]{:S(2)}, u32[]{:S(2)}) collective-permute-start(bf16[1280,128]{1,0:T(8,128)(2,1)S(1)} %get-tuple-element.152), channel_id=1, source_target_pairs={{0,4},{1,5},{2,6},{3,7},{4,0},{5,1},{6,2},{7,3},{8,12},{9,13},{10,... | collective-permute-start | bytes 983048 | tf_op jit(solution)/shard_map/ppermute | solution.py:729
  76.0 15.8 %collective-permute-start.20 = (bf16[1280,128]{1,0:T(8,128)(2,1)S(1)}, bf16[1280,128]{1,0:T(8,128)(2,1)S(1)}, u32[]{:S(2)}, u32[]{:S(2)}) collective-permute-start(bf16[1280,128]{1,0:T(8,128)(2,1)S(1)} %get-tuple-element.153), channel_id=1, source_target_pairs={{0,6},{1,7},{2,4},{3,5},{4,2},{5,3},{6,0},{7,1},{8,14},{9,15},{10,... | collective-permute-start | bytes 983048 | tf_op jit(solution)/shard_map/ppermute | solution.py:729
  92.6 2.3 %collective-permute-start.21 = (bf16[2560,128]{1,0:T(8,128)(2,1)S(1)}, bf16[2560,128]{1,0:T(8,128)(2,1)S(1)}, u32[]{:S(2)}, u32[]{:S(2)}) collective-permute-start(bf16[2560,128]{1,0:T(8,128)(2,1)S(1)} %get-tuple-element.161), channel_id=1, source_target_pairs={{0,1},{1,0},{2,3},{3,2},{4,5},{5,4},{6,7},{7,6},{8,9},{9,8},{10,11... | collective-permute-start | bytes 1966088 | tf_op jit(solution)/shard_map/ppermute | solution.py:729
  92.7 2.2 %collective-permute-start.22 = (bf16[320,128]{1,0:T(8,128)(2,1)S(1)}, bf16[320,128]{1,0:T(8,128)(2,1)S(1)}, u32[]{:S(2)}, u32[]{:S(2)}) collective-permute-start(bf16[320,128]{1,0:T(8,128)(2,1)S(1)} %broadcast_select_fusion), channel_id=1, source_target_pairs={{0,1},{1,0},{2,3},{3,2},{4,5},{5,4},{6,7},{7,6},{8,9},{9,8},{10,11... | collective-permute-start | bytes 245768 | tf_op jit(solution)/shard_map/ppermute | solution.py:729
  95.2 8.9 %collective-permute-start.23 = (bf16[960,128]{1,0:T(8,128)(2,1)S(1)}, bf16[960,128]{1,0:T(8,128)(2,1)S(1)}, u32[]{:S(2)}, u32[]{:S(2)}) collective-permute-start(bf16[960,128]{1,0:T(8,128)(2,1)S(1)} %get-tuple-element.171), channel_id=1, source_target_pairs={{0,2},{1,3},{2,0},{3,1},{4,6},{5,7},{6,4},{7,5},{8,10},{9,11},{10,... | collective-permute-start | bytes 737288 | tf_op jit(solution)/shard_map/ppermute | solution.py:729
  95.7 8.5 %collective-permute-start.24 = (bf16[960,128]{1,0:T(8,128)(2,1)S(1)}, bf16[960,128]{1,0:T(8,128)(2,1)S(1)}, u32[]{:S(2)}, u32[]{:S(2)}) collective-permute-start(bf16[960,128]{1,0:T(8,128)(2,1)S(1)} %get-tuple-element.172), channel_id=1, source_target_pairs={{0,4},{1,5},{2,6},{3,7},{4,0},{5,1},{6,2},{7,3},{8,12},{9,13},{10,... | collective-permute-start | bytes 737288 | tf_op jit(solution)/shard_map/ppermute | solution.py:729
  97.2 11.5 %collective-permute-start.25 = (bf16[960,128]{1,0:T(8,128)(2,1)S(1)}, bf16[960,128]{1,0:T(8,128)(2,1)S(1)}, u32[]{:S(2)}, u32[]{:S(2)}) collective-permute-start(bf16[960,128]{1,0:T(8,128)(2,1)S(1)} %get-tuple-element.173), channel_id=1, source_target_pairs={{0,6},{1,7},{2,4},{3,5},{4,2},{5,3},{6,0},{7,1},{8,14},{9,15},{10,... | collective-permute-start | bytes 737288 | tf_op jit(solution)/shard_map/ppermute | solution.py:729
  99.1 14.3 %collective-permute-start.31 = (bf16[320,128]{1,0:T(8,128)(2,1)S(1)}, bf16[320,128]{1,0:T(8,128)(2,1)S(1)}, u32[]{:S(2)}, u32[]{:S(2)}) collective-permute-start(bf16[320,128]{1,0:T(8,128)(2,1)S(1)} %get-tuple-element.202), channel_id=1, source_target_pairs={{0,24},{1,25},{2,26},{3,27},{4,28},{5,29},{6,30},{7,31},{8,16},{9,... | collective-permute-start | bytes 245768 | tf_op jit(solution)/shard_map/ppermute | solution.py:729
  108.9 17.0 %collective-permute-start.26 = (bf16[480,128]{1,0:T(8,128)(2,1)S(1)}, bf16[480,128]{1,0:T(8,128)(2,1)S(1)}, u32[]{:S(2)}, u32[]{:S(2)}) collective-permute-start(bf16[480,128]{1,0:T(8,128)(2,1)S(1)} %get-tuple-element.179), channel_id=1, source_target_pairs={{0,8},{1,9},{2,10},{3,11},{4,12},{5,13},{6,14},{7,15},{8,0},{9,1},... | collective-permute-start | bytes 368648 | tf_op jit(solution)/shard_map/ppermute | solution.py:729
  109.0 17.0 %collective-permute-start.27 = (bf16[480,128]{1,0:T(8,128)(2,1)S(1)}, bf16[480,128]{1,0:T(8,128)(2,1)S(1)}, u32[]{:S(2)}, u32[]{:S(2)}) collective-permute-start(bf16[480,128]{1,0:T(8,128)(2,1)S(1)} %get-tuple-element.180), channel_id=1, source_target_pairs={{0,16},{1,17},{2,18},{3,19},{4,20},{5,21},{6,22},{7,23},{8,24},{9,... | collective-permute-start | bytes 368648 | tf_op jit(solution)/shard_map/ppermute | solution.py:729
  111.8 14.1 %collective-permute-start.28 = (bf16[480,128]{1,0:T(8,128)(2,1)S(1)}, bf16[480,128]{1,0:T(8,128)(2,1)S(1)}, u32[]{:S(2)}, u32[]{:S(2)}) collective-permute-start(bf16[480,128]{1,0:T(8,128)(2,1)S(1)} %concatenate.40), channel_id=1, source_target_pairs={{0,24},{1,25},{2,26},{3,27},{4,28},{5,29},{6,30},{7,31},{8,16},{9,... | collective-permute-start | bytes 368648 | tf_op jit(solution)/shard_map/ppermute | solution.py:729
  113.4 12.6 %collective-permute-start.30 = (bf16[320,128]{1,0:T(8,128)(2,1)S(1)}, bf16[320,128]{1,0:T(8,128)(2,1)S(1)}, u32[]{:S(2)}, u32[]{:S(2)}) collective-permute-start(bf16[320,128]{1,0:T(8,128)(2,1)S(1)} %get-tuple-element.203), channel_id=1, source_target_pairs={{0,16},{1,17},{2,18},{3,19},{4,20},{5,21},{6,22},{7,23},{8,24},{9,... | collective-permute-start | bytes 245768 | tf_op jit(solution)/shard_map/ppermute | solution.py:729
  113.4 12.6 %collective-permute-start.29 = (bf16[320,128]{1,0:T(8,128)(2,1)S(1)}, bf16[320,128]{1,0:T(8,128)(2,1)S(1)}, u32[]{:S(2)}, u32[]{:S(2)}) collective-permute-start(bf16[320,128]{1,0:T(8,128)(2,1)S(1)} %get-tuple-element.204), channel_id=1, source_target_pairs={{0,8},{1,9},{2,10},{3,11},{4,12},{5,13},{6,14},{7,15},{8,0},{9,1},... | collective-permute-start | bytes 245768 | tf_op jit(solution)/shard_map/ppermute | solution.py:729
  (15 other events, 226.6 us)

commit v2 on v1

--- a/solution.py
+++ b/solution.py
@@ -70,6 +70,10 @@
 
 def flat_rows(entries, count, rows):
     return max((entries * j) // TILE * 8 + rows for j in range(count))
+
+
+def in_hbm(value):
+    return pltpu.with_memory_space_constraint(value, pltpu.HBM)
 
 
 def params(mebibytes):
@@ -142,18 +146,18 @@
     alone = entries // TILE * 8
     edges = [(0, 8), (alone, rows)] if alone > 8 else [(0, rows)]
     for add in (False, True):
-        for ref, numbers in arrays:
+        for ref, (numbers, first) in arrays:
             for t, number in enumerate(numbers):
-                start = tile_row(entries, number ^ me)
+                start, piece = tile_row(entries, number ^ me), first + t * rows
                 for low, high in edges:
                     at = pl.ds(pl.multiple_of(start + low, 8), high - low)
                     if add:
-                        flat[at, :] += ref[t * rows + low : t * rows + high, :].astype(F32)
+                        flat[at, :] += ref[piece + low : piece + high, :].astype(F32)
                     else:
                         flat[at, :] = jnp.zeros((high - low, LANES), F32)
                 if add and alone > 8:
                     at = pl.ds(pl.multiple_of(start + 8, 8), alone - 8)
-                    flat[at, :] = ref[t * rows + 8 : t * rows + alone, :].astype(F32)
+                    flat[at, :] = ref[piece + 8 : piece + alone, :].astype(F32)
 
 
 def read_matrix(flat, row, depth, cols, target):
@@ -205,12 +209,13 @@
 def project_kernel(entries, attn_plan, pos_plan, attn_rows, mlp_rows, me, pos_names, onehot, tokens, *refs):
     attn_arrays = [(refs[i], plan) for i, plan in enumerate(attn_plan)]
     refs = refs[len(attn_plan) :]
-    embedded, normed_out, qkv, w_qkv, w_out, vectors = refs[:6]
-    flat, pos_flat, pos_table = refs[6:]
+    embedded, normed_out, qkv, w_qkv, w_out, vectors, pieces_out = refs[:7]
+    flat, pos_flat, pos_table = refs[7:]
     slots, rows = tokens.shape[0], embedded.shape[0]
 
     pos_flat[...] = jnp.zeros_like(pos_flat)
     for n, (array, first) in enumerate(pos_plan):
+        pieces_out[n * mlp_rows : (n + 1) * mlp_rows, :] = attn_arrays[array][0][first : first + mlp_rows, :]
         name = pos_names[n]
 
         @pl.when(name >= 0)
@@ -272,6 +277,7 @@
         ((D, 3 * D), BF16),
         ((D, D), BF16),
         ((8, D), F32),
+        ((len(pos_plan) * sizes.mlp_rows, LANES), BF16),
     ]
     scratch = [
         pltpu.VMEM((sizes.attn_flat, LANES), F32),
@@ -690,30 +696,26 @@
     return (update, first_new, second_new)
 
 
-def settle_kernel(scale, plans, count, place, *refs):
-    terms, refs = refs[:count], refs[count:]
-    state, outs = (refs[:3], refs[3:6]), (refs[6:10], refs[10:14])
-
-    def added(plan):
-        return sum(terms[n][first : first + rows, :].astype(F32) for n, first, rows in plan)
-
-    other = added(plans[1]) + jnp.where(place[4] > 0, added(plans[2]), 0.0)
-    for n, value in enumerate((added(plans[0]), other)):
-        rows = value.shape[0]
-        gradient = take_share(value, place[2 * n], place[2 * n + 1]) * scale
-        weights, first, second = (tall(ref, rows) for ref in state[n])
-        for ref, result in zip(outs[n], (gradient, *adamw_step(gradient, weights, first, second))):
-            put_flat(ref, result)
-
-
-def settle(scale, place, terms, plans, attn_state, mlp_state):
-    operands = list(terms) + list(attn_state) + list(mlp_state)
-    shapes = [attn_state[0].shape] * 4 + [mlp_state[0].shape] * 4
+def settle_kernel(scale, plan, late_plan, count, place, *refs):
+    terms, state, outs = refs[:count], refs[count : count + 3], refs[count + 3 :]
+    value = sum(terms[n][first : first + rows, :].astype(F32) for n, first, rows in plan)
+    rows = value.shape[0]
+    if late_plan:
+        late = jnp.concatenate([terms[n][first : first + r, :] for n, first, r in late_plan], axis=0)
+        value = value + jnp.where(place[2] > 0, late.astype(F32), 0.0)
+    gradient = take_share(value, place[0], place[1]) * scale
+    weights, first, second = (tall(ref, rows) for ref in state)
+    for ref, result in zip(outs, (gradient, *adamw_step(gradient, weights, first, second))):
+        put_flat(ref, result)
+
+
+def settle(scale, place, terms, plan, late_plan, state):
+    operands = list(terms) + list(state)
     return pl.pallas_call(
-        functools.partial(settle_kernel, scale, plans, len(terms)),
+        functools.partial(settle_kernel, scale, plan, late_plan, len(terms)),
         in_specs=[SMEM_SPEC] + [VMEM_SPEC] * len(operands),
-        out_specs=[VMEM_SPEC] * len(shapes),
-        out_shape=[jax.ShapeDtypeStruct(shape, F32) for shape in shapes],
+        out_specs=[VMEM_SPEC] * 4,
+        out_shape=[jax.ShapeDtypeStruct(state[0].shape, F32)] * 4,
         compiler_params=params(8),
         name="settle",
     )(place, *operands)
@@ -741,9 +743,9 @@
     return [value] + [swap(value, bits) for bits in PLANE]
 
 
-def numbered(arrays):
+def numbered(arrays, along_z, first=0):
     offsets = [core | bits for core in (0, BIT_CORE) for bits in (0, *PLANE)]
-    return [(a, [offset | z * BIT_Z for z in range(4)]) for a, offset in zip(arrays, offsets)]
+    return [(a, ([offset | z * BIT_Z for z in along_z], first)) for a, offset in zip(arrays, offsets)]
 
 
 def sum_plan():
@@ -792,7 +794,7 @@
 
     def project(self, mask, attn_arrays, pos_plan, pos_names):
         self.mask = mask
-        (self.embedded, self.normed_b, self.qkv, self.w_qkv, self.w_out, self.vectors) = project(
+        (self.embedded, self.normed_b, self.qkv, self.w_qkv, self.w_out, self.vectors, self.passed) = project(
             self.entries, attn_arrays, pos_plan, pos_names, mask, self.onehot, self.tokens, self.sizes
         )
 
@@ -827,9 +829,9 @@
     mlp_all = lax.all_gather(piece[sizes.attn_rows :], AXES, axis=0, tiled=True)
     pos_plan = [(1, j * height) for j in range(sizes.pos_count)]
     pos_names = jnp.arange(sizes.pos_count, dtype=jnp.int32)
-    layer.project(jnp.zeros((1,), jnp.int32), [(attn_all, order), (mlp_all, [])], pos_plan, pos_names)
+    layer.project(jnp.zeros((1,), jnp.int32), [(attn_all, (order, 0)), (mlp_all, ([], 0))], pos_plan, pos_names)
     layer.attend()
-    mlp_sent = layer.feed_forward([(mlp_all, order)], layer.mask, [order])
+    mlp_sent = layer.feed_forward([(mlp_all, (order, 0))], layer.mask, [order])
     layer.attend_back()
     pos_grad, attn_sent = layer.project_back([order])
     mlp_terms = [lax.psum_scatter(mlp_sent[0], AXES, scatter_dimension=0, tiled=True)]
@@ -837,8 +839,8 @@
     pos_sum = jnp.pad(lax.psum(pos_grad, AXES), ((0, height), (0, 0)))
     first_row = jnp.minimum((me * layer.entries[1]) // TILE * 8, sizes.pos_flat)
     pos_terms = [lax.dynamic_slice_in_dim(pos_sum, first_row, height, axis=0)]
-    plans = ([(0, 0, sizes.attn_rows)], [(1, 0, height)], [(2, 0, height)])
-    return (layer.output, layer.in_grad), (attn_terms + mlp_terms + pos_terms, plans)
+    plans = ([(0, 0, sizes.attn_rows)], [(0, 0, height)], [(1, 0, height)])
+    return (layer.output, layer.in_grad), (attn_terms, mlp_terms + pos_terms, plans)
 
 
 def step_by_hand(layer, me, piece):
@@ -847,23 +849,29 @@
     z, plane, core = me // BIT_Z, (me // BIT_X) % 4, me % 2
     plan = sum_plan()
     pieces = spread_z(piece)
-    pieces, layer.onehot = together(pieces, layer.onehot)
+    mask, near_mask = me.reshape(1), (me % BIT_Z).reshape(1)
+    pos_names = jnp.stack([jnp.where(plane == n % 4, core if n < 4 else 1 - core, -1) for n in range(8)])
+    pieces, layer.onehot, layer.places, mask, near_mask, pos_names = together(
+        pieces, layer.onehot, layer.places, mask, near_mask, pos_names
+    )
     table = lax.select_n(z, *[p[small:] for p in pieces])
     attn = spread_xy(jnp.concatenate([p[:small] for p in pieces] + [table], axis=0))
     attn, pieces = together(attn, pieces)
     attn = attn + [swap(a, BIT_CORE) for a in attn]
-    mlp = jnp.concatenate([p[small:] for p in pieces], axis=0)
+    mlp = [lax.select_n(z, *[pieces[k ^ here][small:] for here in range(4)]) for k in (1, 2, 3)]
+    mlp = jnp.concatenate(mlp, axis=0)
     attn, mlp = together(attn, mlp)
     mlp_far = swap(mlp, BIT_CORE)
     mlp = spread_xy(mlp)
     at = 4 * small
     pos_plan = [(n, at) for n in range(8)]
-    pos_names = jnp.stack([jnp.where(plane == n % 4, core if n < 4 else 1 - core, -1) for n in range(8)])
-    layer.project(me.reshape(1), numbered(attn), pos_plan, pos_names)
+    layer.project(mask, numbered(attn, range(4)), pos_plan, pos_names)
     layer.attend()
     mlp, mlp_far, layer.residual = together(mlp, mlp_far, layer.residual)
     mlp = mlp + [mlp_far] + [swap(a, BIT_CORE) for a in mlp[1:]]
-    mlp_sent = layer.feed_forward(numbered(mlp), layer.mask, plan)
+    near = [offset | bits for offset in (0, BIT_CORE) for bits in (0, *PLANE)]
+    arrays = numbered(mlp, (1, 2, 3)) + [(layer.passed, (near, 0))]
+    mlp_sent = layer.feed_forward(arrays, near_mask, plan)
 
     parts = add_core(mlp_sent)
     parts, layer.d_residual = together(parts, layer.d_residual)
@@ -877,21 +885,25 @@
     pos_keep = jnp.where(core == 0, pos_parts[0], pos_parts[1])
     pos_send = jnp.where(core == 0, pos_parts[1], pos_parts[0])
     parts, pos = add_core(attn_sent), total([pos_keep, swap(pos_send, BIT_CORE)])
-    sent = [jnp.concatenate([part, pos], axis=0) for part in parts]
+    share = large // 4
+    sent = [
+        jnp.concatenate([part, lax.dynamic_slice_in_dim(pos, (plane ^ k) * share, share, axis=0)], axis=0)
+        for k, part in enumerate(parts)
+    ]
     sent, mlp_terms = together(sent, mlp_terms)
     came = swap_xy(sent)
     mlp_came = swap_z(quarters(total(mlp_terms)))
     came = together(came)[0]
     whole_sum = total(came)
-    pos = whole_sum[at:]
-    sent = [jnp.concatenate([part, pos], axis=0) for part in quarters(whole_sum[:at])]
-    came = swap_z(together(sent)[0])
+    sent = [jnp.concatenate([part, whole_sum[at:]], axis=0) for part in quarters(whole_sum[:at])]
+    came, mlp_came = together(swap_z(together(sent)[0]), mlp_came)
+    pos = spread_xy(total([value[small:] for value in came]))
     plans = (
         [(n, 0, small) for n in range(4)],
-        [(n, 0, large) for n in range(4, 8)],
-        [(n, small, large) for n in range(4)],
+        [(n, 0, large) for n in range(4)],
+        [(n, 0, share) for n in range(4, 8)],
     )
-    return (layer.output, layer.in_grad), (came + mlp_came, plans)
+    return (layer.output, layer.in_grad), (came, mlp_came + pos, plans)
 
 
 def body(
@@ -932,20 +944,23 @@
         ],
         compiler_params=params(8),
         name="align",
-    )(place, attn_params, mlp_params)
+    )(place, in_hbm(attn_params), in_hbm(mlp_params))
 
     pos_full = jnp.pad(pos_map, (0, rows - slots), constant_values=255)
     onehot = (pos_full[:, None] == jnp.arange(256, dtype=jnp.int32)[None, :]).astype(BF16)
     layer = Layer(entries, sizes, slots, tokens, cotangent, lengths, onehot)
+    layer.places = (place[:2], place[2:])
     if by_hand:
         outputs, terms = step_by_hand(layer, me, piece)
     else:
         outputs, terms = step_by_axes(layer, me, piece)
-        place = place.at[4].set(1)
+        layer.places = (place[:2], place[2:].at[2].set(1))
     scale = 1.0 / math.sqrt(slots * count)
     attn_state, mlp_state = (attn_params, attn_first, attn_second), (mlp_params, mlp_first, mlp_second)
-    updated = settle(scale, place, *terms, attn_state, mlp_state)
-    return (*outputs, *updated)
+    attn_terms, mlp_terms, plans = terms
+    attn_new = settle(scale, layer.places[0], attn_terms, plans[0], (), attn_state)
+    mlp_new = settle(scale, layer.places[1], mlp_terms, plans[1], plans[2], mlp_state)
+    return (*outputs, *attn_new, *mlp_new)
 
 
 def solution(mesh):

time: 128 us -> 119 us (0.930)
  waiting for transfers between devices: 50 us -> 35.9 us
  starting transfers between devices: 32 us -> 37.8 us
  local copies, waits for them, and re-layouts: 3.68 us -> 1.76 us
  Pallas kernels: 39.7 us -> 41.1 us
    ppermute x32 -> x35, waiting for transfers between devices: 50 us -> 35.9 us  [swap(): return lax.ppermute(value, AXES, [(j, j ^ bits) for j in range(DEVICES)])]
    ppermute x32 -> x35, starting transfers between devices: 32 us -> 37.8 us  [swap(): return lax.ppermute(value, AXES, [(j, j ^ bits) for j in range(DEVICES)])]
    unnamed x34 -> x30, local copies, waits for them, and re-layouts: 2.74 us -> 0.84 us
    pallas_call x1 -> x2, Pallas kernels: 1.76 us -> 3.07 us  [settle(): pl.pallas_call(functools.partial(settle_kernel, scale, plan, late_plan, l...]
  transfers between devices with their start and end apart: 32 -> 35, of which waited for: 20 -> 20; matrix products, arithmetic and copies ran while one was open for 1% -> 1% of each run, Pallas kernels for 18% -> 20%
where the time goes in v2:
time: 119 us
  Pallas kernels  41.1 us (35%)
  starting transfers between devices  37.8 us (32%)
  waiting for transfers between devices  35.9 us (30%)
  local copies, waits for them, and re-layouts  1.76 us (1%)
  other arithmetic  1.41 us (1%)
    ppermute x35, starting transfers between devices, swap(): return lax.ppermute(value, AXES, [(j, j ^ bits) for j in range(DEVICES)])  37.8 us
    pallas_call x5, Pallas kernels, call(): pl.pallas_call(kernel, in_specs=[SMEM_SPEC if a.dtype == jnp.int32 and a....  36.3 us
    ppermute x35, waiting for transfers between devices, swap(): return lax.ppermute(value, AXES, [(j, j ^ bits) for j in range(DEVICES)])  35.9 us
    pallas_call x2, Pallas kernels, settle(): pl.pallas_call(functools.partial(settle_kernel, scale, plan, late_plan, l...  3.07 us
  transfers between devices with their start and end apart: 35, of which 20 were waited for; matrix products, arithmetic and copies ran while one was open for 1% of the time, Pallas kernels for 20%

profile of v2, /device:TPU:0, one launch (start us, length us, event | category | flops | bytes accessed | tf_op | source)
XLA Modules:
  0.0 119.1 jit_solution(10481411075600727708)
XLA Ops:
  0.8 1.7 %align.1 = bf16[480,128]{1,0:T(8,128)(2,1)S(1)} custom-call(s32[5]{0:T(128)S(1)} %stack.58.place, f32[18504]{0:T(1024)} %refs_4_.1, f32[38688]{0:T(1024)} %refs_8_.1), custom_call_target="tpu_custom_call" | custom-call | tf_op jit(solution)/shard_map/align/pallas_call | solution.py:935
  2.5 3.1 %collective-permute-start = (bf16[480,128]{1,0:T(8,128)(2,1)S(1)}, bf16[480,128]{1,0:T(8,128)(2,1)S(1)}, u32[]{:S(2)}, u32[]{:S(2)}) collective-permute-start(bf16[480,128]{1,0:T(8,128)(2,1)S(1)} %align.1), channel_id=1, source_target_pairs={{0,8},{1,9},{2,10},{3,11},{4,12},{5,13},{6,14},{7,15},{8,0},{9,1},... | collective-permute-start | bytes 368648 | tf_op jit(solution)/shard_map/ppermute | solution.py:731
  5.6 2.6 %collective-permute-start.1 = (bf16[480,128]{1,0:T(8,128)(2,1)S(1)}, bf16[480,128]{1,0:T(8,128)(2,1)S(1)}, u32[]{:S(2)}, u32[]{:S(2)}) collective-permute-start(bf16[480,128]{1,0:T(8,128)(2,1)S(1)} %align.1), channel_id=1, source_target_pairs={{0,16},{1,17},{2,18},{3,19},{4,20},{5,21},{6,22},{7,23},{8,24},{9,... | collective-permute-start | bytes 368648 | tf_op jit(solution)/shard_map/ppermute | solution.py:731
  10.3 7.7 %collective-permute-done.1 = bf16[480,128]{1,0:T(8,128)(2,1)S(1)} collective-permute-done((bf16[480,128]{1,0:T(8,128)(2,1)S(1)}, bf16[480,128]{1,0:T(8,128)(2,1)S(1)}, u32[]{:S(2)}, u32[]{:S(2)}) %collective-permute-start.1) | collective-permute-done | bytes 122912 | tf_op jit(solution)/shard_map/ppermute | solution.py:731
  18.0 1.6 %collective-permute-start.3 = (bf16[960,128]{1,0:T(8,128)(2,1)S(1)}, bf16[960,128]{1,0:T(8,128)(2,1)S(1)}, u32[]{:S(2)}, u32[]{:S(2)}) collective-permute-start(bf16[960,128]{1,0:T(8,128)(2,1)S(1)} %select_dynamic-update-slice_fusion.refs_0_), channel_id=1, source_target_pairs={{0,2},{1,3},{2,0},{3,1},{4,6},{5,7},{6,4},{7,5},{8,10},{9,11},{10,... | collective-permute-start | bytes 737288 | tf_op jit(solution)/shard_map/ppermute | solution.py:731
  19.6 1.5 %collective-permute-start.4 = (bf16[960,128]{1,0:T(8,128)(2,1)S(1)}, bf16[960,128]{1,0:T(8,128)(2,1)S(1)}, u32[]{:S(2)}, u32[]{:S(2)}) collective-permute-start(bf16[960,128]{1,0:T(8,128)(2,1)S(1)} %select_dynamic-update-slice_fusion.refs_0_), channel_id=1, source_target_pairs={{0,4},{1,5},{2,6},{3,7},{4,0},{5,1},{6,2},{7,3},{8,12},{9,13},{10,... | collective-permute-start | bytes 737288 | tf_op jit(solution)/shard_map/ppermute | solution.py:731
  21.6 4.5 %collective-permute-done.3.refs_1_ = bf16[960,128]{1,0:T(8,128)(2,1)S(1)} collective-permute-done((bf16[960,128]{1,0:T(8,128)(2,1)S(1)}, bf16[960,128]{1,0:T(8,128)(2,1)S(1)}, u32[]{:S(2)}, u32[]{:S(2)}) %collective-permute-start.3) | collective-permute-done | bytes 245792 | tf_op jit(solution)/shard_map/ppermute | solution.py:731
  26.1 3.8 %collective-permute-done.4.refs_2_ = bf16[960,128]{1,0:T(8,128)(2,1)S(1)} collective-permute-done((bf16[960,128]{1,0:T(8,128)(2,1)S(1)}, bf16[960,128]{1,0:T(8,128)(2,1)S(1)}, u32[]{:S(2)}, u32[]{:S(2)}) %collective-permute-start.4) | collective-permute-done | bytes 245792 | tf_op jit(solution)/shard_map/ppermute | solution.py:731
  34.5 1.4 %collective-permute-start.12 = (bf16[960,128]{1,0:T(8,128)(2,1)S(1)}, bf16[960,128]{1,0:T(8,128)(2,1)S(1)}, u32[]{:S(2)}, u32[]{:S(2)}) collective-permute-start(bf16[960,128]{1,0:T(8,128)(2,1)S(1)} %pad_maximum_fusion.refs_0_), channel_id=1, source_target_pairs={{0,6},{1,7},{2,4},{3,5},{4,2},{5,3},{6,0},{7,1},{8,14},{9,15},{10,... | collective-permute-start | bytes 737288 | tf_op jit(solution)/shard_map/ppermute | solution.py:731
  36.0 4.2 %project.1 = (f32[1024,384]{1,0:T(8,128)S(1)}, bf16[1024,384]{1,0:T(8,128)(2,1)S(1)}, f32[9,1112,128]{2,1,0:T(8,128)S(1)}, bf16[384,1152]{1,0:T(8,128)(2,1)S(1)}...) custom-call(s32[1]{0:T(128)} %bitcast.5.me, s32[8]{0:T(128)S(1)} %stack.69.pos_names, ...), custom_call_target="tpu_custom_call" | custom-call | flops 9200000000 | bytes 1024 | tf_op jit(solution)/shard_map/project/pallas_call | solution.py:197
  40.2 5.3 %attend.1 = (f32[3,1112,128]{2,1,0:T(8,128)S(1)}, f32[8,320,128]{2,1,0:T(8,128)S(1)}, f32[1024,384]{1,0:T(8,128)S(1)}) custom-call(s32[12]{0:T(128)S(1)} %copy-done.8, f32[9,1112,128]{2,1,0:T(8,128)S(1)} %get-tuple-element.141.qkv, f32[1024,384]{1,0:T(8,128)S(1)} %get-tuple-element.142.embedded.refs_1_, bf16[384,384]{1,0:T(8,128)(2,1)S(1)} %get-tuple-element.143.w_out, ...), custom_call_target="tpu_custom_call" | custom-call | flops 11500000256 | bytes 1024 | tf_op jit(solution)/shard_map/attend/pallas_call | solution.py:197
  49.0 14.4 %feed_forward.1 = (bf16[984,384]{1,0:T(8,128)(2,1)}, f32[1024,384]{1,0:T(8,128)S(1)}, bf16[5120,128]{1,0:T(8,128)(2,1)S(1)}, bf16[1280,128]{1,0:T(8,128)(2,1)S(1...) custom-call(s32[1]{0:T(128)} %bitcast.6.mask, s32[1]{0:T(128)} %bitcast.5.me, ...), custom_call_target="tpu_custom_call" | custom-call | flops 20700000256 | bytes 1024 | tf_op jit(solution)/shard_map/feed_forward/pallas_call | solution.py:197
  63.6 2.9 %collective-permute-done.17 = bf16[5120,128]{1,0:T(8,128)(2,1)S(1)} collective-permute-done((bf16[5120,128]{1,0:T(8,128)(2,1)S(1)}, bf16[5120,128]{1,0:T(8,128)(2,1)S(1)}, u32[]{:S(2)}, u32[]{:S(2)}) %collective-permute-start.17) | collective-permute-done | bytes 1310752 | tf_op jit(solution)/shard_map/ppermute | solution.py:731
  66.8 2.0 %collective-permute-start.18 = (bf16[1280,128]{1,0:T(8,128)(2,1)S(1)}, bf16[1280,128]{1,0:T(8,128)(2,1)S(1)}, u32[]{:S(2)}, u32[]{:S(2)}) collective-permute-start(bf16[1280,128]{1,0:T(8,128)(2,1)S(1)} %get-tuple-element.170), channel_id=1, source_target_pairs={{0,2},{1,3},{2,0},{3,1},{4,6},{5,7},{6,4},{7,5},{8,10},{9,11},{10,... | collective-permute-start | bytes 983048 | tf_op jit(solution)/shard_map/ppermute | solution.py:731
  69.2 1.4 %collective-permute-start.20 = (bf16[1280,128]{1,0:T(8,128)(2,1)S(1)}, bf16[1280,128]{1,0:T(8,128)(2,1)S(1)}, u32[]{:S(2)}, u32[]{:S(2)}) collective-permute-start(bf16[1280,128]{1,0:T(8,128)(2,1)S(1)} %get-tuple-element.172), channel_id=1, source_target_pairs={{0,6},{1,7},{2,4},{3,5},{4,2},{5,3},{6,0},{7,1},{8,14},{9,15},{10,... | collective-permute-start | bytes 983048 | tf_op jit(solution)/shard_map/ppermute | solution.py:731
  70.6 6.8 %attend_back.1 = (f32[9,1112,128]{2,1,0:T(8,128)S(1)}, bf16[1024,384]{1,0:T(8,128)(2,1)S(1)}) custom-call(s32[12]{0:T(128)S(1)} %copy-done.8, f32[9,1112,128]{2,1,0:T(8,128)S(1)} %get-tuple-element.141.qkv, f32[3,1112,128]{2,1,0:T(8,128)S(1)} %get-tuple-element.155.mixed.refs_3_, f32[8,320,128]{2,1,0:T(8,128)S(1)} %get-tuple-element.156.log_total, ...), custom_call_target="tpu_custom_call" | custom-call | flops 13799999488 | bytes 1024 | tf_op jit(solution)/shard_map/attend_back/pallas_call | solution.py:197
  77.3 5.6 %project_back.1 = (bf16[984,384]{1,0:T(8,128)(2,1)}, bf16[624,128]{1,0:T(8,128)(2,1)S(1)}, bf16[2560,128]{1,0:T(8,128)(2,1)S(1)}, bf16[640,128]{1,0:T(8,128)(2,1...) custom-call(s32[1]{0:T(128)} %bitcast.5.me, ...), custom_call_target="tpu_custom_call" | custom-call | flops 11500000256 | bytes 1024 | tf_op jit(solution)/shard_map/project_back/pallas_call | solution.py:197
  83.7 1.8 %collective-permute-done.20 = bf16[1280,128]{1,0:T(8,128)(2,1)S(1)} collective-permute-done((bf16[1280,128]{1,0:T(8,128)(2,1)S(1)}, bf16[1280,128]{1,0:T(8,128)(2,1)S(1)}, u32[]{:S(2)}, u32[]{:S(2)}) %collective-permute-start.20) | collective-permute-done | bytes 327712 | tf_op jit(solution)/shard_map/ppermute | solution.py:731
  86.8 1.6 %collective-permute-done.22 = bf16[320,128]{1,0:T(8,128)(2,1)S(1)} collective-permute-done((bf16[320,128]{1,0:T(8,128)(2,1)S(1)}, bf16[320,128]{1,0:T(8,128)(2,1)S(1)}, u32[]{:S(2)}, u32[]{:S(2)}) %collective-permute-start.22) | collective-permute-done | bytes 81952 | tf_op jit(solution)/shard_map/ppermute | solution.py:731
  89.6 1.7 %collective-permute-start.24 = (bf16[720,128]{1,0:T(8,128)(2,1)S(1)}, bf16[720,128]{1,0:T(8,128)(2,1)S(1)}, u32[]{:S(2)}, u32[]{:S(2)}) collective-permute-start(bf16[720,128]{1,0:T(8,128)(2,1)S(1)} %get-tuple-element.191), channel_id=1, source_target_pairs={{0,4},{1,5},{2,6},{3,7},{4,0},{5,1},{6,2},{7,3},{8,12},{9,13},{10,... | collective-permute-start | bytes 552968 | tf_op jit(solution)/shard_map/ppermute | solution.py:731
  92.7 1.8 %collective-permute-start.29 = (bf16[320,128]{1,0:T(8,128)(2,1)S(1)}, bf16[320,128]{1,0:T(8,128)(2,1)S(1)}, u32[]{:S(2)}, u32[]{:S(2)}) collective-permute-start(bf16[320,128]{1,0:T(8,128)(2,1)S(1)} %get-tuple-element.235), channel_id=1, source_target_pairs={{0,8},{1,9},{2,10},{3,11},{4,12},{5,13},{6,14},{7,15},{8,0},{9,1},... | collective-permute-start | bytes 245768 | tf_op jit(solution)/shard_map/ppermute | solution.py:731
  94.5 2.3 %collective-permute-start.30 = (bf16[320,128]{1,0:T(8,128)(2,1)S(1)}, bf16[320,128]{1,0:T(8,128)(2,1)S(1)}, u32[]{:S(2)}, u32[]{:S(2)}) collective-permute-start(bf16[320,128]{1,0:T(8,128)(2,1)S(1)} %get-tuple-element.234), channel_id=1, source_target_pairs={{0,16},{1,17},{2,18},{3,19},{4,20},{5,21},{6,22},{7,23},{8,24},{9,... | collective-permute-start | bytes 245768 | tf_op jit(solution)/shard_map/ppermute | solution.py:731
  96.8 1.8 %collective-permute-start.31 = (bf16[320,128]{1,0:T(8,128)(2,1)S(1)}, bf16[320,128]{1,0:T(8,128)(2,1)S(1)}, u32[]{:S(2)}, u32[]{:S(2)}) collective-permute-start(bf16[320,128]{1,0:T(8,128)(2,1)S(1)} %get-tuple-element.233), channel_id=1, source_target_pairs={{0,24},{1,25},{2,26},{3,27},{4,28},{5,29},{6,30},{7,31},{8,16},{9,... | collective-permute-start | bytes 245768 | tf_op jit(solution)/shard_map/ppermute | solution.py:731
  100.1 2.8 %collective-permute-start.26 = (bf16[240,128]{1,0:T(8,128)(2,1)S(1)}, bf16[240,128]{1,0:T(8,128)(2,1)S(1)}, u32[]{:S(2)}, u32[]{:S(2)}) collective-permute-start(bf16[240,128]{1,0:T(8,128)(2,1)S(1)} %get-tuple-element.198), channel_id=1, source_target_pairs={{0,8},{1,9},{2,10},{3,11},{4,12},{5,13},{6,14},{7,15},{8,0},{9,1},... | collective-permute-start | bytes 184328 | tf_op jit(solution)/shard_map/ppermute | solution.py:731
  102.9 1.9 %collective-permute-start.27 = (bf16[240,128]{1,0:T(8,128)(2,1)S(1)}, bf16[240,128]{1,0:T(8,128)(2,1)S(1)}, u32[]{:S(2)}, u32[]{:S(2)}) collective-permute-start(bf16[240,128]{1,0:T(8,128)(2,1)S(1)} %get-tuple-element.199), channel_id=1, source_target_pairs={{0,16},{1,17},{2,18},{3,19},{4,20},{5,21},{6,22},{7,23},{8,24},{9,... | collective-permute-start | bytes 184328 | tf_op jit(solution)/shard_map/ppermute | solution.py:731
  104.8 1.4 %collective-permute-start.28 = (bf16[240,128]{1,0:T(8,128)(2,1)S(1)}, bf16[240,128]{1,0:T(8,128)(2,1)S(1)}, u32[]{:S(2)}, u32[]{:S(2)}) collective-permute-start(bf16[240,128]{1,0:T(8,128)(2,1)S(1)} %concatenate.42), channel_id=1, source_target_pairs={{0,24},{1,25},{2,26},{3,27},{4,28},{5,29},{6,30},{7,31},{8,16},{9,... | collective-permute-start | bytes 184328 | tf_op jit(solution)/shard_map/ppermute | solution.py:731
  106.2 2.7 %collective-permute-done.27.refs_2_ = bf16[240,128]{1,0:T(8,128)(2,1)S(1)} collective-permute-done((bf16[240,128]{1,0:T(8,128)(2,1)S(1)}, bf16[240,128]{1,0:T(8,128)(2,1)S(1)}, u32[]{:S(2)}, u32[]{:S(2)}) %collective-permute-start.27) | collective-permute-done | bytes 61472 | tf_op jit(solution)/shard_map/ppermute | solution.py:731
  108.8 2.1 %collective-permute-done.28.refs_3_ = bf16[240,128]{1,0:T(8,128)(2,1)S(1)} collective-permute-done((bf16[240,128]{1,0:T(8,128)(2,1)S(1)}, bf16[240,128]{1,0:T(8,128)(2,1)S(1)}, u32[]{:S(2)}, u32[]{:S(2)}) %collective-permute-start.28) | collective-permute-done | bytes 61472 | tf_op jit(solution)/shard_map/ppermute | solution.py:731
  112.7 1.7 %collective-permute-start.34 = (bf16[80,128]{1,0:T(8,128)(2,1)S(1)}, bf16[80,128]{1,0:T(8,128)(2,1)S(1)}, u32[]{:S(2)}, u32[]{:S(2)}) collective-permute-start(bf16[80,128]{1,0:T(8,128)(2,1)S(1)} %add_convert_fusion.11.refs_4_), channel_id=1, source_target_pairs={{0,6},{1,7},{2,4},{3,5},{4,2},{5,3},{6,0},{7,1},{8,14},{9,15},{10,... | collective-permute-start | bytes 61448 | tf_op jit(solution)/shard_map/ppermute | solution.py:731
  114.5 1.4 %settle.2 = (f32[18504]{0:T(1024)}, f32[18504]{0:T(1024)}, f32[18504]{0:T(1024)}, f32[18504]{0:T(1024)}) custom-call(s32[2]{0:T(128)S(1)} %pad_add_fusion.place, bf16[240,128]{1,0:T(8,128)(2,1)S(1)} %get-tuple-element.205.refs_0_, bf16[240,128]{1,0:T(8,128)(2,1)S(1)} %collective-permute-done.26.refs_1_, ...), custom_call_target="tpu_custom_call" | custom-call | tf_op jit(solution)/shard_map/settle/pallas_call | solution.py:714
  115.9 1.5 %collective-permute-done.34.refs_7_ = bf16[80,128]{1,0:T(8,128)(2,1)S(1)} collective-permute-done((bf16[80,128]{1,0:T(8,128)(2,1)S(1)}, bf16[80,128]{1,0:T(8,128)(2,1)S(1)}, u32[]{:S(2)}, u32[]{:S(2)}) %collective-permute-start.34) | collective-permute-done | bytes 20512 | tf_op jit(solution)/shard_map/ppermute | solution.py:731
  117.4 1.7 %settle.3 = (f32[38688]{0:T(1024)}, f32[38688]{0:T(1024)}, f32[38688]{0:T(1024)}, f32[38688]{0:T(1024)}) custom-call(s32[3]{0:T(128)S(1)} %pad_add_fusion.1.place, bf16[320,128]{1,0:T(8,128)(2,1)S(1)} %get-tuple-element.214.refs_0_, bf16[320,128]{1,0:T(8,128)(2,1)S(1)} %collective-permute-done.29.refs_1_, ...), custom_call_target="tpu_custom_call" | custom-call | tf_op jit(solution)/shard_map/settle/pallas_call | solution.py:714
  (100 shorter events, 19.4 us)
Async XLA Ops:
  2.5 7.7 %collective-permute-start = (bf16[480,128]{1,0:T(8,128)(2,1)S(1)}, bf16[480,128]{1,0:T(8,128)(2,1)S(1)}, u32[]{:S(2)}, u32[]{:S(2)}) collective-permute-start(bf16[480,128]{1,0:T(8,128)(2,1)S(1)} %align.1), channel_id=1, source_target_pairs={{0,8},{1,9},{2,10},{3,11},{4,12},{5,13},{6,14},{7,15},{8,0},{9,1},... | collective-permute-start | bytes 368648 | tf_op jit(solution)/shard_map/ppermute | solution.py:731
  5.6 12.3 %collective-permute-start.1 = (bf16[480,128]{1,0:T(8,128)(2,1)S(1)}, bf16[480,128]{1,0:T(8,128)(2,1)S(1)}, u32[]{:S(2)}, u32[]{:S(2)}) collective-permute-start(bf16[480,128]{1,0:T(8,128)(2,1)S(1)} %align.1), channel_id=1, source_target_pairs={{0,16},{1,17},{2,18},{3,19},{4,20},{5,21},{6,22},{7,23},{8,24},{9,... | collective-permute-start | bytes 368648 | tf_op jit(solution)/shard_map/ppermute | solution.py:731
  8.2 9.7 %collective-permute-start.2 = (bf16[480,128]{1,0:T(8,128)(2,1)S(1)}, bf16[480,128]{1,0:T(8,128)(2,1)S(1)}, u32[]{:S(2)}, u32[]{:S(2)}) collective-permute-start(bf16[480,128]{1,0:T(8,128)(2,1)S(1)} %align.1), channel_id=1, source_target_pairs={{0,24},{1,25},{2,26},{3,27},{4,28},{5,29},{6,30},{7,31},{8,16},{9,... | collective-permute-start | bytes 368648 | tf_op jit(solution)/shard_map/ppermute | solution.py:731
  18.0 8.0 %collective-permute-start.3 = (bf16[960,128]{1,0:T(8,128)(2,1)S(1)}, bf16[960,128]{1,0:T(8,128)(2,1)S(1)}, u32[]{:S(2)}, u32[]{:S(2)}) collective-permute-start(bf16[960,128]{1,0:T(8,128)(2,1)S(1)} %select_dynamic-update-slice_fusion.refs_0_), channel_id=1, source_target_pairs={{0,2},{1,3},{2,0},{3,1},{4,6},{5,7},{6,4},{7,5},{8,10},{9,11},{10,... | collective-permute-start | bytes 737288 | tf_op jit(solution)/shard_map/ppermute | solution.py:731
  19.6 10.3 %collective-permute-start.4 = (bf16[960,128]{1,0:T(8,128)(2,1)S(1)}, bf16[960,128]{1,0:T(8,128)(2,1)S(1)}, u32[]{:S(2)}, u32[]{:S(2)}) collective-permute-start(bf16[960,128]{1,0:T(8,128)(2,1)S(1)} %select_dynamic-update-slice_fusion.refs_0_), channel_id=1, source_target_pairs={{0,4},{1,5},{2,6},{3,7},{4,0},{5,1},{6,2},{7,3},{8,12},{9,13},{10,... | collective-permute-start | bytes 737288 | tf_op jit(solution)/shard_map/ppermute | solution.py:731
  21.1 8.8 %collective-permute-start.5 = (bf16[960,128]{1,0:T(8,128)(2,1)S(1)}, bf16[960,128]{1,0:T(8,128)(2,1)S(1)}, u32[]{:S(2)}, u32[]{:S(2)}) collective-permute-start(bf16[960,128]{1,0:T(8,128)(2,1)S(1)} %select_dynamic-update-slice_fusion.refs_0_), channel_id=1, source_target_pairs={{0,6},{1,7},{2,4},{3,5},{4,2},{5,3},{6,0},{7,1},{8,14},{9,15},{10,... | collective-permute-start | bytes 737288 | tf_op jit(solution)/shard_map/ppermute | solution.py:731
  29.9 1.9 %collective-permute-start.7 = (bf16[960,128]{1,0:T(8,128)(2,1)S(1)}, bf16[960,128]{1,0:T(8,128)(2,1)S(1)}, u32[]{:S(2)}, u32[]{:S(2)}) collective-permute-start(bf16[960,128]{1,0:T(8,128)(2,1)S(1)} %collective-permute-done.3.refs_1_), channel_id=1, source_target_pairs={{0,1},{1,0},{2,3},{3,2},{4,5},{5,4},{6,7},{7,6},{8,9},{9,8},{10,11... | collective-permute-start | bytes 737288 | tf_op jit(solution)/shard_map/ppermute | solution.py:731
  30.4 2.1 %collective-permute-start.9 = (bf16[960,128]{1,0:T(8,128)(2,1)S(1)}, bf16[960,128]{1,0:T(8,128)(2,1)S(1)}, u32[]{:S(2)}, u32[]{:S(2)}) collective-permute-start(bf16[960,128]{1,0:T(8,128)(2,1)S(1)} %collective-permute-done.5.refs_3_), channel_id=1, source_target_pairs={{0,1},{1,0},{2,3},{3,2},{4,5},{5,4},{6,7},{7,6},{8,9},{9,8},{10,11... | collective-permute-start | bytes 737288 | tf_op jit(solution)/shard_map/ppermute | solution.py:731
  32.5 13.0 %collective-permute-start.10 = (bf16[960,128]{1,0:T(8,128)(2,1)S(1)}, bf16[960,128]{1,0:T(8,128)(2,1)S(1)}, u32[]{:S(2)}, u32[]{:S(2)}) collective-permute-start(bf16[960,128]{1,0:T(8,128)(2,1)S(1)} %pad_maximum_fusion.refs_0_), channel_id=1, source_target_pairs={{0,2},{1,3},{2,0},{3,1},{4,6},{5,7},{6,4},{7,5},{8,10},{9,11},{10,... | collective-permute-start | bytes 737288 | tf_op jit(solution)/shard_map/ppermute | solution.py:731
  33.7 11.7 %collective-permute-start.11 = (bf16[960,128]{1,0:T(8,128)(2,1)S(1)}, bf16[960,128]{1,0:T(8,128)(2,1)S(1)}, u32[]{:S(2)}, u32[]{:S(2)}) collective-permute-start(bf16[960,128]{1,0:T(8,128)(2,1)S(1)} %pad_maximum_fusion.refs_0_), channel_id=1, source_target_pairs={{0,4},{1,5},{2,6},{3,7},{4,0},{5,1},{6,2},{7,3},{8,12},{9,13},{10,... | collective-permute-start | bytes 737288 | tf_op jit(solution)/shard_map/ppermute | solution.py:731
  34.5 12.2 %collective-permute-start.12 = (bf16[960,128]{1,0:T(8,128)(2,1)S(1)}, bf16[960,128]{1,0:T(8,128)(2,1)S(1)}, u32[]{:S(2)}, u32[]{:S(2)}) collective-permute-start(bf16[960,128]{1,0:T(8,128)(2,1)S(1)} %pad_maximum_fusion.refs_0_), channel_id=1, source_target_pairs={{0,6},{1,7},{2,4},{3,5},{4,2},{5,3},{6,0},{7,1},{8,14},{9,15},{10,... | collective-permute-start | bytes 737288 | tf_op jit(solution)/shard_map/ppermute | solution.py:731
  36.0 10.8 %collective-permute-start.13 = (bf16[960,128]{1,0:T(8,128)(2,1)S(1)}, bf16[960,128]{1,0:T(8,128)(2,1)S(1)}, u32[]{:S(2)}, u32[]{:S(2)}) collective-permute-start(bf16[960,128]{1,0:T(8,128)(2,1)S(1)} %pad_maximum_fusion.refs_0_), channel_id=1, source_target_pairs={{0,1},{1,0},{2,3},{3,2},{4,5},{5,4},{6,7},{7,6},{8,9},{9,8},{10,11... | collective-permute-start | bytes 737288 | tf_op jit(solution)/shard_map/ppermute | solution.py:731
  46.7 1.9 %collective-permute-start.15 = (bf16[960,128]{1,0:T(8,128)(2,1)S(1)}, bf16[960,128]{1,0:T(8,128)(2,1)S(1)}, u32[]{:S(2)}, u32[]{:S(2)}) collective-permute-start(bf16[960,128]{1,0:T(8,128)(2,1)S(1)} %collective-permute-done.11.refs_2_), channel_id=1, source_target_pairs={{0,1},{1,0},{2,3},{3,2},{4,5},{5,4},{6,7},{7,6},{8,9},{9,8},{10,11... | collective-permute-start | bytes 737288 | tf_op jit(solution)/shard_map/ppermute | solution.py:731
  47.2 1.7 %collective-permute-start.16 = (bf16[960,128]{1,0:T(8,128)(2,1)S(1)}, bf16[960,128]{1,0:T(8,128)(2,1)S(1)}, u32[]{:S(2)}, u32[]{:S(2)}) collective-permute-start(bf16[960,128]{1,0:T(8,128)(2,1)S(1)} %collective-permute-done.12.refs_3_), channel_id=1, source_target_pairs={{0,1},{1,0},{2,3},{3,2},{4,5},{5,4},{6,7},{7,6},{8,9},{9,8},{10,11... | collective-permute-start | bytes 737288 | tf_op jit(solution)/shard_map/ppermute | solution.py:731
  63.4 3.0 %collective-permute-start.17 = (bf16[5120,128]{1,0:T(8,128)(2,1)S(1)}, bf16[5120,128]{1,0:T(8,128)(2,1)S(1)}, u32[]{:S(2)}, u32[]{:S(2)}) collective-permute-start(bf16[5120,128]{1,0:T(8,128)(2,1)S(1)} %get-tuple-element.158), channel_id=1, source_target_pairs={{0,1},{1,0},{2,3},{3,2},{4,5},{5,4},{6,7},{7,6},{8,9},{9,8},{10,11... | collective-permute-start | bytes 3932168 | tf_op jit(solution)/shard_map/ppermute | solution.py:731
  66.8 16.2 %collective-permute-start.18 = (bf16[1280,128]{1,0:T(8,128)(2,1)S(1)}, bf16[1280,128]{1,0:T(8,128)(2,1)S(1)}, u32[]{:S(2)}, u32[]{:S(2)}) collective-permute-start(bf16[1280,128]{1,0:T(8,128)(2,1)S(1)} %get-tuple-element.170), channel_id=1, source_target_pairs={{0,2},{1,3},{2,0},{3,1},{4,6},{5,7},{6,4},{7,5},{8,10},{9,11},{10,... | collective-permute-start | bytes 983048 | tf_op jit(solution)/shard_map/ppermute | solution.py:731
  68.8 14.9 %collective-permute-start.19 = (bf16[1280,128]{1,0:T(8,128)(2,1)S(1)}, bf16[1280,128]{1,0:T(8,128)(2,1)S(1)}, u32[]{:S(2)}, u32[]{:S(2)}) collective-permute-start(bf16[1280,128]{1,0:T(8,128)(2,1)S(1)} %get-tuple-element.171), channel_id=1, source_target_pairs={{0,4},{1,5},{2,6},{3,7},{4,0},{5,1},{6,2},{7,3},{8,12},{9,13},{10,... | collective-permute-start | bytes 983048 | tf_op jit(solution)/shard_map/ppermute | solution.py:731
  69.2 16.3 %collective-permute-start.20 = (bf16[1280,128]{1,0:T(8,128)(2,1)S(1)}, bf16[1280,128]{1,0:T(8,128)(2,1)S(1)}, u32[]{:S(2)}, u32[]{:S(2)}) collective-permute-start(bf16[1280,128]{1,0:T(8,128)(2,1)S(1)} %get-tuple-element.172), channel_id=1, source_target_pairs={{0,6},{1,7},{2,4},{3,5},{4,2},{5,3},{6,0},{7,1},{8,14},{9,15},{10,... | collective-permute-start | bytes 983048 | tf_op jit(solution)/shard_map/ppermute | solution.py:731
  86.2 2.3 %collective-permute-start.21 = (bf16[2560,128]{1,0:T(8,128)(2,1)S(1)}, bf16[2560,128]{1,0:T(8,128)(2,1)S(1)}, u32[]{:S(2)}, u32[]{:S(2)}) collective-permute-start(bf16[2560,128]{1,0:T(8,128)(2,1)S(1)} %get-tuple-element.180), channel_id=1, source_target_pairs={{0,1},{1,0},{2,3},{3,2},{4,5},{5,4},{6,7},{7,6},{8,9},{9,8},{10,11... | collective-permute-start | bytes 1966088 | tf_op jit(solution)/shard_map/ppermute | solution.py:731
  86.3 2.2 %collective-permute-start.22 = (bf16[320,128]{1,0:T(8,128)(2,1)S(1)}, bf16[320,128]{1,0:T(8,128)(2,1)S(1)}, u32[]{:S(2)}, u32[]{:S(2)}) collective-permute-start(bf16[320,128]{1,0:T(8,128)(2,1)S(1)} %broadcast_select_fusion), channel_id=1, source_target_pairs={{0,1},{1,0},{2,3},{3,2},{4,5},{5,4},{6,7},{7,6},{8,9},{9,8},{10,11... | collective-permute-start | bytes 245768 | tf_op jit(solution)/shard_map/ppermute | solution.py:731
  88.8 8.0 %collective-permute-start.23 = (bf16[720,128]{1,0:T(8,128)(2,1)S(1)}, bf16[720,128]{1,0:T(8,128)(2,1)S(1)}, u32[]{:S(2)}, u32[]{:S(2)}) collective-permute-start(bf16[720,128]{1,0:T(8,128)(2,1)S(1)} %get-tuple-element.190), channel_id=1, source_target_pairs={{0,2},{1,3},{2,0},{3,1},{4,6},{5,7},{6,4},{7,5},{8,10},{9,11},{10,... | collective-permute-start | bytes 552968 | tf_op jit(solution)/shard_map/ppermute | solution.py:731
  89.6 10.3 %collective-permute-start.24 = (bf16[720,128]{1,0:T(8,128)(2,1)S(1)}, bf16[720,128]{1,0:T(8,128)(2,1)S(1)}, u32[]{:S(2)}, u32[]{:S(2)}) collective-permute-start(bf16[720,128]{1,0:T(8,128)(2,1)S(1)} %get-tuple-element.191), channel_id=1, source_target_pairs={{0,4},{1,5},{2,6},{3,7},{4,0},{5,1},{6,2},{7,3},{8,12},{9,13},{10,... | collective-permute-start | bytes 552968 | tf_op jit(solution)/shard_map/ppermute | solution.py:731
  91.3 8.6 %collective-permute-start.25 = (bf16[720,128]{1,0:T(8,128)(2,1)S(1)}, bf16[720,128]{1,0:T(8,128)(2,1)S(1)}, u32[]{:S(2)}, u32[]{:S(2)}) collective-permute-start(bf16[720,128]{1,0:T(8,128)(2,1)S(1)} %get-tuple-element.192), channel_id=1, source_target_pairs={{0,6},{1,7},{2,4},{3,5},{4,2},{5,3},{6,0},{7,1},{8,14},{9,15},{10,... | collective-permute-start | bytes 552968 | tf_op jit(solution)/shard_map/ppermute | solution.py:731
  92.7 12.1 %collective-permute-start.29 = (bf16[320,128]{1,0:T(8,128)(2,1)S(1)}, bf16[320,128]{1,0:T(8,128)(2,1)S(1)}, u32[]{:S(2)}, u32[]{:S(2)}) collective-permute-start(bf16[320,128]{1,0:T(8,128)(2,1)S(1)} %get-tuple-element.235), channel_id=1, source_target_pairs={{0,8},{1,9},{2,10},{3,11},{4,12},{5,13},{6,14},{7,15},{8,0},{9,1},... | collective-permute-start | bytes 245768 | tf_op jit(solution)/shard_map/ppermute | solution.py:731
  94.5 11.7 %collective-permute-start.30 = (bf16[320,128]{1,0:T(8,128)(2,1)S(1)}, bf16[320,128]{1,0:T(8,128)(2,1)S(1)}, u32[]{:S(2)}, u32[]{:S(2)}) collective-permute-start(bf16[320,128]{1,0:T(8,128)(2,1)S(1)} %get-tuple-element.234), channel_id=1, source_target_pairs={{0,16},{1,17},{2,18},{3,19},{4,20},{5,21},{6,22},{7,23},{8,24},{9,... | collective-permute-start | bytes 245768 | tf_op jit(solution)/shard_map/ppermute | solution.py:731
  96.8 9.4 %collective-permute-start.31 = (bf16[320,128]{1,0:T(8,128)(2,1)S(1)}, bf16[320,128]{1,0:T(8,128)(2,1)S(1)}, u32[]{:S(2)}, u32[]{:S(2)}) collective-permute-start(bf16[320,128]{1,0:T(8,128)(2,1)S(1)} %get-tuple-element.233), channel_id=1, source_target_pairs={{0,24},{1,25},{2,26},{3,27},{4,28},{5,29},{6,30},{7,31},{8,16},{9,... | collective-permute-start | bytes 245768 | tf_op jit(solution)/shard_map/ppermute | solution.py:731
  100.1 6.1 %collective-permute-start.26 = (bf16[240,128]{1,0:T(8,128)(2,1)S(1)}, bf16[240,128]{1,0:T(8,128)(2,1)S(1)}, u32[]{:S(2)}, u32[]{:S(2)}) collective-permute-start(bf16[240,128]{1,0:T(8,128)(2,1)S(1)} %get-tuple-element.198), channel_id=1, source_target_pairs={{0,8},{1,9},{2,10},{3,11},{4,12},{5,13},{6,14},{7,15},{8,0},{9,1},... | collective-permute-start | bytes 184328 | tf_op jit(solution)/shard_map/ppermute | solution.py:731
  102.9 5.9 %collective-permute-start.27 = (bf16[240,128]{1,0:T(8,128)(2,1)S(1)}, bf16[240,128]{1,0:T(8,128)(2,1)S(1)}, u32[]{:S(2)}, u32[]{:S(2)}) collective-permute-start(bf16[240,128]{1,0:T(8,128)(2,1)S(1)} %get-tuple-element.199), channel_id=1, source_target_pairs={{0,16},{1,17},{2,18},{3,19},{4,20},{5,21},{6,22},{7,23},{8,24},{9,... | collective-permute-start | bytes 184328 | tf_op jit(solution)/shard_map/ppermute | solution.py:731
  104.8 6.1 %collective-permute-start.28 = (bf16[240,128]{1,0:T(8,128)(2,1)S(1)}, bf16[240,128]{1,0:T(8,128)(2,1)S(1)}, u32[]{:S(2)}, u32[]{:S(2)}) collective-permute-start(bf16[240,128]{1,0:T(8,128)(2,1)S(1)} %concatenate.42), channel_id=1, source_target_pairs={{0,24},{1,25},{2,26},{3,27},{4,28},{5,29},{6,30},{7,31},{8,16},{9,... | collective-permute-start | bytes 184328 | tf_op jit(solution)/shard_map/ppermute | solution.py:731
  110.9 5.0 %collective-permute-start.32 = (bf16[80,128]{1,0:T(8,128)(2,1)S(1)}, bf16[80,128]{1,0:T(8,128)(2,1)S(1)}, u32[]{:S(2)}, u32[]{:S(2)}) collective-permute-start(bf16[80,128]{1,0:T(8,128)(2,1)S(1)} %add_convert_fusion.11.refs_4_), channel_id=1, source_target_pairs={{0,2},{1,3},{2,0},{3,1},{4,6},{5,7},{6,4},{7,5},{8,10},{9,11},{10,... | collective-permute-start | bytes 61448 | tf_op jit(solution)/shard_map/ppermute | solution.py:731
  111.9 4.0 %collective-permute-start.33 = (bf16[80,128]{1,0:T(8,128)(2,1)S(1)}, bf16[80,128]{1,0:T(8,128)(2,1)S(1)}, u32[]{:S(2)}, u32[]{:S(2)}) collective-permute-start(bf16[80,128]{1,0:T(8,128)(2,1)S(1)} %add_convert_fusion.11.refs_4_), channel_id=1, source_target_pairs={{0,4},{1,5},{2,6},{3,7},{4,0},{5,1},{6,2},{7,3},{8,12},{9,13},{10,... | collective-permute-start | bytes 61448 | tf_op jit(solution)/shard_map/ppermute | solution.py:731
  112.7 4.7 %collective-permute-start.34 = (bf16[80,128]{1,0:T(8,128)(2,1)S(1)}, bf16[80,128]{1,0:T(8,128)(2,1)S(1)}, u32[]{:S(2)}, u32[]{:S(2)}) collective-permute-start(bf16[80,128]{1,0:T(8,128)(2,1)S(1)} %add_convert_fusion.11.refs_4_), channel_id=1, source_target_pairs={{0,6},{1,7},{2,4},{3,5},{4,2},{5,3},{6,0},{7,1},{8,14},{9,15},{10,... | collective-permute-start | bytes 61448 | tf_op jit(solution)/shard_map/ppermute | solution.py:731
  (16 other events, 208.3 us)

commit v3 on v2

--- a/solution.py
+++ b/solution.py
@@ -624,11 +624,12 @@
     return call(attend_back_kernel, "attend_back", operands, outs, scratch, 22, 12)
 
 
-def project_back_kernel(entries, out_plan, piece, me, *refs):
+def project_back_kernel(entries, out_plan, piece, mlp_rows, pos_count, me, pos_names, *refs):
     (onehot, embedded, normed_b, mixed, d_qkv, d_branch_b, w_qkv, vectors, d_residual) = refs[:9]
-    in_grad, pos_out = refs[9:11]
-    targets = [(refs[11 + i], plan) for i, plan in enumerate(out_plan)]
-    flat, d_qkv_b, d_embedded_b, mixed_b, sums = refs[11 + len(out_plan) :]
+    in_grad, pos_out = refs[9], refs[10 : 10 + pos_count]
+    refs = refs[10 + pos_count :]
+    targets = [(refs[i], plan) for i, plan in enumerate(out_plan)]
+    flat, d_qkv_b, d_embedded_b, mixed_b, sums = refs[len(out_plan) :]
     rows = embedded.shape[0]
     gain = vectors[0:1, :]
     sums[...] = jnp.zeros_like(sums)
@@ -663,18 +664,22 @@
     write_row(flat, ROW_B_OUT, part[D : D + 1])
     for c in range(D_COLS):
         flat[pl.ds(ROW_W_OUT + c, D, stride=D_COLS), :] = part[0:D, c * LANES : (c + 1) * LANES]
-    pack(flat, entries, piece, me[0], targets)
+    pack(flat, entries[0], piece, me[0], targets)
 
     pos_grad = dot(onehot[...], d_embedded_b[...], TN)
-    flat[ROW_GAIN_TWO : pos_out.shape[0], :] = jnp.zeros((pos_out.shape[0] - ROW_GAIN_TWO, LANES), F32)
+    flat[ROW_GAIN_TWO:, :] = jnp.zeros((flat.shape[0] - ROW_GAIN_TWO, LANES), F32)
     for c in range(D_COLS):
         flat[pl.ds(ROW_POS + c, POS, stride=D_COLS), :] = pos_grad[0:POS, c * LANES : (c + 1) * LANES]
-    pos_out[...] = flat[0 : pos_out.shape[0], :].astype(BF16)
-
-
-def project_back(entries, me, kept, out_rows, out_plan, sizes):
+    for n, ref in enumerate(pos_out):
+        if ref.shape[0] == mlp_rows:
+            ref[...] = flat[pl.ds(tile_row(entries[1], pos_names[n]), mlp_rows), :].astype(BF16)
+        else:
+            ref[...] = flat[0 : ref.shape[0], :].astype(BF16)
+
+
+def project_back(entries, me, pos_names, pos_shapes, kept, out_rows, out_plan, sizes):
     rows = kept[1].shape[0]
-    outs = [((out_rows, D), BF16), ((sizes.pos_flat, LANES), BF16)]
+    outs = [((out_rows, D), BF16)] + [((height, LANES), BF16) for height in pos_shapes]
     outs += [((len(n) * sizes.attn_rows, LANES), BF16) for n in out_plan]
     scratch = [
         pltpu.VMEM((max(sizes.attn_flat, sizes.pos_flat), LANES), F32),
@@ -683,8 +688,10 @@
         pltpu.VMEM((rows, D), BF16),
         pltpu.VMEM((2, 8, D), F32),
     ]
-    kernel = functools.partial(project_back_kernel, entries, out_plan, sizes.attn_rows)
-    return call(kernel, "project_back", [me, *kept], outs, scratch, 25, 10)
+    kernel = functools.partial(
+        project_back_kernel, entries, out_plan, sizes.attn_rows, sizes.mlp_rows, len(pos_shapes)
+    )
+    return call(kernel, "project_back", [me, pos_names, *kept], outs, scratch, 25, 10)
 
 
 def adamw_step(gradient, weights, first, second):
@@ -762,9 +769,34 @@
     return [value[k * value.shape[0] // 4 : (k + 1) * value.shape[0] // 4] for k in range(4)]
 
 
-def add_core(sent):
-    came = quarters(swap(sent[0], BIT_CORE))
-    return [total(both) for both in zip(sent[1:], came)]
+def add_kernel(terms, quarter, plane, *refs):
+    outs = refs[len(refs) - terms[-1] :]
+    rows = outs[0].shape[0] - quarter
+    for n, out in enumerate(outs):
+        value = sum(
+            refs[t][n * rows : (n + 1) * rows, :].astype(F32) for t in range(terms[0])
+        )
+        if terms[1]:
+            value = value + refs[terms[0] + n][...].astype(F32)
+        out[0:rows, :] = value.astype(BF16)
+        if quarter:
+            at = pl.ds(pl.multiple_of((plane[0] ^ n) * quarter, 16), quarter)
+            one, two = refs[terms[0] + terms[1] : terms[0] + terms[1] + 2]
+            out[rows : rows + quarter, :] = (one[at, :].astype(F32) + two[at, :].astype(F32)).astype(BF16)
+
+
+def add_parts(stacked, parts, count, plane, late=()):
+    rows = stacked[0].shape[0] // count
+    quarter = late[0].shape[0] // count if late else 0
+    operands = [*stacked, *parts, *late]
+    return pl.pallas_call(
+        functools.partial(add_kernel, (len(stacked), len(parts), count), quarter),
+        in_specs=[SMEM_SPEC] + [VMEM_SPEC] * len(operands),
+        out_specs=[VMEM_SPEC] * count,
+        out_shape=[jax.ShapeDtypeStruct((rows + quarter, LANES), BF16)] * count,
+        compiler_params=params(8),
+        name="add_parts",
+    )(plane, *operands)
 
 
 def swap_xy(parts):
@@ -814,11 +846,13 @@
             self.lengths, self.qkv, self.mixed, self.log_total, self.w_out, self.d_residual
         )
 
-    def project_back(self, plan):
+    def project_back(self, plan, pos_names, pos_shapes):
         kept = (self.onehot, self.embedded, self.normed_b, self.mixed, self.d_qkv, self.d_branch_b)
         kept += (self.w_qkv, self.vectors, self.d_residual)
-        self.in_grad, pos_grad, *sent = project_back(self.entries[0], self.mask, kept, self.slots, plan, self.sizes)
-        return pos_grad, sent
+        self.in_grad, *sent = project_back(
+            self.entries, self.mask, pos_names, pos_shapes, kept, self.slots, plan, self.sizes
+        )
+        return sent[: len(pos_shapes)], sent[len(pos_shapes) :]
 
 
 def step_by_axes(layer, me, piece):
@@ -833,7 +867,7 @@
     layer.attend()
     mlp_sent = layer.feed_forward([(mlp_all, (order, 0))], layer.mask, [order])
     layer.attend_back()
-    pos_grad, attn_sent = layer.project_back([order])
+    (pos_grad,), attn_sent = layer.project_back([order], pos_names, [sizes.pos_flat])
     mlp_terms = [lax.psum_scatter(mlp_sent[0], AXES, scatter_dimension=0, tiled=True)]
     attn_terms = [lax.psum_scatter(attn_sent[0], AXES, scatter_dimension=0, tiled=True)]
     pos_sum = jnp.pad(lax.psum(pos_grad, AXES), ((0, height), (0, 0)))
@@ -851,8 +885,9 @@
     pieces = spread_z(piece)
     mask, near_mask = me.reshape(1), (me % BIT_Z).reshape(1)
     pos_names = jnp.stack([jnp.where(plane == n % 4, core if n < 4 else 1 - core, -1) for n in range(8)])
-    pieces, layer.onehot, layer.places, mask, near_mask, pos_names = together(
-        pieces, layer.onehot, layer.places, mask, near_mask, pos_names
+    back_names, plane_here = jnp.stack([1 - core, core]), plane.reshape(1)
+    pieces, layer.onehot, layer.places, mask, near_mask, pos_names, back_names, plane_here = together(
+        pieces, layer.onehot, layer.places, mask, near_mask, pos_names, back_names, plane_here
     )
     table = lax.select_n(z, *[p[small:] for p in pieces])
     attn = spread_xy(jnp.concatenate([p[:small] for p in pieces] + [table], axis=0))
@@ -873,26 +908,19 @@
     arrays = numbered(mlp, (1, 2, 3)) + [(layer.passed, (near, 0))]
     mlp_sent = layer.feed_forward(arrays, near_mask, plan)
 
-    parts = add_core(mlp_sent)
+    parts = add_parts([swap(mlp_sent[0], BIT_CORE)], mlp_sent[1:], 4, plane_here)
     parts, layer.d_residual = together(parts, layer.d_residual)
     mlp_terms = swap_xy(parts)
     layer.attend_back()
-    pos_grad, attn_sent = layer.project_back(plan)
-    mlp_terms, pos_grad, attn_sent = together(mlp_terms, pos_grad, attn_sent)
-
-    offset = layer.entries[1] // TILE * 8
-    pos_parts = [pos_grad[:large], pos_grad[offset : offset + large]]
-    pos_keep = jnp.where(core == 0, pos_parts[0], pos_parts[1])
-    pos_send = jnp.where(core == 0, pos_parts[1], pos_parts[0])
-    parts, pos = add_core(attn_sent), total([pos_keep, swap(pos_send, BIT_CORE)])
+    (pos_send, pos_keep), attn_sent = layer.project_back(plan, back_names, [large, large])
+    mlp_terms, pos_send, pos_keep, attn_sent = together(mlp_terms, pos_send, pos_keep, attn_sent)
+
     share = large // 4
-    sent = [
-        jnp.concatenate([part, lax.dynamic_slice_in_dim(pos, (plane ^ k) * share, share, axis=0)], axis=0)
-        for k, part in enumerate(parts)
-    ]
+    pos_terms = [pos_keep, swap(pos_send, BIT_CORE)]
+    sent = add_parts([swap(attn_sent[0], BIT_CORE)], attn_sent[1:], 4, plane_here, pos_terms)
     sent, mlp_terms = together(sent, mlp_terms)
     came = swap_xy(sent)
-    mlp_came = swap_z(quarters(total(mlp_terms)))
+    mlp_came = swap_z(add_parts(mlp_terms, [], 4, plane_here))
     came = together(came)[0]
     whole_sum = total(came)
     sent = [jnp.concatenate([part, whole_sum[at:]], axis=0) for part in quarters(whole_sum[:at])]

time: 119 us -> 118 us (level)
  starting transfers between devices: 37.8 us -> 35.4 us
  waiting for transfers between devices: 35.9 us -> 37.4 us
  Pallas kernels: 41.1 us -> 42.3 us
    ppermute x35, starting transfers between devices: 37.8 us -> 35.4 us  [swap(): return lax.ppermute(value, AXES, [(j, j ^ bits) for j in range(DEVICES)])]
    ppermute x35, waiting for transfers between devices: 35.9 us -> 37.4 us  [swap(): return lax.ppermute(value, AXES, [(j, j ^ bits) for j in range(DEVICES)])]
  transfers between devices with their start and end apart: 35 -> 35, of which waited for: 20 -> 23; matrix products, arithmetic and copies ran while one was open for 1% -> 1% of each run, Pallas kernels for 20% -> 20%
where the time goes in v3:
time: 118 us
  Pallas kernels  42.3 us (36%)
  waiting for transfers between devices  37.4 us (32%)
  starting transfers between devices  35.4 us (30%)
    ppermute x35, waiting for transfers between devices, swap(): return lax.ppermute(value, AXES, [(j, j ^ bits) for j in range(DEVICES)])  37.4 us
    pallas_call x5, Pallas kernels, call(): pl.pallas_call(kernel, in_specs=[SMEM_SPEC if a.dtype == jnp.int32 and a....  36.9 us
    ppermute x35, starting transfers between devices, swap(): return lax.ppermute(value, AXES, [(j, j ^ bits) for j in range(DEVICES)])  35.4 us
    pallas_call x2, Pallas kernels, settle(): pl.pallas_call(functools.partial(settle_kernel, scale, plan, late_plan, l...  3.06 us
  transfers between devices with their start and end apart: 35, of which 23 were waited for; matrix products, arithmetic and copies ran while one was open for 1% of the time, Pallas kernels for 20%

profile of v3, /device:TPU:0, one launch (start us, length us, event | category | flops | bytes accessed | tf_op | source)
XLA Modules:
  0.0 117.7 jit_solution(17977174851390180339)
XLA Ops:
  0.8 1.7 %align.1 = bf16[480,128]{1,0:T(8,128)(2,1)S(1)} custom-call(s32[5]{0:T(128)S(1)} %stack.67.place, f32[18504]{0:T(1024)} %refs_4_.1, f32[38688]{0:T(1024)} %refs_8_.1), custom_call_target="tpu_custom_call" | custom-call | tf_op jit(solution)/shard_map/align/pallas_call | solution.py:963
  2.5 5.1 %collective-permute-start.2 = (bf16[480,128]{1,0:T(8,128)(2,1)S(1)}, bf16[480,128]{1,0:T(8,128)(2,1)S(1)}, u32[]{:S(2)}, u32[]{:S(2)}) collective-permute-start(bf16[480,128]{1,0:T(8,128)(2,1)S(1)} %align.1), channel_id=1, source_target_pairs={{0,24},{1,25},{2,26},{3,27},{4,28},{5,29},{6,30},{7,31},{8,16},{9,... | collective-permute-start | bytes 368648 | tf_op jit(solution)/shard_map/ppermute | solution.py:738
  9.5 2.4 %collective-permute-done.2 = bf16[480,128]{1,0:T(8,128)(2,1)S(1)} collective-permute-done((bf16[480,128]{1,0:T(8,128)(2,1)S(1)}, bf16[480,128]{1,0:T(8,128)(2,1)S(1)}, u32[]{:S(2)}, u32[]{:S(2)}) %collective-permute-start.2) | collective-permute-done | bytes 122912 | tf_op jit(solution)/shard_map/ppermute | solution.py:738
  11.9 6.1 %collective-permute-done.1 = bf16[480,128]{1,0:T(8,128)(2,1)S(1)} collective-permute-done((bf16[480,128]{1,0:T(8,128)(2,1)S(1)}, bf16[480,128]{1,0:T(8,128)(2,1)S(1)}, u32[]{:S(2)}, u32[]{:S(2)}) %collective-permute-start.1) | collective-permute-done | bytes 122912 | tf_op jit(solution)/shard_map/ppermute | solution.py:738
  18.1 2.5 %collective-permute-start.5 = (bf16[960,128]{1,0:T(8,128)(2,1)S(1)}, bf16[960,128]{1,0:T(8,128)(2,1)S(1)}, u32[]{:S(2)}, u32[]{:S(2)}) collective-permute-start(bf16[960,128]{1,0:T(8,128)(2,1)S(1)} %select_dynamic-update-slice_fusion.refs_0_), channel_id=1, source_target_pairs={{0,6},{1,7},{2,4},{3,5},{4,2},{5,3},{6,0},{7,1},{8,14},{9,15},{10,... | collective-permute-start | bytes 737288 | tf_op jit(solution)/shard_map/ppermute | solution.py:738
  21.7 6.3 %collective-permute-done.5.refs_3_ = bf16[960,128]{1,0:T(8,128)(2,1)S(1)} collective-permute-done((bf16[960,128]{1,0:T(8,128)(2,1)S(1)}, bf16[960,128]{1,0:T(8,128)(2,1)S(1)}, u32[]{:S(2)}, u32[]{:S(2)}) %collective-permute-start.5) | collective-permute-done | bytes 245792 | tf_op jit(solution)/shard_map/ppermute | solution.py:738
  28.0 3.3 %collective-permute-done.4.refs_2_ = bf16[960,128]{1,0:T(8,128)(2,1)S(1)} collective-permute-done((bf16[960,128]{1,0:T(8,128)(2,1)S(1)}, bf16[960,128]{1,0:T(8,128)(2,1)S(1)}, u32[]{:S(2)}, u32[]{:S(2)}) %collective-permute-start.4) | collective-permute-done | bytes 245792 | tf_op jit(solution)/shard_map/ppermute | solution.py:738
  34.2 1.7 %collective-permute-start.12 = (bf16[960,128]{1,0:T(8,128)(2,1)S(1)}, bf16[960,128]{1,0:T(8,128)(2,1)S(1)}, u32[]{:S(2)}, u32[]{:S(2)}) collective-permute-start(bf16[960,128]{1,0:T(8,128)(2,1)S(1)} %pad_maximum_fusion.refs_0_), channel_id=1, source_target_pairs={{0,6},{1,7},{2,4},{3,5},{4,2},{5,3},{6,0},{7,1},{8,14},{9,15},{10,... | collective-permute-start | bytes 737288 | tf_op jit(solution)/shard_map/ppermute | solution.py:738
  35.8 1.3 %collective-permute-start.11 = (bf16[960,128]{1,0:T(8,128)(2,1)S(1)}, bf16[960,128]{1,0:T(8,128)(2,1)S(1)}, u32[]{:S(2)}, u32[]{:S(2)}) collective-permute-start(bf16[960,128]{1,0:T(8,128)(2,1)S(1)} %pad_maximum_fusion.refs_0_), channel_id=1, source_target_pairs={{0,4},{1,5},{2,6},{3,7},{4,0},{5,1},{6,2},{7,3},{8,12},{9,13},{10,... | collective-permute-start | bytes 737288 | tf_op jit(solution)/shard_map/ppermute | solution.py:738
  37.7 4.2 %project.1 = (f32[1024,384]{1,0:T(8,128)S(1)}, bf16[1024,384]{1,0:T(8,128)(2,1)S(1)}, f32[9,1112,128]{2,1,0:T(8,128)S(1)}, bf16[384,1152]{1,0:T(8,128)(2,1)S(1)}...) custom-call(s32[1]{0:T(128)} %bitcast.5.me, s32[8]{0:T(128)S(1)} %stack.78.pos_names, ...), custom_call_target="tpu_custom_call" | custom-call | flops 9200000000 | bytes 1024 | tf_op jit(solution)/shard_map/project/pallas_call | solution.py:197
  41.9 5.2 %attend.1 = (f32[3,1112,128]{2,1,0:T(8,128)S(1)}, f32[8,320,128]{2,1,0:T(8,128)S(1)}, f32[1024,384]{1,0:T(8,128)S(1)}) custom-call(s32[12]{0:T(128)S(1)} %copy-done.8, f32[9,1112,128]{2,1,0:T(8,128)S(1)} %get-tuple-element.157.qkv, f32[1024,384]{1,0:T(8,128)S(1)} %get-tuple-element.158.embedded.refs_1_, bf16[384,384]{1,0:T(8,128)(2,1)S(1)} %get-tuple-element.159.w_out, ...), custom_call_target="tpu_custom_call" | custom-call | flops 11500000256 | bytes 1024 | tf_op jit(solution)/shard_map/attend/pallas_call | solution.py:197
  47.2 1.4 %collective-permute-done.11.refs_2_ = bf16[960,128]{1,0:T(8,128)(2,1)S(1)} collective-permute-done((bf16[960,128]{1,0:T(8,128)(2,1)S(1)}, bf16[960,128]{1,0:T(8,128)(2,1)S(1)}, u32[]{:S(2)}, u32[]{:S(2)}) %collective-permute-start.11) | collective-permute-done | bytes 245792 | tf_op jit(solution)/shard_map/ppermute | solution.py:738
  50.8 14.4 %feed_forward.1 = (bf16[984,384]{1,0:T(8,128)(2,1)}, f32[1024,384]{1,0:T(8,128)S(1)}, bf16[5120,128]{1,0:T(8,128)(2,1)S(1)}, bf16[1280,128]{1,0:T(8,128)(2,1)S(1...) custom-call(s32[1]{0:T(128)} %bitcast.6.mask, s32[1]{0:T(128)} %bitcast.5.me, ...), custom_call_target="tpu_custom_call" | custom-call | flops 20700000256 | bytes 1024 | tf_op jit(solution)/shard_map/feed_forward/pallas_call | solution.py:197
  65.4 2.9 %collective-permute-done.17.refs_0_ = bf16[5120,128]{1,0:T(8,128)(2,1)S(1)} collective-permute-done((bf16[5120,128]{1,0:T(8,128)(2,1)S(1)}, bf16[5120,128]{1,0:T(8,128)(2,1)S(1)}, u32[]{:S(2)}, u32[]{:S(2)}) %collective-permute-start.17) | collective-permute-done | bytes 1310752 | tf_op jit(solution)/shard_map/ppermute | solution.py:738
  68.6 1.6 %collective-permute-start.18 = (bf16[1280,128]{1,0:T(8,128)(2,1)S(1)}, bf16[1280,128]{1,0:T(8,128)(2,1)S(1)}, u32[]{:S(2)}, u32[]{:S(2)}) collective-permute-start(bf16[1280,128]{1,0:T(8,128)(2,1)S(1)} %get-tuple-element.192), channel_id=1, source_target_pairs={{0,2},{1,3},{2,0},{3,1},{4,6},{5,7},{6,4},{7,5},{8,10},{9,11},{10,... | collective-permute-start | bytes 983048 | tf_op jit(solution)/shard_map/ppermute | solution.py:738
  70.9 1.3 %collective-permute-start.20 = (bf16[1280,128]{1,0:T(8,128)(2,1)S(1)}, bf16[1280,128]{1,0:T(8,128)(2,1)S(1)}, u32[]{:S(2)}, u32[]{:S(2)}) collective-permute-start(bf16[1280,128]{1,0:T(8,128)(2,1)S(1)} %get-tuple-element.194), channel_id=1, source_target_pairs={{0,6},{1,7},{2,4},{3,5},{4,2},{5,3},{6,0},{7,1},{8,14},{9,15},{10,... | collective-permute-start | bytes 983048 | tf_op jit(solution)/shard_map/ppermute | solution.py:738
  72.1 6.8 %attend_back.1 = (f32[9,1112,128]{2,1,0:T(8,128)S(1)}, bf16[1024,384]{1,0:T(8,128)(2,1)S(1)}) custom-call(s32[12]{0:T(128)S(1)} %copy-done.8, f32[9,1112,128]{2,1,0:T(8,128)S(1)} %get-tuple-element.157.qkv, f32[3,1112,128]{2,1,0:T(8,128)S(1)} %get-tuple-element.172.mixed.refs_3_, f32[8,320,128]{2,1,0:T(8,128)S(1)} %get-tuple-element.173.log_total, ...), custom_call_target="tpu_custom_call" | custom-call | flops 13799999488 | bytes 1024 | tf_op jit(solution)/shard_map/attend_back/pallas_call | solution.py:197
  78.9 6.3 %project_back.1 = (bf16[984,384]{1,0:T(8,128)(2,1)}, bf16[320,128]{1,0:T(8,128)(2,1)S(1)}, bf16[320,128]{1,0:T(8,128)(2,1)S(1)}, bf16[2560,128]{1,0:T(8,128)(2,1...) custom-call(s32[1]{0:T(128)} %bitcast.5.me, ...), custom_call_target="tpu_custom_call" | custom-call | flops 11500000256 | bytes 1024 | tf_op jit(solution)/shard_map/project_back/pallas_call | solution.py:197
  85.2 1.5 %collective-permute-done.20.refs_3_ = bf16[1280,128]{1,0:T(8,128)(2,1)S(1)} collective-permute-done((bf16[1280,128]{1,0:T(8,128)(2,1)S(1)}, bf16[1280,128]{1,0:T(8,128)(2,1)S(1)}, u32[]{:S(2)}, u32[]{:S(2)}) %collective-permute-start.20) | collective-permute-done | bytes 327712 | tf_op jit(solution)/shard_map/ppermute | solution.py:738
  87.2 1.7 %collective-permute-done.22.refs_6_ = bf16[320,128]{1,0:T(8,128)(2,1)S(1)} collective-permute-done((bf16[320,128]{1,0:T(8,128)(2,1)S(1)}, bf16[320,128]{1,0:T(8,128)(2,1)S(1)}, u32[]{:S(2)}, u32[]{:S(2)}) %collective-permute-start.22) | collective-permute-done | bytes 81952 | tf_op jit(solution)/shard_map/ppermute | solution.py:738
  89.8 1.7 %collective-permute-start.24 = (bf16[720,128]{1,0:T(8,128)(2,1)S(1)}, bf16[720,128]{1,0:T(8,128)(2,1)S(1)}, u32[]{:S(2)}, u32[]{:S(2)}) collective-permute-start(bf16[720,128]{1,0:T(8,128)(2,1)S(1)} %get-tuple-element.219), channel_id=1, source_target_pairs={{0,4},{1,5},{2,6},{3,7},{4,0},{5,1},{6,2},{7,3},{8,12},{9,13},{10,... | collective-permute-start | bytes 552968 | tf_op jit(solution)/shard_map/ppermute | solution.py:738
  93.0 2.8 %collective-permute-start.30 = (bf16[320,128]{1,0:T(8,128)(2,1)S(1)}, bf16[320,128]{1,0:T(8,128)(2,1)S(1)}, u32[]{:S(2)}, u32[]{:S(2)}) collective-permute-start(bf16[320,128]{1,0:T(8,128)(2,1)S(1)} %get-tuple-element.235), channel_id=1, source_target_pairs={{0,16},{1,17},{2,18},{3,19},{4,20},{5,21},{6,22},{7,23},{8,24},{9,... | collective-permute-start | bytes 245768 | tf_op jit(solution)/shard_map/ppermute | solution.py:738
  96.7 2.2 %collective-permute-start.31 = (bf16[320,128]{1,0:T(8,128)(2,1)S(1)}, bf16[320,128]{1,0:T(8,128)(2,1)S(1)}, u32[]{:S(2)}, u32[]{:S(2)}) collective-permute-start(bf16[320,128]{1,0:T(8,128)(2,1)S(1)} %get-tuple-element.236), channel_id=1, source_target_pairs={{0,24},{1,25},{2,26},{3,27},{4,28},{5,29},{6,30},{7,31},{8,16},{9,... | collective-permute-start | bytes 245768 | tf_op jit(solution)/shard_map/ppermute | solution.py:738
  99.0 1.2 %collective-permute-done.24 = bf16[720,128]{1,0:T(8,128)(2,1)S(1)} collective-permute-done((bf16[720,128]{1,0:T(8,128)(2,1)S(1)}, bf16[720,128]{1,0:T(8,128)(2,1)S(1)}, u32[]{:S(2)}, u32[]{:S(2)}) %collective-permute-start.24) | collective-permute-done | bytes 184352 | tf_op jit(solution)/shard_map/ppermute | solution.py:738
  100.5 3.1 %collective-permute-start.27 = (bf16[240,128]{1,0:T(8,128)(2,1)S(1)}, bf16[240,128]{1,0:T(8,128)(2,1)S(1)}, u32[]{:S(2)}, u32[]{:S(2)}) collective-permute-start(bf16[240,128]{1,0:T(8,128)(2,1)S(1)} %get-tuple-element.227), channel_id=1, source_target_pairs={{0,16},{1,17},{2,18},{3,19},{4,20},{5,21},{6,22},{7,23},{8,24},{9,... | collective-permute-start | bytes 184328 | tf_op jit(solution)/shard_map/ppermute | solution.py:738
  105.0 1.2 %collective-permute-done.27.refs_2_ = bf16[240,128]{1,0:T(8,128)(2,1)S(1)} collective-permute-done((bf16[240,128]{1,0:T(8,128)(2,1)S(1)}, bf16[240,128]{1,0:T(8,128)(2,1)S(1)}, u32[]{:S(2)}, u32[]{:S(2)}) %collective-permute-start.27) | collective-permute-done | bytes 61472 | tf_op jit(solution)/shard_map/ppermute | solution.py:738
  106.2 3.4 %collective-permute-done.28.refs_3_ = bf16[240,128]{1,0:T(8,128)(2,1)S(1)} collective-permute-done((bf16[240,128]{1,0:T(8,128)(2,1)S(1)}, bf16[240,128]{1,0:T(8,128)(2,1)S(1)}, u32[]{:S(2)}, u32[]{:S(2)}) %collective-permute-start.28) | collective-permute-done | bytes 61472 | tf_op jit(solution)/shard_map/ppermute | solution.py:738
  109.7 1.3 %collective-permute-start.34 = (bf16[80,128]{1,0:T(8,128)(2,1)S(1)}, bf16[80,128]{1,0:T(8,128)(2,1)S(1)}, u32[]{:S(2)}, u32[]{:S(2)}) collective-permute-start(bf16[80,128]{1,0:T(8,128)(2,1)S(1)} %add_convert_fusion.1.refs_4_), channel_id=1, source_target_pairs={{0,6},{1,7},{2,4},{3,5},{4,2},{5,3},{6,0},{7,1},{8,14},{9,15},{10,... | collective-permute-start | bytes 61448 | tf_op jit(solution)/shard_map/ppermute | solution.py:738
  110.9 1.3 %collective-permute-start.33 = (bf16[80,128]{1,0:T(8,128)(2,1)S(1)}, bf16[80,128]{1,0:T(8,128)(2,1)S(1)}, u32[]{:S(2)}, u32[]{:S(2)}) collective-permute-start(bf16[80,128]{1,0:T(8,128)(2,1)S(1)} %add_convert_fusion.1.refs_4_), channel_id=1, source_target_pairs={{0,4},{1,5},{2,6},{3,7},{4,0},{5,1},{6,2},{7,3},{8,12},{9,13},{10,... | collective-permute-start | bytes 61448 | tf_op jit(solution)/shard_map/ppermute | solution.py:738
  113.2 1.4 %settle.2 = (f32[18504]{0:T(1024)}, f32[18504]{0:T(1024)}, f32[18504]{0:T(1024)}, f32[18504]{0:T(1024)}) custom-call(s32[2]{0:T(128)S(1)} %get-tuple-element.190.place, bf16[240,128]{1,0:T(8,128)(2,1)S(1)} %get-tuple-element.237.refs_0_, bf16[240,128]{1,0:T(8,128)(2,1)S(1)} %collective-permute-done.26.refs_1_, ...), custom_call_target="tpu_custom_call" | custom-call | tf_op jit(solution)/shard_map/settle/pallas_call | solution.py:721
  114.7 1.3 %collective-permute-done.32.refs_5_ = bf16[80,128]{1,0:T(8,128)(2,1)S(1)} collective-permute-done((bf16[80,128]{1,0:T(8,128)(2,1)S(1)}, bf16[80,128]{1,0:T(8,128)(2,1)S(1)}, u32[]{:S(2)}, u32[]{:S(2)}) %collective-permute-start.32) | collective-permute-done | bytes 20512 | tf_op jit(solution)/shard_map/ppermute | solution.py:738
  116.0 1.7 %settle.3 = (f32[38688]{0:T(1024)}, f32[38688]{0:T(1024)}, f32[38688]{0:T(1024)}, f32[38688]{0:T(1024)}) custom-call(s32[3]{0:T(128)S(1)} %pad_add_fusion.1.place, bf16[320,128]{1,0:T(8,128)(2,1)S(1)} %get-tuple-element.246.refs_0_, bf16[320,128]{1,0:T(8,128)(2,1)S(1)} %collective-permute-done.29.refs_1_, ...), custom_call_target="tpu_custom_call" | custom-call | tf_op jit(solution)/shard_map/settle/pallas_call | solution.py:721
  (86 shorter events, 16.2 us)
Async XLA Ops:
  2.5 9.4 %collective-permute-start.2 = (bf16[480,128]{1,0:T(8,128)(2,1)S(1)}, bf16[480,128]{1,0:T(8,128)(2,1)S(1)}, u32[]{:S(2)}, u32[]{:S(2)}) collective-permute-start(bf16[480,128]{1,0:T(8,128)(2,1)S(1)} %align.1), channel_id=1, source_target_pairs={{0,24},{1,25},{2,26},{3,27},{4,28},{5,29},{6,30},{7,31},{8,16},{9,... | collective-permute-start | bytes 368648 | tf_op jit(solution)/shard_map/ppermute | solution.py:738
  7.6 10.4 %collective-permute-start.1 = (bf16[480,128]{1,0:T(8,128)(2,1)S(1)}, bf16[480,128]{1,0:T(8,128)(2,1)S(1)}, u32[]{:S(2)}, u32[]{:S(2)}) collective-permute-start(bf16[480,128]{1,0:T(8,128)(2,1)S(1)} %align.1), channel_id=1, source_target_pairs={{0,16},{1,17},{2,18},{3,19},{4,20},{5,21},{6,22},{7,23},{8,24},{9,... | collective-permute-start | bytes 368648 | tf_op jit(solution)/shard_map/ppermute | solution.py:738
  7.6 10.4 %collective-permute-start = (bf16[480,128]{1,0:T(8,128)(2,1)S(1)}, bf16[480,128]{1,0:T(8,128)(2,1)S(1)}, u32[]{:S(2)}, u32[]{:S(2)}) collective-permute-start(bf16[480,128]{1,0:T(8,128)(2,1)S(1)} %align.1), channel_id=1, source_target_pairs={{0,8},{1,9},{2,10},{3,11},{4,12},{5,13},{6,14},{7,15},{8,0},{9,1},... | collective-permute-start | bytes 368648 | tf_op jit(solution)/shard_map/ppermute | solution.py:738
  18.1 9.9 %collective-permute-start.5 = (bf16[960,128]{1,0:T(8,128)(2,1)S(1)}, bf16[960,128]{1,0:T(8,128)(2,1)S(1)}, u32[]{:S(2)}, u32[]{:S(2)}) collective-permute-start(bf16[960,128]{1,0:T(8,128)(2,1)S(1)} %select_dynamic-update-slice_fusion.refs_0_), channel_id=1, source_target_pairs={{0,6},{1,7},{2,4},{3,5},{4,2},{5,3},{6,0},{7,1},{8,14},{9,15},{10,... | collective-permute-start | bytes 737288 | tf_op jit(solution)/shard_map/ppermute | solution.py:738
  20.6 10.7 %collective-permute-start.4 = (bf16[960,128]{1,0:T(8,128)(2,1)S(1)}, bf16[960,128]{1,0:T(8,128)(2,1)S(1)}, u32[]{:S(2)}, u32[]{:S(2)}) collective-permute-start(bf16[960,128]{1,0:T(8,128)(2,1)S(1)} %select_dynamic-update-slice_fusion.refs_0_), channel_id=1, source_target_pairs={{0,4},{1,5},{2,6},{3,7},{4,0},{5,1},{6,2},{7,3},{8,12},{9,13},{10,... | collective-permute-start | bytes 737288 | tf_op jit(solution)/shard_map/ppermute | solution.py:738
  21.1 10.3 %collective-permute-start.3 = (bf16[960,128]{1,0:T(8,128)(2,1)S(1)}, bf16[960,128]{1,0:T(8,128)(2,1)S(1)}, u32[]{:S(2)}, u32[]{:S(2)}) collective-permute-start(bf16[960,128]{1,0:T(8,128)(2,1)S(1)} %select_dynamic-update-slice_fusion.refs_0_), channel_id=1, source_target_pairs={{0,2},{1,3},{2,0},{3,1},{4,6},{5,7},{6,4},{7,5},{8,10},{9,11},{10,... | collective-permute-start | bytes 737288 | tf_op jit(solution)/shard_map/ppermute | solution.py:738
  31.5 1.9 %collective-permute-start.7 = (bf16[960,128]{1,0:T(8,128)(2,1)S(1)}, bf16[960,128]{1,0:T(8,128)(2,1)S(1)}, u32[]{:S(2)}, u32[]{:S(2)}) collective-permute-start(bf16[960,128]{1,0:T(8,128)(2,1)S(1)} %collective-permute-done.3.refs_1_), channel_id=1, source_target_pairs={{0,1},{1,0},{2,3},{3,2},{4,5},{5,4},{6,7},{7,6},{8,9},{9,8},{10,11... | collective-permute-start | bytes 737288 | tf_op jit(solution)/shard_map/ppermute | solution.py:738
  32.0 1.7 %collective-permute-start.8 = (bf16[960,128]{1,0:T(8,128)(2,1)S(1)}, bf16[960,128]{1,0:T(8,128)(2,1)S(1)}, u32[]{:S(2)}, u32[]{:S(2)}) collective-permute-start(bf16[960,128]{1,0:T(8,128)(2,1)S(1)} %collective-permute-done.4.refs_2_), channel_id=1, source_target_pairs={{0,1},{1,0},{2,3},{3,2},{4,5},{5,4},{6,7},{7,6},{8,9},{9,8},{10,11... | collective-permute-start | bytes 737288 | tf_op jit(solution)/shard_map/ppermute | solution.py:738
  32.0 2.1 %collective-permute-start.9 = (bf16[960,128]{1,0:T(8,128)(2,1)S(1)}, bf16[960,128]{1,0:T(8,128)(2,1)S(1)}, u32[]{:S(2)}, u32[]{:S(2)}) collective-permute-start(bf16[960,128]{1,0:T(8,128)(2,1)S(1)} %collective-permute-done.5.refs_3_), channel_id=1, source_target_pairs={{0,1},{1,0},{2,3},{3,2},{4,5},{5,4},{6,7},{7,6},{8,9},{9,8},{10,11... | collective-permute-start | bytes 737288 | tf_op jit(solution)/shard_map/ppermute | solution.py:738
  34.0 13.1 %collective-permute-start.13 = (bf16[960,128]{1,0:T(8,128)(2,1)S(1)}, bf16[960,128]{1,0:T(8,128)(2,1)S(1)}, u32[]{:S(2)}, u32[]{:S(2)}) collective-permute-start(bf16[960,128]{1,0:T(8,128)(2,1)S(1)} %pad_maximum_fusion.refs_0_), channel_id=1, source_target_pairs={{0,1},{1,0},{2,3},{3,2},{4,5},{5,4},{6,7},{7,6},{8,9},{9,8},{10,11... | collective-permute-start | bytes 737288 | tf_op jit(solution)/shard_map/ppermute | solution.py:738
  34.2 13.0 %collective-permute-start.12 = (bf16[960,128]{1,0:T(8,128)(2,1)S(1)}, bf16[960,128]{1,0:T(8,128)(2,1)S(1)}, u32[]{:S(2)}, u32[]{:S(2)}) collective-permute-start(bf16[960,128]{1,0:T(8,128)(2,1)S(1)} %pad_maximum_fusion.refs_0_), channel_id=1, source_target_pairs={{0,6},{1,7},{2,4},{3,5},{4,2},{5,3},{6,0},{7,1},{8,14},{9,15},{10,... | collective-permute-start | bytes 737288 | tf_op jit(solution)/shard_map/ppermute | solution.py:738
  35.8 12.7 %collective-permute-start.11 = (bf16[960,128]{1,0:T(8,128)(2,1)S(1)}, bf16[960,128]{1,0:T(8,128)(2,1)S(1)}, u32[]{:S(2)}, u32[]{:S(2)}) collective-permute-start(bf16[960,128]{1,0:T(8,128)(2,1)S(1)} %pad_maximum_fusion.refs_0_), channel_id=1, source_target_pairs={{0,4},{1,5},{2,6},{3,7},{4,0},{5,1},{6,2},{7,3},{8,12},{9,13},{10,... | collective-permute-start | bytes 737288 | tf_op jit(solution)/shard_map/ppermute | solution.py:738
  37.2 11.4 %collective-permute-start.10 = (bf16[960,128]{1,0:T(8,128)(2,1)S(1)}, bf16[960,128]{1,0:T(8,128)(2,1)S(1)}, u32[]{:S(2)}, u32[]{:S(2)}) collective-permute-start(bf16[960,128]{1,0:T(8,128)(2,1)S(1)} %pad_maximum_fusion.refs_0_), channel_id=1, source_target_pairs={{0,2},{1,3},{2,0},{3,1},{4,6},{5,7},{6,4},{7,5},{8,10},{9,11},{10,... | collective-permute-start | bytes 737288 | tf_op jit(solution)/shard_map/ppermute | solution.py:738
  48.6 1.8 %collective-permute-start.15 = (bf16[960,128]{1,0:T(8,128)(2,1)S(1)}, bf16[960,128]{1,0:T(8,128)(2,1)S(1)}, u32[]{:S(2)}, u32[]{:S(2)}) collective-permute-start(bf16[960,128]{1,0:T(8,128)(2,1)S(1)} %collective-permute-done.11.refs_2_), channel_id=1, source_target_pairs={{0,1},{1,0},{2,3},{3,2},{4,5},{5,4},{6,7},{7,6},{8,9},{9,8},{10,11... | collective-permute-start | bytes 737288 | tf_op jit(solution)/shard_map/ppermute | solution.py:738
  65.2 3.0 %collective-permute-start.17 = (bf16[5120,128]{1,0:T(8,128)(2,1)S(1)}, bf16[5120,128]{1,0:T(8,128)(2,1)S(1)}, u32[]{:S(2)}, u32[]{:S(2)}) collective-permute-start(bf16[5120,128]{1,0:T(8,128)(2,1)S(1)} %get-tuple-element.175), channel_id=1, source_target_pairs={{0,1},{1,0},{2,3},{3,2},{4,5},{5,4},{6,7},{7,6},{8,9},{9,8},{10,11... | collective-permute-start | bytes 3932168 | tf_op jit(solution)/shard_map/ppermute | solution.py:738
  68.6 16.6 %collective-permute-start.18 = (bf16[1280,128]{1,0:T(8,128)(2,1)S(1)}, bf16[1280,128]{1,0:T(8,128)(2,1)S(1)}, u32[]{:S(2)}, u32[]{:S(2)}) collective-permute-start(bf16[1280,128]{1,0:T(8,128)(2,1)S(1)} %get-tuple-element.192), channel_id=1, source_target_pairs={{0,2},{1,3},{2,0},{3,1},{4,6},{5,7},{6,4},{7,5},{8,10},{9,11},{10,... | collective-permute-start | bytes 983048 | tf_op jit(solution)/shard_map/ppermute | solution.py:738
  70.1 15.1 %collective-permute-start.19 = (bf16[1280,128]{1,0:T(8,128)(2,1)S(1)}, bf16[1280,128]{1,0:T(8,128)(2,1)S(1)}, u32[]{:S(2)}, u32[]{:S(2)}) collective-permute-start(bf16[1280,128]{1,0:T(8,128)(2,1)S(1)} %get-tuple-element.193), channel_id=1, source_target_pairs={{0,4},{1,5},{2,6},{3,7},{4,0},{5,1},{6,2},{7,3},{8,12},{9,13},{10,... | collective-permute-start | bytes 983048 | tf_op jit(solution)/shard_map/ppermute | solution.py:738
  70.9 15.9 %collective-permute-start.20 = (bf16[1280,128]{1,0:T(8,128)(2,1)S(1)}, bf16[1280,128]{1,0:T(8,128)(2,1)S(1)}, u32[]{:S(2)}, u32[]{:S(2)}) collective-permute-start(bf16[1280,128]{1,0:T(8,128)(2,1)S(1)} %get-tuple-element.194), channel_id=1, source_target_pairs={{0,6},{1,7},{2,4},{3,5},{4,2},{5,3},{6,0},{7,1},{8,14},{9,15},{10,... | collective-permute-start | bytes 983048 | tf_op jit(solution)/shard_map/ppermute | solution.py:738
  86.7 2.2 %collective-permute-start.21 = (bf16[2560,128]{1,0:T(8,128)(2,1)S(1)}, bf16[2560,128]{1,0:T(8,128)(2,1)S(1)}, u32[]{:S(2)}, u32[]{:S(2)}) collective-permute-start(bf16[2560,128]{1,0:T(8,128)(2,1)S(1)} %get-tuple-element.202), channel_id=1, source_target_pairs={{0,1},{1,0},{2,3},{3,2},{4,5},{5,4},{6,7},{7,6},{8,9},{9,8},{10,11... | collective-permute-start | bytes 1966088 | tf_op jit(solution)/shard_map/ppermute | solution.py:738
  86.7 2.2 %collective-permute-start.22 = (bf16[320,128]{1,0:T(8,128)(2,1)S(1)}, bf16[320,128]{1,0:T(8,128)(2,1)S(1)}, u32[]{:S(2)}, u32[]{:S(2)}) collective-permute-start(bf16[320,128]{1,0:T(8,128)(2,1)S(1)} %get-tuple-element.208), channel_id=1, source_target_pairs={{0,1},{1,0},{2,3},{3,2},{4,5},{5,4},{6,7},{7,6},{8,9},{9,8},{10,11... | collective-permute-start | bytes 245768 | tf_op jit(solution)/shard_map/ppermute | solution.py:738
  89.2 7.5 %collective-permute-start.23 = (bf16[720,128]{1,0:T(8,128)(2,1)S(1)}, bf16[720,128]{1,0:T(8,128)(2,1)S(1)}, u32[]{:S(2)}, u32[]{:S(2)}) collective-permute-start(bf16[720,128]{1,0:T(8,128)(2,1)S(1)} %get-tuple-element.218), channel_id=1, source_target_pairs={{0,2},{1,3},{2,0},{3,1},{4,6},{5,7},{6,4},{7,5},{8,10},{9,11},{10,... | collective-permute-start | bytes 552968 | tf_op jit(solution)/shard_map/ppermute | solution.py:738
  89.8 10.3 %collective-permute-start.24 = (bf16[720,128]{1,0:T(8,128)(2,1)S(1)}, bf16[720,128]{1,0:T(8,128)(2,1)S(1)}, u32[]{:S(2)}, u32[]{:S(2)}) collective-permute-start(bf16[720,128]{1,0:T(8,128)(2,1)S(1)} %get-tuple-element.219), channel_id=1, source_target_pairs={{0,4},{1,5},{2,6},{3,7},{4,0},{5,1},{6,2},{7,3},{8,12},{9,13},{10,... | collective-permute-start | bytes 552968 | tf_op jit(solution)/shard_map/ppermute | solution.py:738
  91.6 8.6 %collective-permute-start.25 = (bf16[720,128]{1,0:T(8,128)(2,1)S(1)}, bf16[720,128]{1,0:T(8,128)(2,1)S(1)}, u32[]{:S(2)}, u32[]{:S(2)}) collective-permute-start(bf16[720,128]{1,0:T(8,128)(2,1)S(1)} %get-tuple-element.220), channel_id=1, source_target_pairs={{0,6},{1,7},{2,4},{3,5},{4,2},{5,3},{6,0},{7,1},{8,14},{9,15},{10,... | collective-permute-start | bytes 552968 | tf_op jit(solution)/shard_map/ppermute | solution.py:738
  92.9 10.7 %collective-permute-start.29 = (bf16[320,128]{1,0:T(8,128)(2,1)S(1)}, bf16[320,128]{1,0:T(8,128)(2,1)S(1)}, u32[]{:S(2)}, u32[]{:S(2)}) collective-permute-start(bf16[320,128]{1,0:T(8,128)(2,1)S(1)} %get-tuple-element.234), channel_id=1, source_target_pairs={{0,8},{1,9},{2,10},{3,11},{4,12},{5,13},{6,14},{7,15},{8,0},{9,1},... | collective-permute-start | bytes 245768 | tf_op jit(solution)/shard_map/ppermute | solution.py:738
  93.0 11.8 %collective-permute-start.30 = (bf16[320,128]{1,0:T(8,128)(2,1)S(1)}, bf16[320,128]{1,0:T(8,128)(2,1)S(1)}, u32[]{:S(2)}, u32[]{:S(2)}) collective-permute-start(bf16[320,128]{1,0:T(8,128)(2,1)S(1)} %get-tuple-element.235), channel_id=1, source_target_pairs={{0,16},{1,17},{2,18},{3,19},{4,20},{5,21},{6,22},{7,23},{8,24},{9,... | collective-permute-start | bytes 245768 | tf_op jit(solution)/shard_map/ppermute | solution.py:738
  96.7 8.1 %collective-permute-start.31 = (bf16[320,128]{1,0:T(8,128)(2,1)S(1)}, bf16[320,128]{1,0:T(8,128)(2,1)S(1)}, u32[]{:S(2)}, u32[]{:S(2)}) collective-permute-start(bf16[320,128]{1,0:T(8,128)(2,1)S(1)} %get-tuple-element.236), channel_id=1, source_target_pairs={{0,24},{1,25},{2,26},{3,27},{4,28},{5,29},{6,30},{7,31},{8,16},{9,... | collective-permute-start | bytes 245768 | tf_op jit(solution)/shard_map/ppermute | solution.py:738
  100.4 4.6 %collective-permute-start.26 = (bf16[240,128]{1,0:T(8,128)(2,1)S(1)}, bf16[240,128]{1,0:T(8,128)(2,1)S(1)}, u32[]{:S(2)}, u32[]{:S(2)}) collective-permute-start(bf16[240,128]{1,0:T(8,128)(2,1)S(1)} %get-tuple-element.226), channel_id=1, source_target_pairs={{0,8},{1,9},{2,10},{3,11},{4,12},{5,13},{6,14},{7,15},{8,0},{9,1},... | collective-permute-start | bytes 184328 | tf_op jit(solution)/shard_map/ppermute | solution.py:738
  100.5 5.7 %collective-permute-start.27 = (bf16[240,128]{1,0:T(8,128)(2,1)S(1)}, bf16[240,128]{1,0:T(8,128)(2,1)S(1)}, u32[]{:S(2)}, u32[]{:S(2)}) collective-permute-start(bf16[240,128]{1,0:T(8,128)(2,1)S(1)} %get-tuple-element.227), channel_id=1, source_target_pairs={{0,16},{1,17},{2,18},{3,19},{4,20},{5,21},{6,22},{7,23},{8,24},{9,... | collective-permute-start | bytes 184328 | tf_op jit(solution)/shard_map/ppermute | solution.py:738
  103.6 6.0 %collective-permute-start.28 = (bf16[240,128]{1,0:T(8,128)(2,1)S(1)}, bf16[240,128]{1,0:T(8,128)(2,1)S(1)}, u32[]{:S(2)}, u32[]{:S(2)}) collective-permute-start(bf16[240,128]{1,0:T(8,128)(2,1)S(1)} %concatenate.26), channel_id=1, source_target_pairs={{0,24},{1,25},{2,26},{3,27},{4,28},{5,29},{6,30},{7,31},{8,16},{9,... | collective-permute-start | bytes 184328 | tf_op jit(solution)/shard_map/ppermute | solution.py:738
  109.7 5.0 %collective-permute-start.34 = (bf16[80,128]{1,0:T(8,128)(2,1)S(1)}, bf16[80,128]{1,0:T(8,128)(2,1)S(1)}, u32[]{:S(2)}, u32[]{:S(2)}) collective-permute-start(bf16[80,128]{1,0:T(8,128)(2,1)S(1)} %add_convert_fusion.1.refs_4_), channel_id=1, source_target_pairs={{0,6},{1,7},{2,4},{3,5},{4,2},{5,3},{6,0},{7,1},{8,14},{9,15},{10,... | collective-permute-start | bytes 61448 | tf_op jit(solution)/shard_map/ppermute | solution.py:738
  110.9 3.8 %collective-permute-start.33 = (bf16[80,128]{1,0:T(8,128)(2,1)S(1)}, bf16[80,128]{1,0:T(8,128)(2,1)S(1)}, u32[]{:S(2)}, u32[]{:S(2)}) collective-permute-start(bf16[80,128]{1,0:T(8,128)(2,1)S(1)} %add_convert_fusion.1.refs_4_), channel_id=1, source_target_pairs={{0,4},{1,5},{2,6},{3,7},{4,0},{5,1},{6,2},{7,3},{8,12},{9,13},{10,... | collective-permute-start | bytes 61448 | tf_op jit(solution)/shard_map/ppermute | solution.py:738
  112.2 3.8 %collective-permute-start.32 = (bf16[80,128]{1,0:T(8,128)(2,1)S(1)}, bf16[80,128]{1,0:T(8,128)(2,1)S(1)}, u32[]{:S(2)}, u32[]{:S(2)}) collective-permute-start(bf16[80,128]{1,0:T(8,128)(2,1)S(1)} %add_convert_fusion.1.refs_4_), channel_id=1, source_target_pairs={{0,2},{1,3},{2,0},{3,1},{4,6},{5,7},{6,4},{7,5},{8,10},{9,11},{10,... | collective-permute-start | bytes 61448 | tf_op jit(solution)/shard_map/ppermute | solution.py:738
  (12 other events, 212.8 us)

commit v4 on v3

--- a/solution.py
+++ b/solution.py
@@ -895,7 +895,6 @@
     attn = attn + [swap(a, BIT_CORE) for a in attn]
     mlp = [lax.select_n(z, *[pieces[k ^ here][small:] for here in range(4)]) for k in (1, 2, 3)]
     mlp = jnp.concatenate(mlp, axis=0)
-    attn, mlp = together(attn, mlp)
     mlp_far = swap(mlp, BIT_CORE)
     mlp = spread_xy(mlp)
     at = 4 * small

time: 118 us -> 117 us (level)
  transfers between devices with their start and end apart: 35 -> 35, of which waited for: 23 -> 19; matrix products, arithmetic and copies ran while one was open for 1% -> 1% of each run, Pallas kernels for 20% -> 21%
where the time goes in v4:
time: 117 us; the launch traced here: 116 us
  Pallas kernels  42.3 us (36%)
  waiting for transfers between devices  37.1 us (32%)
  starting transfers between devices  34.3 us (29%)
    ppermute x35, waiting for transfers between devices, swap(): return lax.ppermute(value, AXES, [(j, j ^ bits) for j in range(DEVICES)])  37.1 us
    pallas_call x5, Pallas kernels, call(): pl.pallas_call(kernel, in_specs=[SMEM_SPEC if a.dtype == jnp.int32 and a....  36.9 us
    ppermute x35, starting transfers between devices, swap(): return lax.ppermute(value, AXES, [(j, j ^ bits) for j in range(DEVICES)])  34.3 us
    pallas_call x2, Pallas kernels, settle(): pl.pallas_call(functools.partial(settle_kernel, scale, plan, late_plan, l...  3.06 us
  transfers between devices with their start and end apart: 35, of which 19 were waited for; matrix products, arithmetic and copies ran while one was open for 1% of the time, Pallas kernels for 21%

profile of v4, /device:TPU:0, one launch (start us, length us, event | category | flops | bytes accessed | tf_op | source)
XLA Modules:
  0.0 116.3 jit_solution(4588498027970542737)
XLA Ops:
  0.8 1.7 %align.1 = bf16[480,128]{1,0:T(8,128)(2,1)S(1)} custom-call(s32[5]{0:T(128)S(1)} %stack.67.place, f32[18504]{0:T(1024)} %refs_4_.1, f32[38688]{0:T(1024)} %refs_8_.1), custom_call_target="tpu_custom_call" | custom-call | tf_op jit(solution)/shard_map/align/pallas_call | solution.py:962
  2.5 5.1 %collective-permute-start.2 = (bf16[480,128]{1,0:T(8,128)(2,1)S(1)}, bf16[480,128]{1,0:T(8,128)(2,1)S(1)}, u32[]{:S(2)}, u32[]{:S(2)}) collective-permute-start(bf16[480,128]{1,0:T(8,128)(2,1)S(1)} %align.1), channel_id=1, source_target_pairs={{0,24},{1,25},{2,26},{3,27},{4,28},{5,29},{6,30},{7,31},{8,16},{9,... | collective-permute-start | bytes 368648 | tf_op jit(solution)/shard_map/ppermute | solution.py:738
  9.5 2.4 %collective-permute-done.2 = bf16[480,128]{1,0:T(8,128)(2,1)S(1)} collective-permute-done((bf16[480,128]{1,0:T(8,128)(2,1)S(1)}, bf16[480,128]{1,0:T(8,128)(2,1)S(1)}, u32[]{:S(2)}, u32[]{:S(2)}) %collective-permute-start.2) | collective-permute-done | bytes 122912 | tf_op jit(solution)/shard_map/ppermute | solution.py:738
  11.9 6.1 %collective-permute-done.1 = bf16[480,128]{1,0:T(8,128)(2,1)S(1)} collective-permute-done((bf16[480,128]{1,0:T(8,128)(2,1)S(1)}, bf16[480,128]{1,0:T(8,128)(2,1)S(1)}, u32[]{:S(2)}, u32[]{:S(2)}) %collective-permute-start.1) | collective-permute-done | bytes 122912 | tf_op jit(solution)/shard_map/ppermute | solution.py:738
  18.1 2.5 %collective-permute-start.5 = (bf16[960,128]{1,0:T(8,128)(2,1)S(1)}, bf16[960,128]{1,0:T(8,128)(2,1)S(1)}, u32[]{:S(2)}, u32[]{:S(2)}) collective-permute-start(bf16[960,128]{1,0:T(8,128)(2,1)S(1)} %select_dynamic-update-slice_fusion.refs_0_), channel_id=1, source_target_pairs={{0,6},{1,7},{2,4},{3,5},{4,2},{5,3},{6,0},{7,1},{8,14},{9,15},{10,... | collective-permute-start | bytes 737288 | tf_op jit(solution)/shard_map/ppermute | solution.py:738
  21.7 6.3 %collective-permute-done.5.refs_3_ = bf16[960,128]{1,0:T(8,128)(2,1)S(1)} collective-permute-done((bf16[960,128]{1,0:T(8,128)(2,1)S(1)}, bf16[960,128]{1,0:T(8,128)(2,1)S(1)}, u32[]{:S(2)}, u32[]{:S(2)}) %collective-permute-start.5) | collective-permute-done | bytes 245792 | tf_op jit(solution)/shard_map/ppermute | solution.py:738
  28.0 3.3 %collective-permute-done.4.refs_2_ = bf16[960,128]{1,0:T(8,128)(2,1)S(1)} collective-permute-done((bf16[960,128]{1,0:T(8,128)(2,1)S(1)}, bf16[960,128]{1,0:T(8,128)(2,1)S(1)}, u32[]{:S(2)}, u32[]{:S(2)}) %collective-permute-start.4) | collective-permute-done | bytes 245792 | tf_op jit(solution)/shard_map/ppermute | solution.py:738
  33.0 1.7 %collective-permute-start.8 = (bf16[960,128]{1,0:T(8,128)(2,1)S(1)}, bf16[960,128]{1,0:T(8,128)(2,1)S(1)}, u32[]{:S(2)}, u32[]{:S(2)}) collective-permute-start(bf16[960,128]{1,0:T(8,128)(2,1)S(1)} %pad_maximum_fusion.refs_0_), channel_id=1, source_target_pairs={{0,6},{1,7},{2,4},{3,5},{4,2},{5,3},{6,0},{7,1},{8,14},{9,15},{10,... | collective-permute-start | bytes 737288 | tf_op jit(solution)/shard_map/ppermute | solution.py:738
  34.6 1.3 %collective-permute-start.7 = (bf16[960,128]{1,0:T(8,128)(2,1)S(1)}, bf16[960,128]{1,0:T(8,128)(2,1)S(1)}, u32[]{:S(2)}, u32[]{:S(2)}) collective-permute-start(bf16[960,128]{1,0:T(8,128)(2,1)S(1)} %pad_maximum_fusion.refs_0_), channel_id=1, source_target_pairs={{0,4},{1,5},{2,6},{3,7},{4,0},{5,1},{6,2},{7,3},{8,12},{9,13},{10,... | collective-permute-start | bytes 737288 | tf_op jit(solution)/shard_map/ppermute | solution.py:738
  36.5 4.2 %project.1 = (f32[1024,384]{1,0:T(8,128)S(1)}, bf16[1024,384]{1,0:T(8,128)(2,1)S(1)}, f32[9,1112,128]{2,1,0:T(8,128)S(1)}, bf16[384,1152]{1,0:T(8,128)(2,1)S(1)}...) custom-call(s32[1]{0:T(128)} %bitcast.5.me, s32[8]{0:T(128)S(1)} %stack.78.pos_names, ...), custom_call_target="tpu_custom_call" | custom-call | flops 9200000000 | bytes 1024 | tf_op jit(solution)/shard_map/project/pallas_call | solution.py:197
  40.7 5.2 %attend.1 = (f32[3,1112,128]{2,1,0:T(8,128)S(1)}, f32[8,320,128]{2,1,0:T(8,128)S(1)}, f32[1024,384]{1,0:T(8,128)S(1)}) custom-call(s32[12]{0:T(128)S(1)} %copy-done.8, f32[9,1112,128]{2,1,0:T(8,128)S(1)} %get-tuple-element.139.qkv, f32[1024,384]{1,0:T(8,128)S(1)} %get-tuple-element.140.embedded.refs_1_, bf16[384,384]{1,0:T(8,128)(2,1)S(1)} %get-tuple-element.141.w_out, ...), custom_call_target="tpu_custom_call" | custom-call | flops 11500000256 | bytes 1024 | tf_op jit(solution)/shard_map/attend/pallas_call | solution.py:197
  49.4 14.5 %feed_forward.1 = (bf16[984,384]{1,0:T(8,128)(2,1)}, f32[1024,384]{1,0:T(8,128)S(1)}, bf16[5120,128]{1,0:T(8,128)(2,1)S(1)}, bf16[1280,128]{1,0:T(8,128)(2,1)S(1...) custom-call(s32[1]{0:T(128)} %bitcast.6.mask, s32[1]{0:T(128)} %bitcast.5.me, ...), custom_call_target="tpu_custom_call" | custom-call | flops 20700000256 | bytes 1024 | tf_op jit(solution)/shard_map/feed_forward/pallas_call | solution.py:197
  64.0 2.9 %collective-permute-done.17.refs_0_ = bf16[5120,128]{1,0:T(8,128)(2,1)S(1)} collective-permute-done((bf16[5120,128]{1,0:T(8,128)(2,1)S(1)}, bf16[5120,128]{1,0:T(8,128)(2,1)S(1)}, u32[]{:S(2)}, u32[]{:S(2)}) %collective-permute-start.17) | collective-permute-done | bytes 1310752 | tf_op jit(solution)/shard_map/ppermute | solution.py:738
  67.2 2.2 %collective-permute-start.18 = (bf16[1280,128]{1,0:T(8,128)(2,1)S(1)}, bf16[1280,128]{1,0:T(8,128)(2,1)S(1)}, u32[]{:S(2)}, u32[]{:S(2)}) collective-permute-start(bf16[1280,128]{1,0:T(8,128)(2,1)S(1)} %get-tuple-element.174), channel_id=1, source_target_pairs={{0,2},{1,3},{2,0},{3,1},{4,6},{5,7},{6,4},{7,5},{8,10},{9,11},{10,... | collective-permute-start | bytes 983048 | tf_op jit(solution)/shard_map/ppermute | solution.py:738
  69.5 1.5 %collective-permute-start.20 = (bf16[1280,128]{1,0:T(8,128)(2,1)S(1)}, bf16[1280,128]{1,0:T(8,128)(2,1)S(1)}, u32[]{:S(2)}, u32[]{:S(2)}) collective-permute-start(bf16[1280,128]{1,0:T(8,128)(2,1)S(1)} %get-tuple-element.176), channel_id=1, source_target_pairs={{0,6},{1,7},{2,4},{3,5},{4,2},{5,3},{6,0},{7,1},{8,14},{9,15},{10,... | collective-permute-start | bytes 983048 | tf_op jit(solution)/shard_map/ppermute | solution.py:738
  70.9 6.8 %attend_back.1 = (f32[9,1112,128]{2,1,0:T(8,128)S(1)}, bf16[1024,384]{1,0:T(8,128)(2,1)S(1)}) custom-call(s32[12]{0:T(128)S(1)} %copy-done.8, f32[9,1112,128]{2,1,0:T(8,128)S(1)} %get-tuple-element.139.qkv, f32[3,1112,128]{2,1,0:T(8,128)S(1)} %get-tuple-element.154.mixed.refs_3_, f32[8,320,128]{2,1,0:T(8,128)S(1)} %get-tuple-element.155.log_total, ...), custom_call_target="tpu_custom_call" | custom-call | flops 13799999488 | bytes 1024 | tf_op jit(solution)/shard_map/attend_back/pallas_call | solution.py:197
  77.7 6.3 %project_back.1 = (bf16[984,384]{1,0:T(8,128)(2,1)}, bf16[320,128]{1,0:T(8,128)(2,1)S(1)}, bf16[320,128]{1,0:T(8,128)(2,1)S(1)}, bf16[2560,128]{1,0:T(8,128)(2,1...) custom-call(s32[1]{0:T(128)} %bitcast.5.me, ...), custom_call_target="tpu_custom_call" | custom-call | flops 11500000256 | bytes 1024 | tf_op jit(solution)/shard_map/project_back/pallas_call | solution.py:197
  84.0 1.9 %collective-permute-done.19.refs_2_ = bf16[1280,128]{1,0:T(8,128)(2,1)S(1)} collective-permute-done((bf16[1280,128]{1,0:T(8,128)(2,1)S(1)}, bf16[1280,128]{1,0:T(8,128)(2,1)S(1)}, u32[]{:S(2)}, u32[]{:S(2)}) %collective-permute-start.19) | collective-permute-done | bytes 327712 | tf_op jit(solution)/shard_map/ppermute | solution.py:738
  86.4 1.7 %collective-permute-done.22.refs_6_ = bf16[320,128]{1,0:T(8,128)(2,1)S(1)} collective-permute-done((bf16[320,128]{1,0:T(8,128)(2,1)S(1)}, bf16[320,128]{1,0:T(8,128)(2,1)S(1)}, u32[]{:S(2)}, u32[]{:S(2)}) %collective-permute-start.22) | collective-permute-done | bytes 81952 | tf_op jit(solution)/shard_map/ppermute | solution.py:738
  88.8 1.4 %collective-permute-start.24 = (bf16[720,128]{1,0:T(8,128)(2,1)S(1)}, bf16[720,128]{1,0:T(8,128)(2,1)S(1)}, u32[]{:S(2)}, u32[]{:S(2)}) collective-permute-start(bf16[720,128]{1,0:T(8,128)(2,1)S(1)} %get-tuple-element.201), channel_id=1, source_target_pairs={{0,4},{1,5},{2,6},{3,7},{4,0},{5,1},{6,2},{7,3},{8,12},{9,13},{10,... | collective-permute-start | bytes 552968 | tf_op jit(solution)/shard_map/ppermute | solution.py:738
  90.2 1.8 %collective-permute-start.25 = (bf16[720,128]{1,0:T(8,128)(2,1)S(1)}, bf16[720,128]{1,0:T(8,128)(2,1)S(1)}, u32[]{:S(2)}, u32[]{:S(2)}) collective-permute-start(bf16[720,128]{1,0:T(8,128)(2,1)S(1)} %get-tuple-element.202), channel_id=1, source_target_pairs={{0,6},{1,7},{2,4},{3,5},{4,2},{5,3},{6,0},{7,1},{8,14},{9,15},{10,... | collective-permute-start | bytes 552968 | tf_op jit(solution)/shard_map/ppermute | solution.py:738
  92.2 2.2 %collective-permute-start.30 = (bf16[320,128]{1,0:T(8,128)(2,1)S(1)}, bf16[320,128]{1,0:T(8,128)(2,1)S(1)}, u32[]{:S(2)}, u32[]{:S(2)}) collective-permute-start(bf16[320,128]{1,0:T(8,128)(2,1)S(1)} %get-tuple-element.217), channel_id=1, source_target_pairs={{0,16},{1,17},{2,18},{3,19},{4,20},{5,21},{6,22},{7,23},{8,24},{9,... | collective-permute-start | bytes 245768 | tf_op jit(solution)/shard_map/ppermute | solution.py:738
  94.4 1.5 %collective-permute-done.23 = bf16[720,128]{1,0:T(8,128)(2,1)S(1)} collective-permute-done((bf16[720,128]{1,0:T(8,128)(2,1)S(1)}, bf16[720,128]{1,0:T(8,128)(2,1)S(1)}, u32[]{:S(2)}, u32[]{:S(2)}) %collective-permute-start.23) | collective-permute-done | bytes 184352 | tf_op jit(solution)/shard_map/ppermute | solution.py:738
  95.9 1.7 %collective-permute-start.31 = (bf16[320,128]{1,0:T(8,128)(2,1)S(1)}, bf16[320,128]{1,0:T(8,128)(2,1)S(1)}, u32[]{:S(2)}, u32[]{:S(2)}) collective-permute-start(bf16[320,128]{1,0:T(8,128)(2,1)S(1)} %get-tuple-element.218), channel_id=1, source_target_pairs={{0,24},{1,25},{2,26},{3,27},{4,28},{5,29},{6,30},{7,31},{8,16},{9,... | collective-permute-start | bytes 245768 | tf_op jit(solution)/shard_map/ppermute | solution.py:738
  97.6 1.6 %collective-permute-done.24 = bf16[720,128]{1,0:T(8,128)(2,1)S(1)} collective-permute-done((bf16[720,128]{1,0:T(8,128)(2,1)S(1)}, bf16[720,128]{1,0:T(8,128)(2,1)S(1)}, u32[]{:S(2)}, u32[]{:S(2)}) %collective-permute-start.24) | collective-permute-done | bytes 184352 | tf_op jit(solution)/shard_map/ppermute | solution.py:738
  99.4 2.4 %collective-permute-start.27 = (bf16[240,128]{1,0:T(8,128)(2,1)S(1)}, bf16[240,128]{1,0:T(8,128)(2,1)S(1)}, u32[]{:S(2)}, u32[]{:S(2)}) collective-permute-start(bf16[240,128]{1,0:T(8,128)(2,1)S(1)} %get-tuple-element.209), channel_id=1, source_target_pairs={{0,16},{1,17},{2,18},{3,19},{4,20},{5,21},{6,22},{7,23},{8,24},{9,... | collective-permute-start | bytes 184328 | tf_op jit(solution)/shard_map/ppermute | solution.py:738
  101.8 2.0 %collective-permute-start.28 = (bf16[240,128]{1,0:T(8,128)(2,1)S(1)}, bf16[240,128]{1,0:T(8,128)(2,1)S(1)}, u32[]{:S(2)}, u32[]{:S(2)}) collective-permute-start(bf16[240,128]{1,0:T(8,128)(2,1)S(1)} %concatenate.26), channel_id=1, source_target_pairs={{0,24},{1,25},{2,26},{3,27},{4,28},{5,29},{6,30},{7,31},{8,16},{9,... | collective-permute-start | bytes 184328 | tf_op jit(solution)/shard_map/ppermute | solution.py:738
  103.8 2.6 %collective-permute-done.27.refs_2_ = bf16[240,128]{1,0:T(8,128)(2,1)S(1)} collective-permute-done((bf16[240,128]{1,0:T(8,128)(2,1)S(1)}, bf16[240,128]{1,0:T(8,128)(2,1)S(1)}, u32[]{:S(2)}, u32[]{:S(2)}) %collective-permute-start.27) | collective-permute-done | bytes 61472 | tf_op jit(solution)/shard_map/ppermute | solution.py:738
  106.4 1.4 %collective-permute-done.28.refs_3_ = bf16[240,128]{1,0:T(8,128)(2,1)S(1)} collective-permute-done((bf16[240,128]{1,0:T(8,128)(2,1)S(1)}, bf16[240,128]{1,0:T(8,128)(2,1)S(1)}, u32[]{:S(2)}, u32[]{:S(2)}) %collective-permute-start.28) | collective-permute-done | bytes 61472 | tf_op jit(solution)/shard_map/ppermute | solution.py:738
  107.8 1.7 %collective-permute-start.34 = (bf16[80,128]{1,0:T(8,128)(2,1)S(1)}, bf16[80,128]{1,0:T(8,128)(2,1)S(1)}, u32[]{:S(2)}, u32[]{:S(2)}) collective-permute-start(bf16[80,128]{1,0:T(8,128)(2,1)S(1)} %add_convert_fusion.1.refs_4_), channel_id=1, source_target_pairs={{0,6},{1,7},{2,4},{3,5},{4,2},{5,3},{6,0},{7,1},{8,14},{9,15},{10,... | collective-permute-start | bytes 61448 | tf_op jit(solution)/shard_map/ppermute | solution.py:738
  111.4 1.4 %settle.2 = (f32[18504]{0:T(1024)}, f32[18504]{0:T(1024)}, f32[18504]{0:T(1024)}, f32[18504]{0:T(1024)}) custom-call(s32[2]{0:T(128)S(1)} %get-tuple-element.172.place, bf16[240,128]{1,0:T(8,128)(2,1)S(1)} %get-tuple-element.219.refs_0_, bf16[240,128]{1,0:T(8,128)(2,1)S(1)} %collective-permute-done.26.refs_1_, ...), custom_call_target="tpu_custom_call" | custom-call | tf_op jit(solution)/shard_map/settle/pallas_call | solution.py:721
  114.6 1.7 %settle.3 = (f32[38688]{0:T(1024)}, f32[38688]{0:T(1024)}, f32[38688]{0:T(1024)}, f32[38688]{0:T(1024)}) custom-call(s32[3]{0:T(128)S(1)} %pad_add_fusion.1.place, bf16[320,128]{1,0:T(8,128)(2,1)S(1)} %get-tuple-element.228.refs_0_, bf16[320,128]{1,0:T(8,128)(2,1)S(1)} %collective-permute-done.29.refs_1_, ...), custom_call_target="tpu_custom_call" | custom-call | tf_op jit(solution)/shard_map/settle/pallas_call | solution.py:721
  (86 shorter events, 14.5 us)
Async XLA Ops:
  2.5 9.4 %collective-permute-start.2 = (bf16[480,128]{1,0:T(8,128)(2,1)S(1)}, bf16[480,128]{1,0:T(8,128)(2,1)S(1)}, u32[]{:S(2)}, u32[]{:S(2)}) collective-permute-start(bf16[480,128]{1,0:T(8,128)(2,1)S(1)} %align.1), channel_id=1, source_target_pairs={{0,24},{1,25},{2,26},{3,27},{4,28},{5,29},{6,30},{7,31},{8,16},{9,... | collective-permute-start | bytes 368648 | tf_op jit(solution)/shard_map/ppermute | solution.py:738
  7.6 10.4 %collective-permute-start.1 = (bf16[480,128]{1,0:T(8,128)(2,1)S(1)}, bf16[480,128]{1,0:T(8,128)(2,1)S(1)}, u32[]{:S(2)}, u32[]{:S(2)}) collective-permute-start(bf16[480,128]{1,0:T(8,128)(2,1)S(1)} %align.1), channel_id=1, source_target_pairs={{0,16},{1,17},{2,18},{3,19},{4,20},{5,21},{6,22},{7,23},{8,24},{9,... | collective-permute-start | bytes 368648 | tf_op jit(solution)/shard_map/ppermute | solution.py:738
  7.6 10.4 %collective-permute-start = (bf16[480,128]{1,0:T(8,128)(2,1)S(1)}, bf16[480,128]{1,0:T(8,128)(2,1)S(1)}, u32[]{:S(2)}, u32[]{:S(2)}) collective-permute-start(bf16[480,128]{1,0:T(8,128)(2,1)S(1)} %align.1), channel_id=1, source_target_pairs={{0,8},{1,9},{2,10},{3,11},{4,12},{5,13},{6,14},{7,15},{8,0},{9,1},... | collective-permute-start | bytes 368648 | tf_op jit(solution)/shard_map/ppermute | solution.py:738
  18.1 9.9 %collective-permute-start.5 = (bf16[960,128]{1,0:T(8,128)(2,1)S(1)}, bf16[960,128]{1,0:T(8,128)(2,1)S(1)}, u32[]{:S(2)}, u32[]{:S(2)}) collective-permute-start(bf16[960,128]{1,0:T(8,128)(2,1)S(1)} %select_dynamic-update-slice_fusion.refs_0_), channel_id=1, source_target_pairs={{0,6},{1,7},{2,4},{3,5},{4,2},{5,3},{6,0},{7,1},{8,14},{9,15},{10,... | collective-permute-start | bytes 737288 | tf_op jit(solution)/shard_map/ppermute | solution.py:738
  20.6 10.7 %collective-permute-start.4 = (bf16[960,128]{1,0:T(8,128)(2,1)S(1)}, bf16[960,128]{1,0:T(8,128)(2,1)S(1)}, u32[]{:S(2)}, u32[]{:S(2)}) collective-permute-start(bf16[960,128]{1,0:T(8,128)(2,1)S(1)} %select_dynamic-update-slice_fusion.refs_0_), channel_id=1, source_target_pairs={{0,4},{1,5},{2,6},{3,7},{4,0},{5,1},{6,2},{7,3},{8,12},{9,13},{10,... | collective-permute-start | bytes 737288 | tf_op jit(solution)/shard_map/ppermute | solution.py:738
  21.1 10.3 %collective-permute-start.3 = (bf16[960,128]{1,0:T(8,128)(2,1)S(1)}, bf16[960,128]{1,0:T(8,128)(2,1)S(1)}, u32[]{:S(2)}, u32[]{:S(2)}) collective-permute-start(bf16[960,128]{1,0:T(8,128)(2,1)S(1)} %select_dynamic-update-slice_fusion.refs_0_), channel_id=1, source_target_pairs={{0,2},{1,3},{2,0},{3,1},{4,6},{5,7},{6,4},{7,5},{8,10},{9,11},{10,... | collective-permute-start | bytes 737288 | tf_op jit(solution)/shard_map/ppermute | solution.py:738
  31.5 3.2 %collective-permute-start.11 = (bf16[960,128]{1,0:T(8,128)(2,1)S(1)}, bf16[960,128]{1,0:T(8,128)(2,1)S(1)}, u32[]{:S(2)}, u32[]{:S(2)}) collective-permute-start(bf16[960,128]{1,0:T(8,128)(2,1)S(1)} %collective-permute-done.3.refs_1_), channel_id=1, source_target_pairs={{0,1},{1,0},{2,3},{3,2},{4,5},{5,4},{6,7},{7,6},{8,9},{9,8},{10,11... | collective-permute-start | bytes 737288 | tf_op jit(solution)/shard_map/ppermute | solution.py:738
  32.0 4.0 %collective-permute-start.12 = (bf16[960,128]{1,0:T(8,128)(2,1)S(1)}, bf16[960,128]{1,0:T(8,128)(2,1)S(1)}, u32[]{:S(2)}, u32[]{:S(2)}) collective-permute-start(bf16[960,128]{1,0:T(8,128)(2,1)S(1)} %collective-permute-done.4.refs_2_), channel_id=1, source_target_pairs={{0,1},{1,0},{2,3},{3,2},{4,5},{5,4},{6,7},{7,6},{8,9},{9,8},{10,11... | collective-permute-start | bytes 737288 | tf_op jit(solution)/shard_map/ppermute | solution.py:738
  32.0 4.5 %collective-permute-start.13 = (bf16[960,128]{1,0:T(8,128)(2,1)S(1)}, bf16[960,128]{1,0:T(8,128)(2,1)S(1)}, u32[]{:S(2)}, u32[]{:S(2)}) collective-permute-start(bf16[960,128]{1,0:T(8,128)(2,1)S(1)} %collective-permute-done.5.refs_3_), channel_id=1, source_target_pairs={{0,1},{1,0},{2,3},{3,2},{4,5},{5,4},{6,7},{7,6},{8,9},{9,8},{10,11... | collective-permute-start | bytes 737288 | tf_op jit(solution)/shard_map/ppermute | solution.py:738
  32.6 13.4 %collective-permute-start.9 = (bf16[960,128]{1,0:T(8,128)(2,1)S(1)}, bf16[960,128]{1,0:T(8,128)(2,1)S(1)}, u32[]{:S(2)}, u32[]{:S(2)}) collective-permute-start(bf16[960,128]{1,0:T(8,128)(2,1)S(1)} %pad_maximum_fusion.refs_0_), channel_id=1, source_target_pairs={{0,1},{1,0},{2,3},{3,2},{4,5},{5,4},{6,7},{7,6},{8,9},{9,8},{10,11... | collective-permute-start | bytes 737288 | tf_op jit(solution)/shard_map/ppermute | solution.py:738
  33.0 13.0 %collective-permute-start.8 = (bf16[960,128]{1,0:T(8,128)(2,1)S(1)}, bf16[960,128]{1,0:T(8,128)(2,1)S(1)}, u32[]{:S(2)}, u32[]{:S(2)}) collective-permute-start(bf16[960,128]{1,0:T(8,128)(2,1)S(1)} %pad_maximum_fusion.refs_0_), channel_id=1, source_target_pairs={{0,6},{1,7},{2,4},{3,5},{4,2},{5,3},{6,0},{7,1},{8,14},{9,15},{10,... | collective-permute-start | bytes 737288 | tf_op jit(solution)/shard_map/ppermute | solution.py:738
  34.6 12.5 %collective-permute-start.7 = (bf16[960,128]{1,0:T(8,128)(2,1)S(1)}, bf16[960,128]{1,0:T(8,128)(2,1)S(1)}, u32[]{:S(2)}, u32[]{:S(2)}) collective-permute-start(bf16[960,128]{1,0:T(8,128)(2,1)S(1)} %pad_maximum_fusion.refs_0_), channel_id=1, source_target_pairs={{0,4},{1,5},{2,6},{3,7},{4,0},{5,1},{6,2},{7,3},{8,12},{9,13},{10,... | collective-permute-start | bytes 737288 | tf_op jit(solution)/shard_map/ppermute | solution.py:738
  35.9 11.2 %collective-permute-start.6 = (bf16[960,128]{1,0:T(8,128)(2,1)S(1)}, bf16[960,128]{1,0:T(8,128)(2,1)S(1)}, u32[]{:S(2)}, u32[]{:S(2)}) collective-permute-start(bf16[960,128]{1,0:T(8,128)(2,1)S(1)} %pad_maximum_fusion.refs_0_), channel_id=1, source_target_pairs={{0,2},{1,3},{2,0},{3,1},{4,6},{5,7},{6,4},{7,5},{8,10},{9,11},{10,... | collective-permute-start | bytes 737288 | tf_op jit(solution)/shard_map/ppermute | solution.py:738
  47.2 1.8 %collective-permute-start.15 = (bf16[960,128]{1,0:T(8,128)(2,1)S(1)}, bf16[960,128]{1,0:T(8,128)(2,1)S(1)}, u32[]{:S(2)}, u32[]{:S(2)}) collective-permute-start(bf16[960,128]{1,0:T(8,128)(2,1)S(1)} %collective-permute-done.7.refs_2_), channel_id=1, source_target_pairs={{0,1},{1,0},{2,3},{3,2},{4,5},{5,4},{6,7},{7,6},{8,9},{9,8},{10,11... | collective-permute-start | bytes 737288 | tf_op jit(solution)/shard_map/ppermute | solution.py:738
  63.8 3.0 %collective-permute-start.17 = (bf16[5120,128]{1,0:T(8,128)(2,1)S(1)}, bf16[5120,128]{1,0:T(8,128)(2,1)S(1)}, u32[]{:S(2)}, u32[]{:S(2)}) collective-permute-start(bf16[5120,128]{1,0:T(8,128)(2,1)S(1)} %get-tuple-element.157), channel_id=1, source_target_pairs={{0,1},{1,0},{2,3},{3,2},{4,5},{5,4},{6,7},{7,6},{8,9},{9,8},{10,11... | collective-permute-start | bytes 3932168 | tf_op jit(solution)/shard_map/ppermute | solution.py:738
  67.2 16.8 %collective-permute-start.18 = (bf16[1280,128]{1,0:T(8,128)(2,1)S(1)}, bf16[1280,128]{1,0:T(8,128)(2,1)S(1)}, u32[]{:S(2)}, u32[]{:S(2)}) collective-permute-start(bf16[1280,128]{1,0:T(8,128)(2,1)S(1)} %get-tuple-element.174), channel_id=1, source_target_pairs={{0,2},{1,3},{2,0},{3,1},{4,6},{5,7},{6,4},{7,5},{8,10},{9,11},{10,... | collective-permute-start | bytes 983048 | tf_op jit(solution)/shard_map/ppermute | solution.py:738
  69.4 16.5 %collective-permute-start.19 = (bf16[1280,128]{1,0:T(8,128)(2,1)S(1)}, bf16[1280,128]{1,0:T(8,128)(2,1)S(1)}, u32[]{:S(2)}, u32[]{:S(2)}) collective-permute-start(bf16[1280,128]{1,0:T(8,128)(2,1)S(1)} %get-tuple-element.175), channel_id=1, source_target_pairs={{0,4},{1,5},{2,6},{3,7},{4,0},{5,1},{6,2},{7,3},{8,12},{9,13},{10,... | collective-permute-start | bytes 983048 | tf_op jit(solution)/shard_map/ppermute | solution.py:738
  69.5 16.4 %collective-permute-start.20 = (bf16[1280,128]{1,0:T(8,128)(2,1)S(1)}, bf16[1280,128]{1,0:T(8,128)(2,1)S(1)}, u32[]{:S(2)}, u32[]{:S(2)}) collective-permute-start(bf16[1280,128]{1,0:T(8,128)(2,1)S(1)} %get-tuple-element.176), channel_id=1, source_target_pairs={{0,6},{1,7},{2,4},{3,5},{4,2},{5,3},{6,0},{7,1},{8,14},{9,15},{10,... | collective-permute-start | bytes 983048 | tf_op jit(solution)/shard_map/ppermute | solution.py:738
  85.9 2.2 %collective-permute-start.21 = (bf16[2560,128]{1,0:T(8,128)(2,1)S(1)}, bf16[2560,128]{1,0:T(8,128)(2,1)S(1)}, u32[]{:S(2)}, u32[]{:S(2)}) collective-permute-start(bf16[2560,128]{1,0:T(8,128)(2,1)S(1)} %get-tuple-element.184), channel_id=1, source_target_pairs={{0,1},{1,0},{2,3},{3,2},{4,5},{5,4},{6,7},{7,6},{8,9},{9,8},{10,11... | collective-permute-start | bytes 1966088 | tf_op jit(solution)/shard_map/ppermute | solution.py:738
  85.9 2.2 %collective-permute-start.22 = (bf16[320,128]{1,0:T(8,128)(2,1)S(1)}, bf16[320,128]{1,0:T(8,128)(2,1)S(1)}, u32[]{:S(2)}, u32[]{:S(2)}) collective-permute-start(bf16[320,128]{1,0:T(8,128)(2,1)S(1)} %get-tuple-element.190), channel_id=1, source_target_pairs={{0,1},{1,0},{2,3},{3,2},{4,5},{5,4},{6,7},{7,6},{8,9},{9,8},{10,11... | collective-permute-start | bytes 245768 | tf_op jit(solution)/shard_map/ppermute | solution.py:738
  88.4 7.5 %collective-permute-start.23 = (bf16[720,128]{1,0:T(8,128)(2,1)S(1)}, bf16[720,128]{1,0:T(8,128)(2,1)S(1)}, u32[]{:S(2)}, u32[]{:S(2)}) collective-permute-start(bf16[720,128]{1,0:T(8,128)(2,1)S(1)} %get-tuple-element.200), channel_id=1, source_target_pairs={{0,2},{1,3},{2,0},{3,1},{4,6},{5,7},{6,4},{7,5},{8,10},{9,11},{10,... | collective-permute-start | bytes 552968 | tf_op jit(solution)/shard_map/ppermute | solution.py:738
  88.8 10.3 %collective-permute-start.24 = (bf16[720,128]{1,0:T(8,128)(2,1)S(1)}, bf16[720,128]{1,0:T(8,128)(2,1)S(1)}, u32[]{:S(2)}, u32[]{:S(2)}) collective-permute-start(bf16[720,128]{1,0:T(8,128)(2,1)S(1)} %get-tuple-element.201), channel_id=1, source_target_pairs={{0,4},{1,5},{2,6},{3,7},{4,0},{5,1},{6,2},{7,3},{8,12},{9,13},{10,... | collective-permute-start | bytes 552968 | tf_op jit(solution)/shard_map/ppermute | solution.py:738
  90.2 9.0 %collective-permute-start.25 = (bf16[720,128]{1,0:T(8,128)(2,1)S(1)}, bf16[720,128]{1,0:T(8,128)(2,1)S(1)}, u32[]{:S(2)}, u32[]{:S(2)}) collective-permute-start(bf16[720,128]{1,0:T(8,128)(2,1)S(1)} %get-tuple-element.202), channel_id=1, source_target_pairs={{0,6},{1,7},{2,4},{3,5},{4,2},{5,3},{6,0},{7,1},{8,14},{9,15},{10,... | collective-permute-start | bytes 552968 | tf_op jit(solution)/shard_map/ppermute | solution.py:738
  92.1 9.7 %collective-permute-start.29 = (bf16[320,128]{1,0:T(8,128)(2,1)S(1)}, bf16[320,128]{1,0:T(8,128)(2,1)S(1)}, u32[]{:S(2)}, u32[]{:S(2)}) collective-permute-start(bf16[320,128]{1,0:T(8,128)(2,1)S(1)} %get-tuple-element.216), channel_id=1, source_target_pairs={{0,8},{1,9},{2,10},{3,11},{4,12},{5,13},{6,14},{7,15},{8,0},{9,1},... | collective-permute-start | bytes 245768 | tf_op jit(solution)/shard_map/ppermute | solution.py:738
  92.2 11.6 %collective-permute-start.30 = (bf16[320,128]{1,0:T(8,128)(2,1)S(1)}, bf16[320,128]{1,0:T(8,128)(2,1)S(1)}, u32[]{:S(2)}, u32[]{:S(2)}) collective-permute-start(bf16[320,128]{1,0:T(8,128)(2,1)S(1)} %get-tuple-element.217), channel_id=1, source_target_pairs={{0,16},{1,17},{2,18},{3,19},{4,20},{5,21},{6,22},{7,23},{8,24},{9,... | collective-permute-start | bytes 245768 | tf_op jit(solution)/shard_map/ppermute | solution.py:738
  95.9 7.9 %collective-permute-start.31 = (bf16[320,128]{1,0:T(8,128)(2,1)S(1)}, bf16[320,128]{1,0:T(8,128)(2,1)S(1)}, u32[]{:S(2)}, u32[]{:S(2)}) collective-permute-start(bf16[320,128]{1,0:T(8,128)(2,1)S(1)} %get-tuple-element.218), channel_id=1, source_target_pairs={{0,24},{1,25},{2,26},{3,27},{4,28},{5,29},{6,30},{7,31},{8,16},{9,... | collective-permute-start | bytes 245768 | tf_op jit(solution)/shard_map/ppermute | solution.py:738
  99.3 4.5 %collective-permute-start.26 = (bf16[240,128]{1,0:T(8,128)(2,1)S(1)}, bf16[240,128]{1,0:T(8,128)(2,1)S(1)}, u32[]{:S(2)}, u32[]{:S(2)}) collective-permute-start(bf16[240,128]{1,0:T(8,128)(2,1)S(1)} %get-tuple-element.208), channel_id=1, source_target_pairs={{0,8},{1,9},{2,10},{3,11},{4,12},{5,13},{6,14},{7,15},{8,0},{9,1},... | collective-permute-start | bytes 184328 | tf_op jit(solution)/shard_map/ppermute | solution.py:738
  99.4 7.0 %collective-permute-start.27 = (bf16[240,128]{1,0:T(8,128)(2,1)S(1)}, bf16[240,128]{1,0:T(8,128)(2,1)S(1)}, u32[]{:S(2)}, u32[]{:S(2)}) collective-permute-start(bf16[240,128]{1,0:T(8,128)(2,1)S(1)} %get-tuple-element.209), channel_id=1, source_target_pairs={{0,16},{1,17},{2,18},{3,19},{4,20},{5,21},{6,22},{7,23},{8,24},{9,... | collective-permute-start | bytes 184328 | tf_op jit(solution)/shard_map/ppermute | solution.py:738
  101.8 6.0 %collective-permute-start.28 = (bf16[240,128]{1,0:T(8,128)(2,1)S(1)}, bf16[240,128]{1,0:T(8,128)(2,1)S(1)}, u32[]{:S(2)}, u32[]{:S(2)}) collective-permute-start(bf16[240,128]{1,0:T(8,128)(2,1)S(1)} %concatenate.26), channel_id=1, source_target_pairs={{0,24},{1,25},{2,26},{3,27},{4,28},{5,29},{6,30},{7,31},{8,16},{9,... | collective-permute-start | bytes 184328 | tf_op jit(solution)/shard_map/ppermute | solution.py:738
  107.8 5.0 %collective-permute-start.34 = (bf16[80,128]{1,0:T(8,128)(2,1)S(1)}, bf16[80,128]{1,0:T(8,128)(2,1)S(1)}, u32[]{:S(2)}, u32[]{:S(2)}) collective-permute-start(bf16[80,128]{1,0:T(8,128)(2,1)S(1)} %add_convert_fusion.1.refs_4_), channel_id=1, source_target_pairs={{0,6},{1,7},{2,4},{3,5},{4,2},{5,3},{6,0},{7,1},{8,14},{9,15},{10,... | collective-permute-start | bytes 61448 | tf_op jit(solution)/shard_map/ppermute | solution.py:738
  109.5 3.8 %collective-permute-start.33 = (bf16[80,128]{1,0:T(8,128)(2,1)S(1)}, bf16[80,128]{1,0:T(8,128)(2,1)S(1)}, u32[]{:S(2)}, u32[]{:S(2)}) collective-permute-start(bf16[80,128]{1,0:T(8,128)(2,1)S(1)} %add_convert_fusion.1.refs_4_), channel_id=1, source_target_pairs={{0,4},{1,5},{2,6},{3,7},{4,0},{5,1},{6,2},{7,3},{8,12},{9,13},{10,... | collective-permute-start | bytes 61448 | tf_op jit(solution)/shard_map/ppermute | solution.py:738
  110.8 3.8 %collective-permute-start.32 = (bf16[80,128]{1,0:T(8,128)(2,1)S(1)}, bf16[80,128]{1,0:T(8,128)(2,1)S(1)}, u32[]{:S(2)}, u32[]{:S(2)}) collective-permute-start(bf16[80,128]{1,0:T(8,128)(2,1)S(1)} %add_convert_fusion.1.refs_4_), channel_id=1, source_target_pairs={{0,2},{1,3},{2,0},{3,1},{4,6},{5,7},{6,4},{7,5},{8,10},{9,11},{10,... | collective-permute-start | bytes 61448 | tf_op jit(solution)/shard_map/ppermute | solution.py:738
  (12 other events, 205.5 us)
